TPU v7x, 32 devices: a whole 2x2x4 slice. The times are simulated.
32 devices in a mesh: dp: 4 (over x, core), fsdp: 8 (over z, y).
Axes of the slice: x: 2, y: 2, z: 4, core: 2. Of those that a mesh axis runs over, the one named last changes fastest.
Arguments:
- targets: float32 [32, 64, 768], P(('dp', 'fsdp')), may hold values from -6 to 6
- passages: bfloat16 [32, 1920, 768], P('dp', 'fsdp'), may hold values from -6 to 6
- tgt_len: int32 [32], P(('dp', 'fsdp')), may hold values from 8 to 64, as said below
- out_grad: float32 [32, 64, 768], P(('dp', 'fsdp')), may hold values from -6 to 6
- ln_self: bfloat16 [768], P(('dp', 'fsdp')), may hold values from 0.099609375 to 1.8984375
- rel_bias: bfloat16 [384], P(('dp', 'fsdp')), may hold values from -6 to 6
- self_q: bfloat16 [768, 768], P(('dp', 'fsdp')), may hold values from -0.0546875 to 0.0546875
- self_kv: bfloat16 [768, 1536], P(('dp', 'fsdp')), may hold values from -0.21875 to 0.21875
- self_out: bfloat16 [768, 768], P(('dp', 'fsdp')), may hold values from -0.3125 to 0.3125
- ln_cross: bfloat16 [768], P(('dp', 'fsdp')), may hold values from 0.099609375 to 1.8984375
- cross_q: bfloat16 [768, 768], P(('dp', 'fsdp')), may hold values from -0.0546875 to 0.0546875
- cross_kv: bfloat16 [768, 1536], P(('dp', 'fsdp')), may hold values from -0.21875 to 0.21875
- cross_out: bfloat16 [768, 768], P(('dp', 'fsdp')), may hold values from -1.25 to 1.25
- ln_ff: bfloat16 [768], P(('dp', 'fsdp')), may hold values from 0.099609375 to 1.8984375
- ff_in: bfloat16 [768, 3072], P(('dp', 'fsdp')), may hold values from -0.21875 to 0.21875
- ff_out: bfloat16 [3072, 768], P(('dp', 'fsdp')), may hold values from -0.109375 to 0.109375
Outputs:
- block_out: float32 [32, 64, 768], P(('dp', 'fsdp'))
- target_grad: float32 [32, 64, 768], P(('dp', 'fsdp'))
- passage_grad: bfloat16 [32, 1920, 768], P('dp', 'fsdp')
- ln_self_grad: float32 [768], P(('dp', 'fsdp'))
- rel_bias_grad: float32 [384], P(('dp', 'fsdp'))
- self_q_grad: float32 [768, 768], P(('dp', 'fsdp'))
- self_kv_grad: float32 [768, 1536], P(('dp', 'fsdp'))
- self_out_grad: float32 [768, 768], P(('dp', 'fsdp'))
- ln_cross_grad: float32 [768], P(('dp', 'fsdp'))
- cross_q_grad: float32 [768, 768], P(('dp', 'fsdp'))
- cross_kv_grad: float32 [768, 1536], P(('dp', 'fsdp'))
- cross_out_grad: float32 [768, 768], P(('dp', 'fsdp'))
- ln_ff_grad: float32 [768], P(('dp', 'fsdp'))
- ff_in_grad: float32 [768, 3072], P(('dp', 'fsdp'))
- ff_out_grad: float32 [3072, 768], P(('dp', 'fsdp'))
Inputs may be any that keep to these rules, and one draw needn't show every extreme that they name: `tgt_len`: each query's length is 64, 32 or 8 by its task (about 6, 6 and 4 queries in 16); the first query has 64.
All inputs are finite; a program needn't handle non-finite values.
Results may differ from a plain program's by a relative error of at most 0.03.
Values may be sent and summed in bfloat16 or wider, within the bound.
A program may use at most 192 MiB of HBM per device.

v0:
```python
import math

import jax
import jax.numpy as jnp
from jax import lax
from jax.sharding import PartitionSpec as P

HEADS = 12
DK = 64
BUCKETS = 32


EPS = 1e-06
NEG = -1e30
HIGH = lax.Precision.HIGHEST


def bucket_limits():
    limits = []
    for target_bucket in range(1, 16):
        distance = 16
        while int(math.log(distance / 16.0) / math.log(8.0) * 16.0) < target_bucket:
            distance = distance + 1
        limits.append(distance)
    return limits


def bucket_table(length):
    positions = jnp.arange(length, dtype=jnp.int32)
    distance = jnp.maximum(positions[:, None] - positions[None, :], 0)
    larger = jnp.full_like(distance, 16)
    for limit_value in bucket_limits():
        larger = larger + (distance >= limit_value).astype(jnp.int32)
    return jnp.where(distance < 16, distance, jnp.minimum(larger, 31))


def normed(values, gain_vec):
    return values * lax.rsqrt(jnp.mean(values * values, axis=-1, keepdims=True) + EPS) * gain_vec


def gelu_fn(values):
    return jax.nn.gelu(values, approximate=True)


def matmul(left, right):
    return jnp.dot(left, right, preferred_element_type=jnp.float32)


def left_contract(left, right):
    return lax.dot_general(
        left, right, (((0,), (0,)), ((), ())), preferred_element_type=jnp.float32
    )


def right_contract(left, right):
    return lax.dot_general(
        left, right, (((1,), (1,)), ((), ())), preferred_element_type=jnp.float32
    )


def split_blocks(kv_rows):
    total_rows = kv_rows.shape[0]
    block_rows = total_rows
    while block_rows > 1024 and block_rows % 2 == 0:
        block_rows = block_rows // 2
    return kv_rows.reshape(total_rows // block_rows, block_rows, kv_rows.shape[1])


def cross_stats(q_heads, kv_rows):
    model_width = kv_rows.shape[1] // 2
    query_rows = q_heads.shape[0]

    def absorb(carried, kv_block):
        running_top, running_sum = carried
        key_heads = kv_block[:, :model_width].reshape(kv_block.shape[0], HEADS, DK)
        scores = jnp.einsum("ihd,jhd->hij", q_heads, key_heads, preferred_element_type=jnp.float32)
        new_top = jnp.maximum(running_top, jnp.max(scores, axis=2))
        new_sum = running_sum * jnp.exp(running_top - new_top) + jnp.sum(
            jnp.exp(scores - new_top[:, :, None]), axis=2
        )
        return ((new_top, new_sum), None)

    initial = (
        jnp.full((HEADS, query_rows), NEG, jnp.float32),
        jnp.zeros((HEADS, query_rows), jnp.float32),
    )
    result, _ = lax.scan(absorb, initial, split_blocks(kv_rows))
    return result


def cross_values(q_heads, kv_rows, lse):
    model_width = kv_rows.shape[1] // 2
    query_rows = q_heads.shape[0]

    def absorb(carried, kv_block):
        key_heads = kv_block[:, :model_width].reshape(kv_block.shape[0], HEADS, DK)
        value_heads = kv_block[:, model_width:].reshape(kv_block.shape[0], HEADS, DK)
        scores = jnp.einsum("ihd,jhd->hij", q_heads, key_heads, preferred_element_type=jnp.float32)
        probs_low = jnp.exp(scores - lse[:, :, None]).astype(jnp.bfloat16)
        return (
            carried
            + jnp.einsum(
                "hij,jhd->ihd", probs_low, value_heads, preferred_element_type=jnp.float32
            ),
            None,
        )

    summed, _ = lax.scan(
        absorb, jnp.zeros((query_rows, HEADS, DK), jnp.float32), split_blocks(kv_rows)
    )
    return summed.reshape(query_rows, model_width)


def cross_back(q_heads, kv_rows, lse, grad_heads, delta):
    model_width = kv_rows.shape[1] // 2
    query_rows = q_heads.shape[0]

    def absorb(carried, kv_block):
        block_rows = kv_block.shape[0]
        key_heads = kv_block[:, :model_width].reshape(block_rows, HEADS, DK)
        value_heads = kv_block[:, model_width:].reshape(block_rows, HEADS, DK)
        scores = jnp.einsum("ihd,jhd->hij", q_heads, key_heads, preferred_element_type=jnp.float32)
        probs = jnp.exp(scores - lse[:, :, None])
        grad_values = jnp.einsum(
            "hij,ihd->jhd",
            probs.astype(jnp.bfloat16),
            grad_heads,
            preferred_element_type=jnp.float32,
        )
        grad_probs = jnp.einsum(
            "ihd,jhd->hij", grad_heads, value_heads, preferred_element_type=jnp.float32
        )
        grad_scores = (probs * (grad_probs - delta[:, :, None])).astype(jnp.bfloat16)
        grad_keys = jnp.einsum(
            "hij,ihd->jhd", grad_scores, q_heads, preferred_element_type=jnp.float32
        )
        carried = carried + jnp.einsum(
            "hij,jhd->ihd", grad_scores, key_heads, preferred_element_type=jnp.float32
        )
        grad_block = jnp.concatenate(
            [
                grad_keys.reshape(block_rows, model_width),
                grad_values.reshape(block_rows, model_width),
            ],
            axis=1,
        )
        return (carried, grad_block.astype(jnp.bfloat16))

    grad_query, grad_kv = lax.scan(
        absorb, jnp.zeros((query_rows, HEADS, DK), jnp.float32), split_blocks(kv_rows)
    )
    return (
        grad_query.reshape(query_rows, model_width),
        grad_kv.reshape(kv_rows.shape[0], kv_rows.shape[1]),
    )


def per_device(
    targets,
    passages,
    tgt_len,
    out_grad,
    ln_self,
    rel_bias,
    self_q,
    self_kv,
    self_out,
    ln_cross,
    cross_q,
    cross_kv,
    cross_out,
    ln_ff,
    ff_in,
    ff_out,
):
    (
        gain_self,
        bias_full,
        selfq_full,
        selfkv_full,
        selfout_full,
        gain_cross,
        crossq_full,
        crosskv_full,
        crossout_full,
        gain_ff,
        ffin_full,
        ffout_full,
    ) = (
        lax.all_gather(ln_self, ("dp", "fsdp"), axis=0, tiled=True),
        lax.all_gather(rel_bias, ("dp", "fsdp"), axis=0, tiled=True),
        lax.all_gather(self_q, ("dp", "fsdp"), axis=0, tiled=True),
        lax.all_gather(self_kv, ("dp", "fsdp"), axis=0, tiled=True),
        lax.all_gather(self_out, ("dp", "fsdp"), axis=0, tiled=True),
        lax.all_gather(ln_cross, ("dp", "fsdp"), axis=0, tiled=True),
        lax.all_gather(cross_q, ("dp", "fsdp"), axis=0, tiled=True),
        lax.all_gather(cross_kv, ("dp", "fsdp"), axis=0, tiled=True),
        lax.all_gather(cross_out, ("dp", "fsdp"), axis=0, tiled=True),
        lax.all_gather(ln_ff, ("dp", "fsdp"), axis=0, tiled=True),
        lax.all_gather(ff_in, ("dp", "fsdp"), axis=0, tiled=True),
        lax.all_gather(ff_out, ("dp", "fsdp"), axis=0, tiled=True),
    )
    gain_self = gain_self.astype(jnp.float32)
    gain_cross = gain_cross.astype(jnp.float32)
    gain_ff = gain_ff.astype(jnp.float32)
    tokens = targets[0]
    tmax_rows = tokens.shape[0]
    model_width = tokens.shape[1]
    positions = jnp.arange(tmax_rows)
    live = (positions < tgt_len[0]).astype(jnp.float32)
    h_one = normed(tokens, gain_self).astype(jnp.bfloat16)
    q_self = matmul(h_one, selfq_full).astype(jnp.bfloat16)
    kv_self = matmul(h_one, selfkv_full).astype(jnp.bfloat16)
    qs_heads = q_self.reshape(tmax_rows, HEADS, DK)
    ks_heads = kv_self[:, :model_width].reshape(tmax_rows, HEADS, DK)
    vs_heads = kv_self[:, model_width:].reshape(tmax_rows, HEADS, DK)
    onehot = (bucket_table(tmax_rows).reshape(-1)[None, :] == jnp.arange(BUCKETS)[:, None]).astype(
        jnp.float32
    )
    bias_heads = jnp.dot(
        bias_full.astype(jnp.float32).reshape(HEADS, BUCKETS), onehot, precision=HIGH
    ).reshape(HEADS, tmax_rows, tmax_rows)
    allowed = positions[:, None] >= positions[None, :]
    scores_self = (
        jnp.einsum("ihd,jhd->hij", qs_heads, ks_heads, preferred_element_type=jnp.float32)
        + bias_heads
    )
    probs_self = jax.nn.softmax(jnp.where(allowed, scores_self, NEG), axis=-1)
    probs_low = probs_self.astype(jnp.bfloat16)
    att_self = (
        jnp.einsum("hij,jhd->ihd", probs_low, vs_heads, preferred_element_type=jnp.float32)
        .reshape(tmax_rows, model_width)
        .astype(jnp.bfloat16)
    )
    x_one = tokens + matmul(att_self, selfout_full)
    h_two = normed(x_one, gain_cross).astype(jnp.bfloat16)
    q_cross = matmul(h_two, crossq_full).astype(jnp.bfloat16)
    q_heads = q_cross.reshape(tmax_rows, HEADS, DK)
    enc_rows = lax.all_to_all(passages, "fsdp", split_axis=0, concat_axis=1, tiled=True)[0]
    kv_cross = matmul(enc_rows, crosskv_full).astype(jnp.bfloat16)
    running_top, running_sum = cross_stats(q_heads, kv_cross)
    lse_cross = running_top + jnp.log(running_sum)
    att_cross = cross_values(q_heads, kv_cross, lse_cross).astype(jnp.bfloat16)
    x_two = x_one + matmul(att_cross, crossout_full)
    h_three = normed(x_two, gain_ff).astype(jnp.bfloat16)
    pre_act = matmul(h_three, ffin_full)
    act_low = gelu_fn(pre_act).astype(jnp.bfloat16)
    block_out = live[:, None] * (x_two + matmul(act_low, ffout_full))
    grad_three = live[:, None] * out_grad[0]
    grad_low = grad_three.astype(jnp.bfloat16)
    gw_ffout = left_contract(act_low, grad_low)
    grad_act = right_contract(grad_low, ffout_full)
    _, gelu_back = jax.vjp(gelu_fn, pre_act)
    grad_pre = gelu_back(grad_act)[0].astype(jnp.bfloat16)
    gw_ffin = left_contract(h_three, grad_pre)
    grad_hthree = right_contract(grad_pre, ffin_full)
    _, norm_back = jax.vjp(normed, x_two, gain_ff)
    grad_xtwo_norm, gg_ff = norm_back(grad_hthree)
    grad_xtwo = grad_three + grad_xtwo_norm
    grad_xtwo_low = grad_xtwo.astype(jnp.bfloat16)
    gw_crossout = left_contract(att_cross, grad_xtwo_low)
    grad_attc = right_contract(grad_xtwo_low, crossout_full).astype(jnp.bfloat16)
    delta_cross = jnp.sum(
        (grad_attc.astype(jnp.float32) * att_cross.astype(jnp.float32)).reshape(
            tmax_rows, HEADS, DK
        ),
        axis=2,
    ).T
    grad_qc, grad_kvc = cross_back(
        q_heads, kv_cross, lse_cross, grad_attc.reshape(tmax_rows, HEADS, DK), delta_cross
    )
    gw_crosskv = left_contract(enc_rows, grad_kvc)
    grad_enc = right_contract(grad_kvc, crosskv_full).astype(jnp.bfloat16)
    passage_grad = lax.all_to_all(grad_enc[None], "fsdp", split_axis=1, concat_axis=0, tiled=True)
    grad_qc_low = grad_qc.astype(jnp.bfloat16)
    gw_crossq = left_contract(h_two, grad_qc_low)
    grad_htwo = right_contract(grad_qc_low, crossq_full)
    _, norm_back = jax.vjp(normed, x_one, gain_cross)
    grad_xone_norm, gg_cross = norm_back(grad_htwo)
    grad_xone = grad_xtwo + grad_xone_norm
    grad_xone_low = grad_xone.astype(jnp.bfloat16)
    gw_selfout = left_contract(att_self, grad_xone_low)
    grad_atts = (
        right_contract(grad_xone_low, selfout_full)
        .astype(jnp.bfloat16)
        .reshape(tmax_rows, HEADS, DK)
    )
    grad_probs = jnp.einsum("ihd,jhd->hij", grad_atts, vs_heads, preferred_element_type=jnp.float32)
    grad_scores = (
        probs_self * (grad_probs - jnp.sum(probs_self * grad_probs, axis=2, keepdims=True))
    ).astype(jnp.bfloat16)
    grad_vs = jnp.einsum(
        "hij,ihd->jhd", probs_low, grad_atts, preferred_element_type=jnp.float32
    ).reshape(tmax_rows, model_width)
    grad_qs = (
        jnp.einsum("hij,jhd->ihd", grad_scores, ks_heads, preferred_element_type=jnp.float32)
        .reshape(tmax_rows, model_width)
        .astype(jnp.bfloat16)
    )
    grad_ks = jnp.einsum(
        "hij,ihd->jhd", grad_scores, qs_heads, preferred_element_type=jnp.float32
    ).reshape(tmax_rows, model_width)
    grad_kvs = jnp.concatenate([grad_ks, grad_vs], axis=1).astype(jnp.bfloat16)
    gb_table = jnp.dot(
        grad_scores.astype(jnp.float32).reshape(HEADS, tmax_rows * tmax_rows),
        onehot.T,
        precision=HIGH,
    ).reshape(HEADS * BUCKETS)
    gw_selfq = left_contract(h_one, grad_qs)
    gw_selfkv = left_contract(h_one, grad_kvs)
    grad_hone = right_contract(grad_qs, selfq_full) + right_contract(grad_kvs, selfkv_full)
    _, norm_back = jax.vjp(normed, tokens, gain_self)
    grad_tok_norm, gg_self = norm_back(grad_hone)
    target_grad = grad_xone + grad_tok_norm
    (
        ln_self_grad,
        rel_bias_grad,
        self_q_grad,
        self_kv_grad,
        self_out_grad,
        ln_cross_grad,
        cross_q_grad,
        cross_kv_grad,
        cross_out_grad,
        ln_ff_grad,
        ff_in_grad,
        ff_out_grad,
    ) = (
        lax.psum_scatter(gg_self, ("dp", "fsdp"), scatter_dimension=0, tiled=True),
        lax.psum_scatter(gb_table, ("dp", "fsdp"), scatter_dimension=0, tiled=True),
        lax.psum_scatter(gw_selfq, ("dp", "fsdp"), scatter_dimension=0, tiled=True),
        lax.psum_scatter(gw_selfkv, ("dp", "fsdp"), scatter_dimension=0, tiled=True),
        lax.psum_scatter(gw_selfout, ("dp", "fsdp"), scatter_dimension=0, tiled=True),
        lax.psum_scatter(gg_cross, ("dp", "fsdp"), scatter_dimension=0, tiled=True),
        lax.psum_scatter(gw_crossq, ("dp", "fsdp"), scatter_dimension=0, tiled=True),
        lax.psum_scatter(gw_crosskv, ("dp", "fsdp"), scatter_dimension=0, tiled=True),
        lax.psum_scatter(gw_crossout, ("dp", "fsdp"), scatter_dimension=0, tiled=True),
        lax.psum_scatter(gg_ff, ("dp", "fsdp"), scatter_dimension=0, tiled=True),
        lax.psum_scatter(gw_ffin, ("dp", "fsdp"), scatter_dimension=0, tiled=True),
        lax.psum_scatter(gw_ffout, ("dp", "fsdp"), scatter_dimension=0, tiled=True),
    )
    return (
        block_out[None],
        target_grad[None],
        passage_grad,
        ln_self_grad,
        rel_bias_grad,
        self_q_grad,
        self_kv_grad,
        self_out_grad,
        ln_cross_grad,
        cross_q_grad,
        cross_kv_grad,
        cross_out_grad,
        ln_ff_grad,
        ff_in_grad,
        ff_out_grad,
    )


def solution(mesh):
    placed = (
        P(("dp", "fsdp"), None, None),
        P("dp", "fsdp", None),
        P(("dp", "fsdp")),
        P(("dp", "fsdp"), None, None),
        P(("dp", "fsdp")),
        P(("dp", "fsdp")),
        P(("dp", "fsdp"), None),
        P(("dp", "fsdp"), None),
        P(("dp", "fsdp"), None),
        P(("dp", "fsdp")),
        P(("dp", "fsdp"), None),
        P(("dp", "fsdp"), None),
        P(("dp", "fsdp"), None),
        P(("dp", "fsdp")),
        P(("dp", "fsdp"), None),
        P(("dp", "fsdp"), None),
    )
    return jax.shard_map(
        per_device,
        mesh=mesh,
        in_specs=placed,
        out_specs=(
            P(("dp", "fsdp"), None, None),
            P(("dp", "fsdp"), None, None),
            P("dp", "fsdp", None),
            P(("dp", "fsdp")),
            P(("dp", "fsdp")),
            P(("dp", "fsdp"), None),
            P(("dp", "fsdp"), None),
            P(("dp", "fsdp"), None),
            P(("dp", "fsdp")),
            P(("dp", "fsdp"), None),
            P(("dp", "fsdp"), None),
            P(("dp", "fsdp"), None),
            P(("dp", "fsdp")),
            P(("dp", "fsdp"), None),
            P(("dp", "fsdp"), None),
        ),
        check_vma=False,
    )
```

profile of v0, /device:TPU:0, one launch (start us, length us, event | category | flops | bytes accessed | tf_op | source)
XLA Modules:
  0.0 1516.5 jit_solution(5769498483615900632)
XLA Ops:
  21.2 87.3 %all-reduce.9 = (bf16[768]{0:T(1024)(128)(2,1)S(1)}, bf16[384]{0:T(512)(128)(2,1)S(1)}, bf16[768]{0:T(1024)(128)(2,1)S(1)}, bf16[768]{0:T(1024)(128)(2,1)S(1)}) all-reduce(bf16[768]{0:T(1024)(128)(2,1)S(1)} %dynamic-update-slice, bf16[384]{0:T(512)(128)(2,1)S(1)} %dynamic-update-slice.1, ...), channel_id=1, replica_groups=mesh['dp'=4,'fsdp'=8] {'dp','fsdp'}, use_global_device_ids=true, to_apply=%add | all-reduce | flops 2688 | bytes 10752
  113.8 52.5 %all-gather.9.cloned.1.call-done = bf16[768,1536]{1,0:T(8,128)(2,1)} async-done(((bf16[24,1536]{1,0:T(8,128)(2,1)}), bf16[768,1536]{1,0:T(8,128)(2,1)}) %all-gather.9.cloned.1.call-update) | async-done | bytes 2359312 | tf_op jit(solution)/shard_map/all_gather | solution.py:193
  170.4 52.0 %all-gather.13.cloned.1.call-done = bf16[768,768]{1,0:T(8,128)(2,1)} async-done(((bf16[24,768]{1,0:T(8,128)(2,1)}), bf16[768,768]{1,0:T(8,128)(2,1)}) %all-gather.13.cloned.1.call-update) | async-done | bytes 1179664 | tf_op jit(solution)/shard_map/all_gather | solution.py:194
  224.1 54.1 %all-gather.17.cloned.1.call-done = bf16[768,768]{1,0:T(8,128)(2,1)} async-done(((bf16[24,768]{1,0:T(8,128)(2,1)}), bf16[768,768]{1,0:T(8,128)(2,1)}) %all-gather.17.cloned.1.call-update) | async-done | bytes 1179664 | tf_op jit(solution)/shard_map/all_gather | solution.py:196
  280.3 56.8 %all-gather.15.cloned.1.call-done = bf16[768,1536]{1,0:T(8,128)(2,1)} async-done(((bf16[24,1536]{1,0:T(8,128)(2,1)}), bf16[768,1536]{1,0:T(8,128)(2,1)}) %all-gather.15.cloned.1.call-update) | async-done | bytes 2359312 | tf_op jit(solution)/shard_map/all_gather | solution.py:197
  337.2 9.8 convolution_convert_fusion.2
  347.0 8.5 copy.115
  355.5 8.6 while.37
  364.8 9.9 while.38
  375.9 17.1 %all-gather.19.cloned.1.call-done = bf16[768,768]{1,0:T(8,128)(2,1)} async-done(((bf16[24,768]{1,0:T(8,128)(2,1)}), bf16[768,768]{1,0:T(8,128)(2,1)}) %all-gather.19.cloned.1.call-update) | async-done | bytes 1179664 | tf_op jit(solution)/shard_map/all_gather | solution.py:198
  394.8 63.7 %all-gather.21.cloned.1.call-done = bf16[768,3072]{1,0:T(8,128)(2,1)} async-done(((bf16[24,3072]{1,0:T(8,128)(2,1)}), bf16[768,3072]{1,0:T(8,128)(2,1)}) %all-gather.21.cloned.1.call-update) | async-done | bytes 4718608 | tf_op jit(solution)/shard_map/all_gather | solution.py:200
  461.9 62.1 %all-gather.23.cloned.1.call-done = bf16[3072,768]{1,0:T(8,128)(2,1)} async-done(((bf16[96,768]{1,0:T(8,128)(2,1)}), bf16[3072,768]{1,0:T(8,128)(2,1)}) %all-gather.23.cloned.1.call-update) | async-done | bytes 4718608 | tf_op jit(solution)/shard_map/all_gather | solution.py:201
  531.5 34.9 %while.39 = (s32[]{:T(128)}, f32[64,12,64]{0,2,1:T(8,128)}, bf16[2,960,1536]{2,1,0:T(8,128)(2,1)}, bf16[2,960,1536]{1,2,0:T(8,128)(2,1)}, bf16[64,12,64]{0,2,1:T...) while((s32[]{:T(128)}, f32[64,12,64]{0,2,1:T(8,128)}, ...), condition=%wide.region_14.15_spmd.clone, body=%wide.region_13.14_spmd.clone.sunk | while | flops 483753984 | bytes 62727348 | solution.py:149
  580.9 11.4 reduce-scatter.13.cloned.1.call-start
  597.6 9.6 convolution_bitcast_fusion.1
  635.0 22.3 %copy.157 = bf16[1,1920,768]{2,0,1:T(2,128)(2,1)} copy(bf16[1,1920,768]{2,1,0:T(8,128)(2,1)S(1)} %fusion.11) | data formatting | bytes 5898240 | tf_op jit(solution)/shard_map/broadcast_in_dim | solution.py:274
  657.9 17.9 %reduce = bf16[1920,768]{1,0:T(8,128)(2,1)S(1)} reduce(bf16[1920,1,768]{2,1,0:T(2,128)(2,1)} %bitcast.224, bf16[]{:T(256)} %broadcast.309), dimensions={1}, to_apply=%bitcast.157.reduce_sub_computation | reduce | bytes 5898242
  695.3 81.8 %all-reduce.8 = (f32[768]{0:T(1024)}, f32[384]{0:T(512)}, f32[768]{0:T(1024)}, f32[768]{0:T(1024)}) all-reduce(f32[768]{0:T(1024)S(1)} %get-tuple-element.317, f32[384]{0:T(512)} %reshape.309, f32[768]{0:T(1024)S(1)} %get-tuple-element.315, f32[768]{0:T(1024)S(1)} %copy-done.49), channel_id=2, replica_groups=mesh['dp'=4,'fsdp'=8] {'dp','fsdp'}, use_global_device_ids=true, to_apply=%region_19.20.clone | all-reduce | flops 2688 | bytes 21504
  798.6 98.4 %reduce-scatter.17.cloned.1.call-done = f32[24,768]{1,0:T(8,128)} async-done(((f32[768,768]{1,0:T(8,128)}), f32[24,768]{1,0:T(8,128)}) %reduce-scatter.17.cloned.1.call-update) | async-done | bytes 73744 | tf_op jit(solution)/shard_map/reduce_scatter | solution.py:335
  897.0 104.6 %reduce-scatter.19.cloned.1.call-done = f32[24,768]{1,0:T(8,128)} async-done(((f32[768,768]{1,0:T(8,128)}), f32[24,768]{1,0:T(8,128)}) %reduce-scatter.19.cloned.1.call-update) | async-done | bytes 73744 | tf_op jit(solution)/shard_map/reduce_scatter | solution.py:337
  1001.7 112.1 %reduce-scatter.13.cloned.1.call-done = f32[24,1536]{1,0:T(8,128)} async-done(((f32[768,1536]{1,0:T(8,128)}), f32[24,1536]{1,0:T(8,128)}) %reduce-scatter.13.cloned.1.call-update) | async-done | bytes 147472 | tf_op jit(solution)/shard_map/reduce_scatter | solution.py:332
  1113.8 112.9 %reduce-scatter.25.cloned.1.call-done = f32[24,1536]{1,0:T(8,128)} async-done(((f32[768,1536]{1,0:T(8,128)}), f32[24,1536]{1,0:T(8,128)}) %reduce-scatter.25.cloned.1.call-update) | async-done | bytes 147472
  1226.7 141.1 %reduce-scatter.21.cloned.1.call-done = f32[24,3072]{1,0:T(8,128)} async-done(((f32[768,3072]{1,0:T(8,128)}), f32[24,3072]{1,0:T(8,128)}) %reduce-scatter.21.cloned.1.call-update) | async-done | bytes 294928 | tf_op jit(solution)/shard_map/reduce_scatter | solution.py:339
  1367.7 142.0 %reduce-scatter.23.cloned.1.call-done = f32[96,768]{1,0:T(8,128)} async-done(((f32[3072,768]{1,0:T(8,128)}), f32[96,768]{1,0:T(8,128)}) %reduce-scatter.23.cloned.1.call-update) | async-done | bytes 294928 | tf_op jit(solution)/shard_map/reduce_scatter | solution.py:340
  (311 shorter events, 182.0 us)
Async XLA Ops:
  7.2 104.8 %all-gather.11.cloned.1.call-start = ((), (), s32[]{:S(2)}) async-start(), calls=%async_computation.11 | async-start | bytes 1216512 | tf_op jit(solution)/shard_map/all_gather | solution.py:192
  7.9 158.4 %all-gather.9.cloned.1.call-start = ((), (), s32[]{:S(2)}) async-start(), calls=%async_computation.10 | async-start | bytes 2433024 | tf_op jit(solution)/shard_map/all_gather | solution.py:193
  8.7 213.6 %all-gather.13.cloned.1.call-start = ((), (), s32[]{:S(2)}) async-start(), calls=%async_computation.12 | async-start | bytes 1216512 | tf_op jit(solution)/shard_map/all_gather | solution.py:194
  9.4 268.8 %all-gather.17.cloned.1.call-start = ((), (), s32[]{:S(2)}) async-start(), calls=%async_computation.14 | async-start | bytes 1216512 | tf_op jit(solution)/shard_map/all_gather | solution.py:196
  10.0 327.2 %all-gather.15.cloned.1.call-start = ((), (), s32[]{:S(2)}) async-start(), calls=%async_computation.13 | async-start | bytes 2433024 | tf_op jit(solution)/shard_map/all_gather | solution.py:197
  10.6 382.5 %all-gather.19.cloned.1.call-start = ((), (), s32[]{:S(2)}) async-start(), calls=%async_computation.15 | async-start | bytes 1216512 | tf_op jit(solution)/shard_map/all_gather | solution.py:198
  11.1 447.4 %all-gather.21.cloned.1.call-start = ((), (), s32[]{:S(2)}) async-start(), calls=%async_computation.16 | async-start | bytes 4866048 | tf_op jit(solution)/shard_map/all_gather | solution.py:200
  11.9 325.2 %all-to-all-start = ((bf16[8,240,768]{2,1,0:T(8,128)(2,1)}), bf16[8,240,768]{2,1,0:T(8,128)(2,1)}, u32[]{:S(2)}, u32[]{:S(2)}) async-start(bf16[8,240,768]{2,1,0:T(8,128)(2,1)} %param.23), calls=%async_computation | async-start | bytes 5898240 | tf_op jit(solution)/shard_map/all_to_all | solution.py:239
  19.4 504.6 %all-gather.23.cloned.1.call-start = ((), (), s32[]{:S(2)}) async-start(), calls=%async_computation.17 | async-start | bytes 4866048 | tf_op jit(solution)/shard_map/all_gather | solution.py:201
  20.1 778.5 %reduce-scatter.11.cloned.1.call-start = ((), (), s32[]{:S(2)}) async-start(), calls=%async_computation.18 | async-start | bytes 2433024 | tf_op jit(solution)/shard_map/reduce_scatter | solution.py:331
  109.9 168.3 %copy-start.44 = (f32[768]{0:T(1024)}, f32[768]{0:T(1024)S(1)}, u32[]{:S(2)}) copy-start(f32[768]{0:T(1024)S(1)} %convert_element_type.294) | copy-start | bytes 9220
  170.3 176.6 %copy-start.34 = (bf16[12,64,64]{2,1,0:T(8,128)(2,1)}, bf16[12,64,64]{2,1,0:T(8,128)(2,1)S(1)}, u32[]{:S(2)}) copy-start(bf16[12,64,64]{2,1,0:T(8,128)(2,1)S(1)} %convolution_convert_fusion.8) | copy-start | bytes 294916
  394.8 135.5 %copy-start.5 = (f32[64,768]{1,0:T(8,128)}, f32[64,768]{1,0:T(8,128)S(1)}, u32[]{:S(2)}) copy-start(f32[64,768]{1,0:T(8,128)S(1)} %get-tuple-element.376) | copy-start | bytes 589828
  394.8 129.2 %copy-start.31 = (f32[1,64,768]{2,1,0:T(8,128)S(1)}, f32[1,64,768]{2,1,0:T(8,128)}, u32[]{:S(2)}) copy-start(f32[1,64,768]{2,1,0:T(8,128)} %param.25) | copy-start | bytes 589828
  394.8 129.1 %copy-start.56 = (f32[64]{0:T(128)S(1)}, f32[64]{0:T(128)}, u32[]{:S(2)}) copy-start(f32[64]{0:T(128)} %compare_convert_fusion) | copy-start | bytes 772
  394.8 135.5 %copy-start.50 = (f32[64]{0:T(128)}, f32[64]{0:T(128)S(1)}, u32[]{:S(2)}) copy-start(f32[64]{0:T(128)S(1)} %fusion.54) | copy-start | bytes 772
  574.9 223.7 %reduce-scatter.15.cloned.1.call-start = ((), (), s32[]{:S(2)}) async-start(), calls=%async_computation.20 | async-start | bytes 2433024 | tf_op jit(solution)/shard_map/reduce_scatter | solution.py:333
  576.9 320.2 %reduce-scatter.17.cloned.1.call-start = ((), (), s32[]{:S(2)}) async-start(), calls=%async_computation.21 | async-start | bytes 2433024 | tf_op jit(solution)/shard_map/reduce_scatter | solution.py:335
  578.9 422.7 %reduce-scatter.19.cloned.1.call-start = ((), (), s32[]{:S(2)}) async-start(), calls=%async_computation.22 | async-start | bytes 2433024 | tf_op jit(solution)/shard_map/reduce_scatter | solution.py:337
  580.9 532.9 %reduce-scatter.13.cloned.1.call-start = ((), (), s32[]{:S(2)}) async-start(), calls=%async_computation.19 | async-start | bytes 4866048 | tf_op jit(solution)/shard_map/reduce_scatter | solution.py:332
  597.6 629.1 %reduce-scatter.25.cloned.1.call-start = ((), (), s32[]{:S(2)}) async-start(), calls=%async_computation.25 | async-start | bytes 4866048
  613.4 754.4 %reduce-scatter.21.cloned.1.call-start = ((), (), s32[]{:S(2)}) async-start(), calls=%async_computation.23 | async-start | bytes 9732096 | tf_op jit(solution)/shard_map/reduce_scatter | solution.py:339
  619.6 890.1 %reduce-scatter.23.cloned.1.call-start = ((), (), s32[]{:S(2)}) async-start(), calls=%async_computation.24 | async-start | bytes 9732096 | tf_op jit(solution)/shard_map/reduce_scatter | solution.py:340
  679.3 109.4 %all-to-all-start.1 = ((bf16[8,2,92160]{2,1,0:T(2,128)(2,1)}), bf16[8,2,92160]{2,1,0:T(2,128)(2,1)S(1)}, u32[]{:S(2)}, u32[]{:S(2)}) async-start(bf16[8,2,92160]{2,1,0:T(2,128)(2,1)} %reshape.325), calls=%async_computation.1 | async-start | bytes 5898240 | tf_op jit(solution)/shard_map/all_to_all | solution.py:274
  (63 other events, 1637.7 us)
Sparse Core Ops, SparseCore 0:
  10.9 96.0 all-gather.10
  109.9 56.2 all-gather.8
  169.2 53.0 all-gather.12
  225.1 53.0 all-gather.16
  280.9 56.1 all-gather.14
  339.9 53.0 all-gather.18
  395.9 62.5 all-gather.20
  461.4 62.4 all-gather.22
  575.0 97.7 reduce-scatter.10
  679.3 113.6 reduce-scatter.14
  798.9 98.0 reduce-scatter.16
  903.6 98.0 reduce-scatter.18
  1007.7 106.0 reduce-scatter.12
  1120.6 106.0 reduce-scatter.24
  1233.0 134.6 reduce-scatter.20
  1375.1 134.5 reduce-scatter.22
where the time goes:
time: 1520 us
  waiting for transfers between devices  1070 us (70%)
  blocking collectives  169 us (11%)
  matrix products  104 us (7%)
  local copies, waits for them, and re-layouts  98.5 us (6%)
  other arithmetic  29.9 us (2%)
  starting transfers between devices  23.7 us (2%)
  between operations  15.8 us (1%)
    unnamed x2, blocking collectives  169 us
    reduce_scatter x1, waiting for transfers between devices, per_device(): lax.psum_scatter(gw_ffout, ('dp', 'fsdp'), scatter_dimension=0, tiled=True)  142 us
    reduce_scatter x1, waiting for transfers between devices, per_device(): lax.psum_scatter(gw_ffin, ('dp', 'fsdp'), scatter_dimension=0, tiled=True)  141 us
    unnamed x17, waiting for transfers between devices  118 us
    reduce_scatter x1, waiting for transfers between devices, per_device(): lax.psum_scatter(gw_selfkv, ('dp', 'fsdp'), scatter_dimension=0, tiled=True)  112 us
    reduce_scatter x1, waiting for transfers between devices, per_device(): lax.psum_scatter(gw_crossout, ('dp', 'fsdp'), scatter_dimension=0, tiled=...  105 us
    reduce_scatter x1, waiting for transfers between devices, per_device(): lax.psum_scatter(gw_crossq, ('dp', 'fsdp'), scatter_dimension=0, tiled=True)  98.4 us
    all_gather x1, waiting for transfers between devices, per_device(): lax.all_gather(ff_in, ('dp', 'fsdp'), axis=0, tiled=True)  63.7 us
  transfers between devices with their start and end apart: 18, of which 13 were waited for; matrix products, arithmetic and copies ran while one was open for 12% of the time, Pallas kernels for 0%

commit v1 on v0

v1 whole, which is shorter than its diff:
```python
import functools
import math

import jax
import jax.numpy as jnp
from jax import lax
from jax.experimental import pallas as pl
from jax.experimental.pallas import tpu as pltpu
from jax.sharding import PartitionSpec as P

HEADS = 12
DK = 64
BUCKETS = 32
QUAD = 4
WIDE = QUAD * DK
EPS = 1e-06
NEG = -1e30
HIGH = lax.Precision.HIGHEST
BF = jnp.bfloat16
F32 = jnp.float32
PIECES = 8
SQ, SK, SV, SO, CQ, CK, CV, CO = range(PIECES)
ZDIM = 4


def up16(n):
    return (n + 15) // 16 * 16


def bucket_limits():
    limits = []
    for target_bucket in range(1, 16):
        distance = 16
        while int(math.log(distance / 16.0) / math.log(8.0) * 16.0) < target_bucket:
            distance = distance + 1
        limits.append(distance)
    return limits


def bucket_of(distance):
    larger = jnp.full_like(distance, 16)
    for limit_value in bucket_limits():
        larger = larger + (distance >= limit_value).astype(jnp.int32)
    return jnp.where(distance < 16, distance, jnp.minimum(larger, 31))


def iota(shape, axis):
    return lax.broadcasted_iota(jnp.int32, shape, axis)


def nn(a, b):
    return lax.dot_general(a, b, (((1,), (0,)), ((), ())), preferred_element_type=F32)


def nt(a, b):
    return lax.dot_general(a, b, (((1,), (1,)), ((), ())), preferred_element_type=F32)


def tn(a, b):
    return lax.dot_general(a, b, (((0,), (0,)), ((), ())), preferred_element_type=F32)


def nn_high(a, b):
    return lax.dot_general(
        a, b, (((1,), (0,)), ((), ())), preferred_element_type=F32, precision=HIGH
    )


def normed(v, gain):
    return v * lax.rsqrt(jnp.mean(v * v, axis=-1, keepdims=True) + EPS) * gain


def norm_back(v, gain, dy):
    s = lax.rsqrt(jnp.mean(v * v, axis=-1, keepdims=True) + EPS)
    dyg = dy * gain
    gain_grad = jnp.sum(dy * v * s, axis=0, keepdims=True)
    dv = s * dyg - v * (s * s * s) * jnp.mean(dyg * v, axis=-1, keepdims=True)
    return dv, gain_grad


def gelu_pair(u):
    cst = 0.7978845608028654
    cubic = 0.044715
    th = jnp.tanh(cst * (u + cubic * u * u * u))
    half = 0.5 * (1.0 + th)
    slope = half + 0.5 * u * (1.0 - th * th) * cst * (1.0 + 3.0 * cubic * u * u)
    return u * half, slope


class Sizes:
    def __init__(self, mesh_shape, width, rows, targets, shard, ff_shard, hidden):
        self.Z = ZDIM
        self.X = mesh_shape["dp"] // 2
        self.Y = mesh_shape["fsdp"] // self.Z
        self.D = width
        self.R = rows
        self.T = targets
        self.r = shard
        self.rb = up16(2 * shard)
        self.nh = width // 2
        self.rff = ff_shard
        self.rbf = up16(2 * ff_shard)
        self.rfi = up16(shard)
        self.inside = shard % 8 == 0
        self.hid = hidden


def sems(sz):
    return 13 * sz.Y * sz.Z + 20 * (sz.X + sz.Y + sz.Z) + 8 * sz.X * sz.Y


def layout(sz):
    X, Y, Z, D, T, R = sz.X, sz.Y, sz.Z, sz.D, sz.T, sz.R
    rb, nh, rbf, rfi, hid = sz.rb, sz.nh, sz.rbf, sz.rfi, sz.hid
    half = PIECES // 2
    V = pltpu.VMEM
    sums = dict(
        rc=V((PIECES, X, Y, Z, rb, nh), BF),
        r1a=V((half, X - 1, Y, Z, rb, nh), BF),
        r1b=V((half, Y - 1, X, Z, rb, nh), BF),
        r2a=V((half, Y - 1, Z, rb, nh), BF),
        r2b=V((half, X - 1, Z, rb, nh), BF),
        rz=V((PIECES, Z - 1, rb, nh), BF),
    )
    return dict(
        **(sums if sz.inside else {}),
        gw=V((PIECES, 2, X, Y, Z, rb, nh), BF),
        w=V((PIECES, D, D), BF),
        acc=V((D, D), F32),
        lift=V((Y * Z * sz.r if sz.r % 8 else 8, D), F32),
        cell=V((max(rb, rbf, rfi), max(nh, hid)), F32),
        smb=V((2, X, Y, Z, 16, 128), BF),
        gain=V((16, D), F32),
        bias=V((HEADS // QUAD, WIDE, T), F32),
        spread=V((128, D), F32),
        mask=V((WIDE, WIDE), BF),
        pas=V((Y * Z, R, D), BF),
        kv=V((Y * Z, R, 2 * D), BF),
        h1=V((T, D), BF),
        qs=V((T, D), BF),
        ks=V((T, D), BF),
        vs=V((T, D), BF),
        os=V((T, D), BF),
        ps=V((HEADS // QUAD, WIDE, T), F32),
        x1=V((T, D), F32),
        h2=V((T, D), BF),
        x2=V((T, D), F32),
        oc=V((T, D), BF),
        dx=V((T, D), F32),
        qc=V((Z, Y, T, D), BF),
        h3=V((Z, Y, T, D), BF),
        g3=V((Z, Y, T, D), BF),
        do=V((Z, Y, T, D), BF),
        dr=V((Z, Y, 8, D), F32),
        po=V((Y, Z, T, D), BF),
        pst=V((Y, Z, T, 128), F32),
        ryo=V((Y - 1, Z, T, D), BF),
        ryst=V((Y - 1, Z, T, 128), F32),
        rzo=V((Z - 1, T, D), BF),
        rzst=V((Z - 1, T, 128), F32),
        py=V((Y, Z, T, D), BF),
        ryy=V((Y - 1, Z, T, D), BF),
        rzy=V((Z - 1, T, D), BF),
        fog=V((2, X, rbf, nh), BF),
        fo=V((hid, D), BF),
        fz=V((Z, Y, rfi, hid), BF),
        fig=V((2, X, Y, Z, rfi, hid), BF),
        fi=V((D, hid), BF),
        gl=V((Y, Z * T, hid), BF),
        du=V((Y, Z * T, hid), BF),
        gfo=V((2, X, rbf, nh), BF),
        rfo1=V((X, rbf, nh), BF),
        rfo2=V((X - 1, rbf, nh), BF),
        gfi=V((2, X, Y, Z, rfi, hid), BF),
        rfi1=V((X, Y, Z, rfi, hid), BF),
        rfi2=V((X - 1, Y, Z, rfi, hid), BF),
        rfi3=V((Y - 1, Z, rfi, hid), BF),
        rfi4=V((Z - 1, Y, rfi, hid), BF),
        sm=V((8, D), F32),
        rsm=V((1 + (X - 1) + (Y - 1) + (Z - 1), 8, D), F32),
        ssem=pltpu.SemaphoreType.DMA((sems(sz),)),
        rsem=pltpu.SemaphoreType.DMA((sems(sz),)),
        lsem=pltpu.SemaphoreType.DMA((1 + Y * Z,)),
    )


INPUTS = ("tok", "pas_in", "live", "og", "small", "sq", "skv", "so", "cq", "ckv", "co", "fi_in", "fo_in")
OUTPUTS = (
    "bo", "tg", "pg", "g_ls", "g_rb", "g_sq", "g_skv", "g_so",
    "g_lc", "g_cq", "g_ckv", "g_co", "g_lf", "g_fi", "g_fo",
)


def block_kernel(sz, names, *refs):
    n_in, n_out = len(INPUTS), len(OUTPUTS)
    m = dict(zip(INPUTS, refs[:n_in]))
    m.update(zip(OUTPUTS, refs[n_in : n_in + n_out]))
    m.update(zip(names, refs[n_in + n_out :]))
    X, Y, Z, D, T, R = sz.X, sz.Y, sz.Z, sz.D, sz.T, sz.R
    r, rb, nh, rff, rbf, rfi, hid = sz.r, sz.rb, sz.nh, sz.rff, sz.rbf, sz.rfi, sz.hid
    NQ = HEADS // QUAD
    YZ = Y * Z
    dp = lax.axis_index("dp")
    fs = lax.axis_index("fsdp")
    x, c = dp // 2, dp % 2
    z, y = fs // Y, fs % Y
    oth = 1 - c

    def xs(b):
        return (x + b) % X

    def ys(b):
        return (y + b) % Y

    def zs(b):
        return (z + b) % Z

    def dev(x_=None, c_=None, y_=None, z_=None):
        x_ = x if x_ is None else x_
        c_ = c if c_ is None else c_
        y_ = y if y_ is None else y_
        z_ = z if z_ is None else z_
        return (x_ * 2 + c_, z_ * Y + y_)

    ssem, rsem, lsem = m["ssem"], m["rsem"], m["lsem"]
    n_sems = sems(sz)
    used = [0]
    pending = []

    def take(n=1):
        at = used[0]
        used[0] += n
        assert used[0] <= n_sems
        return at

    def copy_at(i, src, dst, to):
        return pltpu.make_async_remote_copy(
            src_ref=src, dst_ref=dst, send_sem=ssem.at[i], recv_sem=rsem.at[i],
            device_id=to, device_id_type=pl.DeviceIdType.MESH,
        )

    def send(src, dst, to):
        cp = copy_at(take(), src, dst, to)
        cp.start()
        pending.append(cp)
        return cp

    def got(cps):
        for cp in cps:
            cp.wait_recv()

    def sent(cps):
        for cp in cps:
            cp.wait_send()
        pending[:] = [cp for cp in pending if all(cp is not done for done in cps)]

    def drain():
        sent(list(pending))

    partners = [dev(c_=oth)]
    partners += [dev(x_=xs(b)) for b in range(1, X)]
    partners += [dev(y_=ys(b)) for b in range(1, Y)]
    partners += [dev(z_=zs(b)) for b in range(1, Z)]
    bar = pltpu.get_barrier_semaphore()
    for p in partners:
        pl.semaphore_signal(bar, inc=1, device_id=p, device_id_type=pl.DeviceIdType.MESH)
    load_pas = pltpu.make_async_copy(m["pas_in"], m["pas"], lsem.at[0])
    load_pas.start()
    pl.semaphore_wait(bar, len(partners))

    mask = m["mask"]
    mask[...] = (iota((WIDE, WIDE), 0) // DK == iota((WIDE, WIDE), 1) // DK).astype(F32).astype(BF)

    def stack4(v):
        return jnp.concatenate([v, v, v, v], axis=0) * mask[...]

    def fold4(u):
        lane = iota((T, WIDE), 1)
        out = u[0:T]
        for h in range(1, QUAD):
            out = jnp.where(lane >= h * DK, u[h * T : (h + 1) * T], out)
        return out

    def quad(t):
        return slice(t * WIDE, (t + 1) * WIDE)

    cell, lift = m["cell"], m["lift"]

    def put_halves(dst, left, right, rows, total):
        if rows % 8 == 0 and 2 * rows == total:
            dst[...] = jnp.concatenate([left, right], axis=0).astype(BF)
        else:
            cols = left.shape[1]
            cell[0:total, 0:cols] = jnp.zeros((total, cols), F32)
            cell[0:rows, 0:cols] = left
            cell[rows : 2 * rows, 0:cols] = right
            dst[...] = cell[0:total, 0:cols].astype(BF)

    def get_halves(v, rows):
        if rows % 8 == 0:
            return v[0:rows], v[rows : 2 * rows]
        cell[0 : v.shape[0], 0 : v.shape[1]] = v
        return cell[0:rows, 0 : v.shape[1]], cell[rows : 2 * rows, 0 : v.shape[1]]

    def ag_z(buf):
        return [
            send(buf.at[c, x, y, z], buf.at[c, x, y, z], dev(z_=zs(a))) for a in range(1, Z)
        ]

    def line_to(buf, y_first):
        if y_first:
            return [send(buf.at[c, x, y], buf.at[c, x, y], dev(y_=ys(b))) for b in range(1, Y)]
        return [send(buf.at[c, x, y], buf.at[c, x, y], dev(x_=xs(b))) for b in range(1, X)]

    def ag_t2(buf, y_first):
        out = []
        if y_first:
            for b in range(1, Y):
                for d in range(1, X):
                    out.append(send(buf.at[c, x, ys(b)], buf.at[c, x, ys(b)], dev(x_=xs(d))))
        else:
            for b in range(1, X):
                for d in range(1, Y):
                    out.append(send(buf.at[c, xs(b), y], buf.at[c, xs(b), y], dev(y_=ys(d))))
        return out

    def ag_core(buf):
        return [send(buf.at[c], buf.at[c], dev(c_=oth))]

    gw, w, smb = m["gw"], m["w"], m["smb"]
    smb[c, x, y, z] = m["small"][...]
    sources = (
        (m["sq"], 0), (m["skv"], 0), (m["skv"], D), (m["so"], 0),
        (m["cq"], 0), (m["ckv"], 0), (m["ckv"], D), (m["co"], 0),
    )
    for p, (ref, off) in enumerate(sources):
        v = ref[:, off : off + D].astype(F32)
        put_halves(gw.at[p, c, x, y, z], v[:, 0:nh], v[:, nh:D], r, rb)
    steps = [[(smb, True), (gw.at[0], True)]]
    steps += [[(gw.at[p], p % 2 == 0)] for p in range(1, PIECES)]
    zc = [[ag_z(buf) for buf, _ in group] for group in steps]

    g3 = m["g3"]
    live = m["live"][:, 0:1]
    g3[z, y] = (live * m["og"][...]).astype(BF)

    def act_start(base, bufs):
        for n, buf in enumerate(bufs):
            for a in range(1, Z):
                copy_at(base + n * YZ + a, buf.at[z, y], buf.at[z, y], dev(z_=zs(a))).start()

    def act_forward(base, bufs, a):
        zi = zs(a)
        for n, buf in enumerate(bufs):
            for b in range(1, Y):
                copy_at(
                    base + n * YZ + b * Z + (Z - a) % Z, buf.at[zi, y], buf.at[zi, y], dev(y_=ys(b))
                ).start()

    def act_wait(base, bufs, t):
        at = base + (Y - t // Z) % Y * Z + (Z - t % Z) % Z
        for n, buf in enumerate(bufs):
            copy_at(at + n * YZ, buf.at[z, y], buf.at[z, y], dev(z_=zs(1))).wait_recv()

    def act_done(base, bufs):
        for n, buf in enumerate(bufs):
            for t in range(1, YZ):
                copy_at(base + n * YZ + t, buf.at[z, y], buf.at[z, y], dev(z_=zs(1))).wait_send()

    g3_base = take(YZ)
    act_start(g3_base, [g3])
    fog, fo, fz, fig, fi = m["fog"], m["fo"], m["fz"], m["fig"], m["fi"]
    fz[z] = m["fi_in"][pl.ds(z * Y, Y)]
    fi_z = [
        send(m["fi_in"].at[pl.ds(zs(a) * Y, Y)], fz.at[z], dev(z_=zs(a))) for a in range(1, Z)
    ]
    vfo = m["fo_in"][...].astype(F32)
    put_halves(fog.at[c, x], vfo[:, 0:nh], vfo[:, nh:D], rff, rbf)
    fo_x = [send(fog.at[c, x], fog.at[c, x], dev(x_=xs(b))) for b in range(1, X)]

    spread = m["spread"]
    lane = iota((128, D), 1)
    row = iota((128, D), 0)
    spread[...] = ((lane >= row * DK) & (lane < row * DK + DK)).astype(F32)
    tlane = iota((T, 128), 1)

    def unpack(p):
        group = 2 * Y * r

        def body(g, carry):
            x_ = g // (2 * (Z // 2))
            c_ = (g // (Z // 2)) % 2
            zp = g % (Z // 2)
            lefts, rights = [], []
            at = 0
            for dz in range(2):
                for yy in range(Y):
                    lo, hi = get_halves(gw[p, c_, x_, yy, 2 * zp + dz].astype(F32), r)
                    if r % 8 == 0:
                        lefts.append(lo)
                        rights.append(hi)
                    else:
                        lift[at : at + r, 0:nh] = lo
                        lift[at : at + r, nh:D] = hi
                    at += r
            rows = pl.ds(pl.multiple_of(g * group, 16), group)
            if r % 8 == 0:
                w[p, rows, 0:nh] = jnp.concatenate(lefts, axis=0).astype(BF)
                w[p, rows, nh:D] = jnp.concatenate(rights, axis=0).astype(BF)
            else:
                w[p, rows, :] = lift[0:group, :].astype(BF)
            return carry

        lax.fori_loop(0, X * 2 * (Z // 2), body, 0)

    gain = m["gain"]
    bias = m["bias"]
    rbs = HEADS * BUCKETS // (2 * X * YZ)

    def read_small():
        gain[...] = jnp.zeros_like(gain)
        flat = HEADS * BUCKETS

        def body(k, tot):
            c_ = (k // YZ) % 2
            x_ = k // (2 * YZ)
            z_ = (k % YZ) // Y
            y_ = k % Y
            b = smb[c_, x_, y_, z_]
            l0, n0 = iota((128, D), 0), iota((128, D), 1)
            place = ((n0 - l0 == k * r) & (l0 < r)).astype(F32).astype(BF)
            gain[...] += nn(b, place)
            l1, n1 = iota((128, flat), 0), iota((128, flat), 1)
            place1 = ((n1 - l1 == k * rbs) & (l1 < rbs)).astype(F32).astype(BF)
            return tot + nn(b, place1)

        tot = lax.fori_loop(0, 2 * X * YZ, body, jnp.zeros((16, flat), F32))
        per = jnp.broadcast_to(tot[3:4, :], (16, flat))
        h0, n0 = iota((16, flat), 0), iota((16, flat), 1)
        per = jnp.where((n0 >= h0 * BUCKETS) & (n0 < h0 * BUCKETS + BUCKETS), per, 0.0)
        nb, mb = iota((flat, 128), 0), iota((flat, 128), 1)
        dist = jnp.where(mb == 0, 0, 128 - mb)
        hot = ((nb & (BUCKETS - 1)) == bucket_of(dist)).astype(F32).astype(BF)
        table = nn(per.astype(BF), hot)
        for h in range(HEADS):
            wide = jnp.broadcast_to(table[h : h + 1, :], (T, 128))
            rolled = pltpu.roll(wide, 0, 1, stride=1, stride_axis=0)
            bias[h // QUAD, (h % QUAD) * T : (h % QUAD + 1) * T, :] = rolled[:, 0:T]

    tok = m["tok"]

    def self_forward():
        m["h1"][...] = normed(tok[...], gain[0:1, :]).astype(BF)
        h1 = m["h1"][...]
        m["qs"][...] = nn(h1, w[SQ]).astype(BF)
        m["ks"][...] = nn(h1, w[SK]).astype(BF)
        m["vs"][...] = nn(h1, w[SV]).astype(BF)
        allowed = iota((WIDE, T), 1) <= (iota((WIDE, T), 0) & (T - 1))
        for t in range(NQ):
            s = nt(stack4(m["qs"][:, quad(t)]), m["ks"][:, quad(t)]) + bias[t]
            s = jnp.where(allowed, s, NEG)
            e = jnp.exp(s - jnp.max(s, axis=1, keepdims=True))
            pr = e / jnp.sum(e, axis=1, keepdims=True)
            m["ps"][t] = pr
            m["os"][:, quad(t)] = fold4(nn(pr.astype(BF), m["vs"][:, quad(t)])).astype(BF)

    qc = m["qc"]
    qc_base = take(YZ)

    def self_out():
        x1 = tok[...] + nn(m["os"][...], w[SO])
        m["x1"][...] = x1
        m["h2"][...] = normed(x1, gain[1:2, :]).astype(BF)

    def cross_query():
        qc[z, y] = nn(m["h2"][...], w[CQ]).astype(BF)
        act_start(qc_base, [qc])

    kv, pas = m["kv"], m["pas"]

    def project(p, off):
        def body(q, carry):
            kv[q, :, off : off + D] = nn(pas[q], w[p]).astype(BF)
            return carry

        lax.fori_loop(0, YZ, body, 0)

    def g3_forward():
        for a in range(Z):
            if a:
                act_wait(g3_base, [g3], a)
            act_forward(g3_base, [g3], a)

    def ff_unpack():
        for x_ in range(X):
            for c_ in range(2):
                lo, hi = get_halves(fog[c_, x_].astype(F32), rff)
                rows = slice((x_ * 2 + c_) * rff, (x_ * 2 + c_ + 1) * rff)
                if rff % 16 == 0:
                    fo[rows, 0:nh] = lo.astype(BF)
                    fo[rows, nh:D] = hi.astype(BF)
                else:
                    m["acc"][rows, 0:nh] = lo
                    m["acc"][rows, nh:D] = hi
        if rff % 16:
            fo[...] = m["acc"][0:hid, 0:D].astype(BF)
        group = 2 * Y * r

        def body(g, carry):
            x_ = g // (2 * (Z // 2))
            c_ = (g // (Z // 2)) % 2
            zp = g % (Z // 2)
            parts = []
            at = 0
            for dz in range(2):
                for yy in range(Y):
                    v = fig[c_, x_, yy, 2 * zp + dz].astype(F32)
                    if r % 8 == 0:
                        parts.append(v[0:r])
                    else:
                        cell[0:rfi, 0:hid] = v
                        lift[at : at + r, 0:hid] = cell[0:r, 0:hid]
                    at += r
            rows = pl.ds(pl.multiple_of(g * group, 16), group)
            if r % 8 == 0:
                fi[rows, :] = jnp.concatenate(parts, axis=0).astype(BF)
            else:
                fi[rows, :] = lift[0:group, 0:hid].astype(BF)
            return carry

        lax.fori_loop(0, X * 2 * (Z // 2), body, 0)

    ff_state = {}

    def ff_step(k):
        if k == 0:
            got(fi_z)
            fig[c, x, y] = fz[:, pl.ds(y, 1)].reshape(Z, rfi, hid)
            ff_state["y"] = [
                send(fz.at[:, ys(b)], fig.at[c, x, y], dev(y_=ys(b))) for b in range(1, Y)
            ]
            got(fo_x)
            ff_state["fo"] = [send(fog.at[c], fog.at[c], dev(c_=oth))]
        elif k == 1:
            got(ff_state["y"])
            ff_state["x"] = [
                send(fig.at[c, x], fig.at[c, x], dev(x_=xs(b))) for b in range(1, X)
            ]
        elif k == 2:
            got(ff_state["x"])
            ff_state["core"] = [send(fig.at[c], fig.at[c], dev(c_=oth))]
        elif k == 3:
            got(ff_state["core"])
            got(ff_state["fo"])
            ff_unpack()

    def after(p):
        if p == 0:
            read_small()
        elif p == SV:
            self_forward()
        elif p == SO:
            self_out()
        elif p == CQ:
            cross_query()
        elif p == CK:
            load_pas.wait()
            project(CK, 0)
        elif p == CV:
            project(CV, D)

    sc, tc, cc = {}, {}, {}
    n_steps = len(steps)
    for s in range(n_steps + 3):
        if s < n_steps:
            sc[s], tc[s] = [], []
            for cps, (buf, y_first) in zip(zc[s], steps[s]):
                got(cps)
                sc[s].append(line_to(buf, y_first))
                tc[s].append(line_to(buf, not y_first))
        if 0 <= s - 1 < n_steps:
            for n, (buf, y_first) in enumerate(steps[s - 1]):
                got(sc[s - 1][n])
                tc[s - 1][n] = tc[s - 1][n] + ag_t2(buf, y_first)
        if 0 <= s - 2 < n_steps:
            cc[s - 2] = []
            for n, (buf, y_first) in enumerate(steps[s - 2]):
                got(tc[s - 2][n])
                cc[s - 2].append(ag_core(buf))
        if s == 4:
            g3_forward()
            ff_step(0)
        elif s == 6:
            ff_step(1)
        elif s == 8:
            ff_step(2)
        if 0 <= s - 3 < n_steps:
            for cps in cc[s - 3]:
                got(cps)
            unpack(s - 3)
            after(s - 3)
    ff_step(3)
    drain()

    po, pst, ryo, ryst, rzo, rzst = (m[k] for k in ("po", "pst", "ryo", "ryst", "rzo", "rzst"))

    def rs_y_base():
        return take((Y - 1) * Z)

    def rs_y_send(base, src, dst, b, a):
        zi = zs(a)
        copy_at(base + (b - 1) * Z + a, src.at[b, zi], dst.at[b - 1, zi], dev(y_=ys(b))).start()

    def rs_y_wait(base, src, dst, b, a):
        copy_at(base + (b - 1) * Z + a, src.at[b, 0], dst.at[b - 1, 0], dev(y_=ys(1))).wait_recv()

    def rs_y_done(base, src, dst):
        for b in range(1, Y):
            for a in range(Z):
                copy_at(
                    base + (b - 1) * Z + a, src.at[b, 0], dst.at[b - 1, 0], dev(y_=ys(1))
                ).wait_send()

    yo_base, yst_base = rs_y_base(), rs_y_base()

    def attend(t, carry):
        a = t % Z
        b = t // Z
        zi = zs(a)
        yi = ys(b)
        qi = zi * Y + yi

        @pl.when(t > 0)
        def _():
            act_wait(qc_base, [qc], t)

        @pl.when(t < Z)
        def _():
            act_forward(qc_base, [qc], a)

        st = jnp.zeros((T, 128), F32)
        for k in range(NQ):
            qb = stack4(qc[zi, yi, :, quad(k)])
            s = nt(qb, kv[qi, :, quad(k)])
            top = jnp.max(s, axis=1, keepdims=True)
            e = jnp.exp(s - top)
            tot = jnp.sum(e, axis=1, keepdims=True)
            u = nn(e.astype(BF), kv[qi, :, D + k * WIDE : D + (k + 1) * WIDE])
            po[b, zi, :, quad(k)] = fold4(u * (1.0 / tot)).astype(BF)
            lse = top + jnp.log(tot)
            for h in range(QUAD):
                st = jnp.where(tlane == k * QUAD + h, lse[h * T : (h + 1) * T], st)
        pst[b, zi] = st

        @pl.when(t >= Z)
        def _():
            rs_y_send(yo_base, po, ryo, b, a)
            rs_y_send(yst_base, pst, ryst, b, a)

        return carry

    lax.fori_loop(0, YZ, attend, 0)

    def merge(parts):
        top = parts[0][1]
        for _, st in parts[1:]:
            top = jnp.maximum(top, st)
        ws = [jnp.exp(st - top) for _, st in parts]
        tot = ws[0]
        for v in ws[1:]:
            tot = tot + v
        out = jnp.zeros((T, D), F32)
        for (o, _), v in zip(parts, ws):
            out = out + nn_high(v / tot, spread[...]) * o.astype(F32)
        return out, top + jnp.log(tot)

    zo = []
    for a in range(1, Z):
        zi = zs(a)
        for b in range(1, Y):
            rs_y_wait(yo_base, po, ryo, b, a)
            rs_y_wait(yst_base, pst, ryst, b, a)
        o, st = merge([(po[0, zi], pst[0, zi])] + [(ryo[b - 1, zi], ryst[b - 1, zi]) for b in range(1, Y)])
        po[0, zi] = o.astype(BF)
        pst[0, zi] = st
        zo.append(send(po.at[0, zi], rzo.at[a - 1], dev(z_=zi)))
        zo.append(send(pst.at[0, zi], rzst.at[a - 1], dev(z_=zi)))
    for b in range(1, Y):
        rs_y_wait(yo_base, po, ryo, b, 0)
        rs_y_wait(yst_base, pst, ryst, b, 0)
    got(zo)
    o, lse = merge(
        [(po[0, z], pst[0, z])]
        + [(ryo[b - 1, z], ryst[b - 1, z]) for b in range(1, Y)]
        + [(rzo[a - 1], rzst[a - 1]) for a in range(1, Z)]
    )
    m["oc"][...] = o.astype(BF)
    m["pst"][0, z] = lse
    x2 = m["x1"][...] + nn(m["oc"][...], w[CO])
    m["x2"][...] = x2
    h3 = m["h3"]
    h3[z, y] = normed(x2, gain[2:3, :]).astype(BF)
    h3_base = take(YZ)
    act_start(h3_base, [h3])
    act_done(qc_base, [qc])
    rs_y_done(yo_base, po, ryo)
    rs_y_done(yst_base, pst, ryst)

    ph, ryh, rzh = po, ryo, rzo
    py, ryy, rzy = (m[k] for k in ("py", "ryy", "rzy"))
    sent(zo)
    gl, du = m["gl"], m["du"]
    yh = []
    for b in range(Y):
        yi = ys(b)
        for a in range(Z):
            if b or a:
                act_wait(h3_base, [h3], b * Z + a)
            if b == 0:
                act_forward(h3_base, [h3], a)
            else:
                act_wait(g3_base, [g3], b * Z + a)
        hb = h3[:, pl.ds(yi, 1)].reshape(Z * T, D)
        gb = g3[:, pl.ds(yi, 1)].reshape(Z * T, D)
        u = nn(hb, fi[...])
        act, slope = gelu_pair(u)
        gl[b] = act.astype(BF)
        du[b] = (nt(gb, fo[...]) * slope).astype(BF)
        ph[b] = nt(du[b], fi[...]).astype(BF).reshape(Z, T, D)
        if b:
            yh.append(send(ph.at[b], ryh.at[b - 1], dev(y_=yi)))
    yy = []
    for b in range(Y):
        py[b] = nn(gl[b], fo[...]).astype(BF).reshape(Z, T, D)
        if b:
            yy.append(send(py.at[b], ryy.at[b - 1], dev(y_=ys(b))))
    act_done(h3_base, [h3])
    act_done(g3_base, [g3])

    def rs_z_stage(part, ry, rzb):
        cps = []
        for a in range(1, Z):
            zi = zs(a)
            tot = part[0, zi].astype(F32)
            for b in range(1, Y):
                tot = tot + ry[b - 1, zi].astype(F32)
            part[0, zi] = tot.astype(BF)
            cps.append(send(part.at[0, zi], rzb.at[a - 1], dev(z_=zi)))
        return cps

    def rs_total(part, ry, rzb):
        tot = part[0, z].astype(F32)
        for b in range(1, Y):
            tot = tot + ry[b - 1, z].astype(F32)
        for a in range(1, Z):
            tot = tot + rzb[a - 1].astype(F32)
        return tot

    got(yh)
    zh = rs_z_stage(ph, ryh, rzh)

    acc = m["acc"]
    gfo, rfo1, rfo2 = m["gfo"], m["rfo1"], m["rfo2"]
    gfi, rfi1, rfi2, rfi3, rfi4 = (m[k] for k in ("gfi", "rfi1", "rfi2", "rfi3", "rfi4"))

    def add_to(dst, src):
        dst[...] = (dst[...].astype(F32) + src[...].astype(F32)).astype(BF)

    def ff_out_grad():
        for b in range(Y):
            v = tn(gl[b], g3[:, pl.ds(ys(b), 1)].reshape(Z * T, D))
            if b == 0:
                acc[0:hid, 0:D] = v
            else:
                acc[0:hid, 0:D] += v
        for x_ in range(X):
            for c_ in range(2):
                lo = (x_ * 2 + c_) * rff
                put_halves(
                    gfo.at[c_, x_], acc[lo : lo + rff, 0:nh], acc[lo : lo + rff, nh:D], rff, rbf
                )
        return [send(gfo.at[oth], rfo1, dev(c_=oth))]

    def ff_in_grad():
        for b in range(Y):
            v = tn(h3[:, pl.ds(ys(b), 1)].reshape(Z * T, D), du[b])
            if b == 0:
                acc[:, 0:hid] = v
            else:
                acc[:, 0:hid] += v
        group = YZ * r

        def body(k, carry):
            x_ = k // 2
            c_ = k % 2
            if r % 8:
                lift[0:group, 0:hid] = acc[pl.ds(pl.multiple_of(k * group, 8), group), 0:hid]
            for z_ in range(Z):
                for y_ in range(Y):
                    at = (z_ * Y + y_) * r
                    if r % 8 == 0:
                        v = acc[pl.ds(pl.multiple_of(k * group + at, 8), r), 0:hid]
                        pad = jnp.zeros((rfi - r, hid), F32)
                        gfi[c_, x_, y_, z_] = jnp.concatenate([v, pad], axis=0).astype(BF)
                    else:
                        cell[0:rfi, 0:hid] = jnp.zeros((rfi, hid), F32)
                        cell[0:r, 0:hid] = lift[at : at + r, 0:hid]
                        gfi[c_, x_, y_, z_] = cell[0:rfi, 0:hid].astype(BF)
            return carry

        lax.fori_loop(0, 2 * X, body, 0)
        return [send(gfi.at[oth], rfi1, dev(c_=oth))]

    def ff_out_x(cps):
        got(cps)
        for x_ in range(X):
            add_to(gfo.at[c, x_], rfo1.at[x_])
        return [send(gfo.at[c, xs(b)], rfo2.at[b - 1], dev(x_=xs(b))) for b in range(1, X)]

    def ff_out_end(cps):
        got(cps)
        v = gfo[c, x].astype(F32)
        for b in range(1, X):
            v = v + rfo2[b - 1].astype(F32)
        lo, hi = get_halves(v, rff)
        m["g_fo"][:, 0:nh] = lo
        m["g_fo"][:, nh:D] = hi

    def ff_in_x(cps):
        got(cps)
        for x_ in range(X):
            for y_ in range(Y):
                add_to(gfi.at[c, x_, y_], rfi1.at[x_, y_])
        return [send(gfi.at[c, xs(b)], rfi2.at[b - 1], dev(x_=xs(b))) for b in range(1, X)]

    def ff_in_y(cps):
        got(cps)
        for b in range(1, X):
            for y_ in range(Y):
                add_to(gfi.at[c, x, y_], rfi2.at[b - 1, y_])
        return [send(gfi.at[c, x, ys(b)], rfi3.at[b - 1], dev(y_=ys(b))) for b in range(1, Y)]

    def ff_in_z(cps):
        got(cps)
        out = []
        for a in range(1, Z):
            zi = zs(a)
            out.append(send(gfi.at[c, x, y, zi], rfi4.at[a - 1, 0], dev(z_=zi)))
            for b in range(1, Y):
                out.append(send(rfi3.at[b - 1, zi], rfi4.at[a - 1, b], dev(z_=zi)))
        return out

    def ff_in_end(cps):
        got(cps)
        for a in range(Z):
            for b in range(Y):
                j = zs(Z - a) * Y + ys(Y - b)
                if a:
                    v = rfi4[a - 1, b]
                elif b:
                    v = rfi3[b - 1, z]
                else:
                    v = gfi[c, x, y, z]
                v = v.astype(F32)
                if r % 8 == 0:
                    m["g_fi"][j] = v[0:r]
                else:
                    cell[0:rfi, 0:hid] = v
                    m["g_fi"][j] = cell[0:r, 0:hid]

    rc, r1a, r1b, r2a, r2b, rz = (m.get(k) for k in ("rc", "r1a", "r1b", "r2a", "r2b", "rz"))

    def pack_grad(p):
        group = YZ * r
        if not sz.inside:
            name, off = targets[p]
            out = m[name].at[:, off : off + D]
            cp = pltpu.make_async_copy(acc, out, lsem.at[0])
            cp.start()
            cp.wait()
            return None

        def body(k, carry):
            x_ = k // 2
            c_ = k % 2
            for z_ in range(Z):
                for y_ in range(Y):
                    rows = pl.ds(pl.multiple_of(k * group + (z_ * Y + y_) * r, 8), r)
                    left, right = acc[rows, 0:nh], acc[rows, nh:D]
                    put_halves(gw.at[p, c_, x_, y_, z_], left, right, r, rb)
            return carry

        lax.fori_loop(0, 2 * X, body, 0)
        return [send(gw.at[p, oth], rc.at[p], dev(c_=oth))]

    def rs_first(p, cps):
        got(cps)

        def body(k, carry):
            x_ = k // Y
            y_ = k % Y
            add_to(gw.at[p, c, x_, y_], rc.at[p, x_, y_])
            return carry

        lax.fori_loop(0, X * Y, body, 0)
        if p % 2 == 0:
            return [
                send(gw.at[p, c, xs(b)], r1a.at[p // 2, b - 1], dev(x_=xs(b))) for b in range(1, X)
            ]
        return [
            send(gw.at[p, c, :, ys(b)], r1b.at[p // 2, b - 1], dev(y_=ys(b))) for b in range(1, Y)
        ]

    def rs_second(p, cps):
        got(cps)
        if p % 2 == 0:
            for b in range(1, X):
                for y_ in range(Y):
                    add_to(gw.at[p, c, x, y_], r1a.at[p // 2, b - 1, y_])
            return [
                send(gw.at[p, c, x, ys(b)], r2a.at[p // 2, b - 1], dev(y_=ys(b)))
                for b in range(1, Y)
            ]
        for b in range(1, Y):
            for x_ in range(X):
                add_to(gw.at[p, c, x_, y], r1b.at[p // 2, b - 1, x_])
        return [
            send(gw.at[p, c, xs(b), y], r2b.at[p // 2, b - 1], dev(x_=xs(b))) for b in range(1, X)
        ]

    def rs_third(p, cps):
        got(cps)
        if p % 2 == 0:
            for b in range(1, Y):
                add_to(gw.at[p, c, x, y], r2a.at[p // 2, b - 1])
        else:
            for b in range(1, X):
                add_to(gw.at[p, c, x, y], r2b.at[p // 2, b - 1])
        return [
            send(gw.at[p, c, x, y, zs(a)], rz.at[p, a - 1], dev(z_=zs(a))) for a in range(1, Z)
        ]

    targets = {
        SQ: ("g_sq", 0), SK: ("g_skv", 0), SV: ("g_skv", D), SO: ("g_so", 0),
        CQ: ("g_cq", 0), CK: ("g_ckv", 0), CV: ("g_ckv", D), CO: ("g_co", 0),
    }

    def rs_last(p, cps):
        got(cps)
        v = gw[p, c, x, y, z].astype(F32)
        for a in range(1, Z):
            v = v + rz[p, a - 1].astype(F32)
        lo, hi = get_halves(v, r)
        name, off = targets[p]
        m[name][:, off : off + nh] = lo
        m[name][:, off + nh : off + D] = hi

    stages = (rs_first, rs_second, rs_third, rs_last) if sz.inside else ()
    moving = {}

    def grad_of(p, lhs, rhs):
        acc[...] = tn(lhs, rhs)
        grad_out(p)

    def grad_out(p):
        moving[p] = (0, pack_grad(p))

    def push(p):
        k, cps = moving[p]
        if k < len(stages):
            moving[p] = (k + 1, stages[k](p, cps))

    def push_all(ps):
        for p in ps:
            push(p)

    fo_c = ff_out_grad()
    fi_c = ff_in_grad()
    got(zh)
    sm = m["sm"]
    sm[...] = jnp.zeros_like(sm)
    dh3 = rs_total(ph, ryh, rzh)
    dv, gg = norm_back(m["x2"][...], gain[2:3, :], dh3)
    sm[2:3, :] = gg
    dx2 = live * m["og"][...] + dv
    m["dx"][...] = dx2
    dx2l = dx2.astype(BF)
    doc = nt(dx2l, w[CO]).astype(BF)
    do, dr = m["do"], m["dr"]
    do[z, y] = doc
    pick = iota((T, D), 0) == (iota((T, D), 1) & (T - 1))

    def as_row(st):
        return jnp.sum(jnp.where(pick, nn_high(st, spread[...]), 0.0), axis=0, keepdims=True)

    prod = doc.astype(F32) * m["oc"][...].astype(F32)
    delta = lax.dot_general(
        prod, spread[...], (((1,), (1,)), ((), ())), preferred_element_type=F32, precision=HIGH
    )
    dr[z, y] = jnp.zeros((8, D), F32)
    dr[z, y, 0:1, :] = as_row(m["pst"][0, z])
    dr[z, y, 1:2, :] = as_row(delta)
    do_base = take(2 * YZ)
    act_start(do_base, [do, dr])
    grad_of(CO, m["oc"][...], dx2l)
    fo_x2 = ff_out_x(fo_c)
    fi_x2 = ff_in_x(fi_c)
    got(yy)
    zy = rs_z_stage(py, ryy, rzy)

    pq, ryq, rzq = po, ryo, rzo
    sent(yh + zh)
    yq_base = rs_y_base()

    def attend_back(t, carry):
        a = t % Z
        b = t // Z
        zi = zs(a)
        yi = ys(b)
        qi = zi * Y + yi

        @pl.when(t > 0)
        def _():
            act_wait(do_base, [do, dr], t)

        @pl.when(t < Z)
        def _():
            act_forward(do_base, [do, dr], a)

        for k in range(NQ):
            qb = stack4(qc[zi, yi, :, quad(k)])
            db = stack4(do[zi, yi, :, quad(k)])
            kt = kv[qi, :, quad(k)]
            vt = kv[qi, :, D + k * WIDE : D + (k + 1) * WIDE]
            pt = jnp.exp(nt(kt, qb) - dr[zi, yi, 0:1, quad(k)])
            ds = (pt * (nt(vt, db) - dr[zi, yi, 1:2, quad(k)])).astype(BF)
            pq[b, zi, :, quad(k)] = fold4(tn(ds, kt)).astype(BF)
            kv[qi, :, quad(k)] = nn(ds, qb).astype(BF)
            kv[qi, :, D + k * WIDE : D + (k + 1) * WIDE] = nn(pt.astype(BF), db).astype(BF)

        @pl.when(t >= Z)
        def _():
            rs_y_send(yq_base, pq, ryq, b, a)

        return carry

    lax.fori_loop(0, YZ, attend_back, 0)
    fi_y2 = ff_in_y(fi_x2)
    push(CO)
    for a in range(Z):
        for b in range(1, Y):
            rs_y_wait(yq_base, pq, ryq, b, a)
    zq = rs_z_stage(pq, ryq, rzq)

    for p, off in ((CK, 0), (CV, D)):
        if R % 16 == 0:
            acc[...] = tn(pas[...].reshape(YZ * R, D), kv[:, :, off : off + D].reshape(YZ * R, D))
        else:
            acc[...] = jnp.zeros_like(acc)

            def kv_grad(q, carry):
                acc[...] += tn(pas[q], kv[q, :, off : off + D])
                return carry

            lax.fori_loop(0, YZ, kv_grad, 0)
        grad_out(p)
        push(CO)

    def row_grad(q, carry):
        pas[q] = (nt(kv[q, :, 0:D], w[CK]) + nt(kv[q, :, D : 2 * D], w[CV])).astype(BF)
        pltpu.make_async_copy(pas.at[q], m["pg"].at[q], lsem.at[1 + q]).start()
        return carry

    lax.fori_loop(0, YZ, row_grad, 0)
    fi_z2 = ff_in_z(fi_y2)
    ff_out_end(fo_x2)

    got(zq)
    dqc = rs_total(pq, ryq, rzq).astype(BF)
    dh2 = nt(dqc, w[CQ])
    dv, gg = norm_back(m["x1"][...], gain[1:2, :], dh2)
    sm[1:2, :] = gg
    dx1 = m["dx"][...] + dv
    m["dx"][...] = dx1
    dx1l = dx1.astype(BF)
    grad_of(CQ, m["h2"][...], dqc)
    push_all([CK, CV, CO])
    grad_of(SO, m["os"][...], dx1l)
    push_all([CQ, CK, CV, CO])
    ff_in_end(fi_z2)
    got(zy)
    yt = rs_total(py, ryy, rzy)
    m["bo"][...] = live * (m["x2"][...] + yt)

    m["oc"][...] = nt(dx1l, w[SO]).astype(BF)
    grads = [[], [], []]
    tail = []
    for t in range(NQ):
        db = stack4(m["oc"][:, quad(t)])
        qb = stack4(m["qs"][:, quad(t)])
        pr = m["ps"][t]
        dps = nt(db, m["vs"][:, quad(t)])
        dss = (pr * (dps - jnp.sum(pr * dps, axis=1, keepdims=True))).astype(BF)
        grads[0].append(fold4(nn(dss, m["ks"][:, quad(t)])).astype(BF))
        grads[1].append(tn(dss, qb).astype(BF))
        grads[2].append(tn(pr.astype(BF), db).astype(BF))
        back = (iota((T, 128), 1) == T - 1 - iota((T, 128), 0)).astype(F32).astype(BF)
        turned = nn(dss, back)
        for h in range(QUAD):
            part = pltpu.roll(turned[h * T : (h + 1) * T], 0, 1, stride=1, stride_axis=0)
            tail.append(jnp.sum(part, axis=0, keepdims=True))
    dqs, dks, dvs = (jnp.concatenate(g, axis=1) for g in grads)
    h1 = m["h1"][...]
    push_all([SO, CQ, CK, CV, CO])
    grad_of(SV, h1, dvs)
    push_all([SO, CQ, CK, CV, CO])
    grad_of(SQ, h1, dqs)
    push_all([SV, SO, CQ, CK, CV, CO])
    grad_of(SK, h1, dks)
    push_all([SQ, SV, SO, CQ, CK, CV, CO])
    dh1 = nt(dqs, w[SQ]) + nt(dks, w[SK]) + nt(dvs, w[SV])
    dv, gg = norm_back(tok[...], gain[0:1, :], dh1)
    sm[0:1, :] = gg
    m["tg"][...] = m["dx"][...] + dv
    flat = HEADS * BUCKETS
    diag = jnp.concatenate(tail + [jnp.zeros((16 - HEADS, 128), F32)], axis=0)
    mi, bi = iota((128, 128), 0), iota((128, 128), 1)
    hot = ((mi >= T - 1) & (bucket_of(mi - (T - 1)) == bi) & (bi < BUCKETS)).astype(F32)
    table = nn_high(diag, hot)
    bb, nb = iota((128, flat), 0), iota((128, flat), 1)
    wide = nn_high(table, ((nb & (BUCKETS - 1)) == bb).astype(F32))
    h0, n0 = iota((16, flat), 0), iota((16, flat), 1)
    own = (n0 >= h0 * BUCKETS) & (n0 < h0 * BUCKETS + BUCKETS)
    sm[3:4, 0:flat] = jnp.sum(jnp.where(own, wide, 0.0), axis=0, keepdims=True)

    rsm = m["rsm"]
    slot = [0]

    def small_sum(devs):
        first = slot[0]
        cps = []
        for to in devs:
            cps.append(send(sm, rsm.at[slot[0]], to))
            slot[0] += 1
        got(cps)
        sent(cps)
        for k in range(first, slot[0]):
            sm[...] += rsm[k]

    small_sum([dev(c_=oth)])
    push_all([SK, SQ, SV, SO, CQ, CK, CV, CO])
    small_sum([dev(x_=xs(b)) for b in range(1, X)])
    push_all([SK, SQ, SV, SO, CQ, CK, CV, CO])
    small_sum([dev(y_=ys(b)) for b in range(1, Y)])
    push_all([SK, SQ, SV, SO, CQ, CK, CV, CO])
    small_sum([dev(z_=zs(a)) for a in range(1, Z)])
    while any(k < len(stages) for k, _ in moving.values()):
        push_all([SK, SQ, SV, SO, CQ, CK, CV, CO])
    me = dp * YZ + fs
    nd, ld = iota((D, 128), 0), iota((D, 128), 1)
    mine = nn_high(sm[...], ((nd == me * r + ld) & (ld < r)).astype(F32))
    mine_b = nn_high(sm[...], ((nd == me * rbs + ld) & (ld < rbs)).astype(F32))
    m["g_ls"][...] = mine[0:1, 0:r]
    m["g_lc"][...] = mine[1:2, 0:r]
    m["g_lf"][...] = mine[2:3, 0:r]
    m["g_rb"][...] = mine_b[3:4, 0:rbs]

    act_done(do_base, [do, dr])
    rs_y_done(yq_base, pq, ryq)
    drain()

    def pg_wait(q, carry):
        pltpu.make_async_copy(pas.at[q], m["pg"].at[q], lsem.at[1 + q]).wait()
        return carry

    lax.fori_loop(0, YZ, pg_wait, 0)


def per_device(
    sz,
    targets, passages, tgt_len, out_grad, ln_self, rel_bias, self_q, self_kv, self_out,
    ln_cross, cross_q, cross_kv, cross_out, ln_ff, ff_in, ff_out,
):
    T, D, r, hid, rfi, rff = sz.T, sz.D, sz.r, sz.hid, sz.rfi, sz.rff
    nfs = sz.Y * sz.Z
    ndp = 2 * sz.X
    live = (jnp.arange(T) < tgt_len[0]).astype(F32)
    live = jnp.broadcast_to(live[:, None], (T, 128))

    def line(v):
        return jnp.pad(v, (0, 128 - v.shape[0]))

    small = jnp.stack([line(ln_self), line(ln_cross), line(ln_ff), line(rel_bias)])
    small = jnp.pad(small, ((0, 12), (0, 0)))
    fi_in = ff_in.reshape(r, ndp, nfs, rff).transpose(2, 0, 1, 3).reshape(nfs, r, hid)
    fi_in = jnp.pad(fi_in, ((0, 0), (0, rfi - r), (0, 0)))
    scratch = layout(sz)
    names = tuple(scratch)
    gr = r if sz.inside else D
    vm = pl.BlockSpec(memory_space=pltpu.VMEM)
    hbm = pl.BlockSpec(memory_space=pl.ANY)
    shape = jax.ShapeDtypeStruct
    rbs = rel_bias.shape[0]
    out_shape = (
        shape((T, D), F32), shape((T, D), F32), shape(passages.shape, BF),
        shape((1, r), F32), shape((1, rbs), F32),
        shape((gr, D), F32), shape((gr, 2 * D), F32), shape((gr, D), F32),
        shape((1, r), F32), shape((gr, D), F32), shape((gr, 2 * D), F32), shape((gr, D), F32),
        shape((1, r), F32), shape((nfs, r, hid), F32), shape((rff, D), F32),
    )
    weight_outs = ("g_sq", "g_skv", "g_so", "g_cq", "g_ckv", "g_co")
    apart = ("pg",) if sz.inside else ("pg",) + weight_outs
    outs = pl.pallas_call(
        functools.partial(block_kernel, sz, names),
        out_shape=out_shape,
        in_specs=[hbm if n == "pas_in" else vm for n in INPUTS],
        out_specs=tuple(hbm if n in apart else vm for n in OUTPUTS),
        scratch_shapes=tuple(scratch.values()),
        compiler_params=pltpu.CompilerParams(
            collective_id=0, has_side_effects=True, vmem_limit_bytes=63 * 2**20
        ),
        cost_estimate=pl.CostEstimate(
            flops=20 * 10**9, bytes_accessed=2 * 10**7, transcendentals=4 * 10**6
        ),
    )(
        targets[0], passages, live, out_grad[0], small, self_q, self_kv, self_out,
        cross_q, cross_kv, cross_out, fi_in, ff_out,
    )
    (bo, tg, pg, g_ls, g_rb, g_sq, g_skv, g_so, g_lc, g_cq, g_ckv, g_co, g_lf, g_fi, g_fo) = outs
    if not sz.inside:
        g_sq, g_skv, g_so, g_cq, g_ckv, g_co = (
            lax.psum_scatter(g, ("dp", "fsdp"), scatter_dimension=0, tiled=True)
            for g in (g_sq, g_skv, g_so, g_cq, g_ckv, g_co)
        )
    g_fi = g_fi.reshape(nfs, r, ndp, rff).transpose(1, 2, 0, 3).reshape(r, ndp * nfs * rff)
    return (
        bo[None], tg[None], pg, g_ls[0], g_rb[0], g_sq, g_skv, g_so,
        g_lc[0], g_cq, g_ckv, g_co, g_lf[0], g_fi, g_fo,
    )


def solution(mesh):
    both = ("dp", "fsdp")
    rows3, rows2, rows1 = P(both, None, None), P(both, None), P(both)
    placed = (
        rows3, P("dp", "fsdp", None), rows1, rows3, rows1, rows1, rows2, rows2, rows2,
        rows1, rows2, rows2, rows2, rows1, rows2, rows2,
    )
    outs = (
        rows3, rows3, P("dp", "fsdp", None), rows1, rows1, rows2, rows2, rows2,
        rows1, rows2, rows2, rows2, rows1, rows2, rows2,
    )

    def run(*args):
        targets, passages, self_q, ff_out = args[0], args[1], args[6], args[15]
        sz = Sizes(
            mesh.shape,
            targets.shape[2], passages.shape[1], targets.shape[1],
            self_q.shape[0], ff_out.shape[0],
            ff_out.shape[0] * mesh.shape["dp"],
        )
        return per_device(sz, *args)

    return jax.shard_map(run, mesh=mesh, in_specs=placed, out_specs=outs, check_vma=False)
```

time: 1520 us -> 274 us (0.18)
  waiting for transfers between devices: 1070 us -> 0 us
  Pallas kernels: 0 us -> 252 us
  blocking collectives: 169 us -> 0 us
  matrix products: 104 us -> 0 us
  local copies, waits for them, and re-layouts: 98.5 us -> 19.9 us
  other arithmetic: 29.9 us -> 0.61 us
  starting transfers between devices: 23.7 us -> 0 us
    reduce_scatter x7 -> x0, waiting for transfers between devices: 598 us -> none  [the longest x1 142 us: per_device(): lax.psum_scatter(gw_ffout, ('dp', 'fsdp'), scatter_dimension=0, tiled=True)]
    all_gather x8 -> x0, waiting for transfers between devices: 358 us -> none  [the longest x1 63.7 us: per_device(): lax.all_gather(ff_in, ('dp', 'fsdp'), axis=0, tiled=True)]
    pallas_call x0 -> x1, Pallas kernels: none -> 252 us  [per_device(): pl.pallas_call(functools.partial(block_kernel, sz, names), out_shape=out_...]
    unnamed x2 -> x0, blocking collectives: 169 us -> none
    unnamed x17 -> x0, waiting for transfers between devices: 118 us -> none
    dot_general x46 -> x0, matrix products: 104 us -> none  [the longest x8 30.5 us: left_contract(): lax.dot_general(left, right, (((0,), (0,)), ((), ())), preferred_element_...]
    unnamed x144 -> x38, local copies, waits for them, and re-layouts: 40.3 us -> 11.5 us
    broadcast_in_dim x1, local copies, waits for them, and re-layouts: 22.3 us -> 0.69 us  [per_device(): live = jnp.broadcast_to(live[:, None], (T, 128))]
  transfers between devices with their start and end apart: 18 -> 0, of which waited for: 13 -> 0; matrix products, arithmetic and copies ran while one was open for 12% -> 0% of each run, Pallas kernels for 0% -> 0%
where the time goes in v1:
time: 274 us
  Pallas kernels  252 us (92%)
  local copies, waits for them, and re-layouts  19.9 us (7%)
    pallas_call x1, Pallas kernels, per_device(): pl.pallas_call(functools.partial(block_kernel, sz, names), out_shape=out_...  252 us
    unnamed x38, local copies, waits for them, and re-layouts  11.5 us

profile of v1, /device:TPU:0, one launch (start us, length us, event | category | flops | bytes accessed | tf_op | source)
XLA Modules:
  0.0 273.8 jit_solution(11569116337978263438)
XLA Ops:
  1.3 0.7 pad_bitcast_fusion.2
  2.0 0.7 pad_bitcast_fusion
  2.7 0.6 fusion.6.refs_4_
  3.3 0.7 broadcast_in_dim.12.refs_2_
  4.0 1.1 reshape.47
  5.3 0.7 pad.27.refs_11_
  6.0 251.9 %shard_map.271 = (f32[64,768]{1,0:T(8,128)}, f32[64,768]{1,0:T(8,128)}, bf16[8,240,768]{2,1,0:T(8,128)(2,1)}, f32[1,24]{1,0:T(1,128)}, f32[1,12]{1,0:T(1,128)}, ...) custom-call(f32[64,768]{1,0:T(8,128)} %bitcast.28, ...), custom_call_target="tpu_custom_call" | custom-call | flops 20000000000 | bytes 20000000 | tf_op jit(solution)/shard_map/pallas_call | solution.py:1213
  257.9 1.4 reshape.49
  259.3 1.0 copy.32
  260.3 1.9 reshape.50
  262.2 1.6 copy.50
  263.8 1.6 copy.51
  265.5 1.6 copy.52
  267.1 0.5 copy.53
  267.6 0.5 copy.54
  268.2 0.6 copy.55
  268.8 0.7 copy.56
  269.5 0.6 copy.57
  270.1 0.5 copy.58
  270.6 0.6 copy.59
  271.2 0.7 copy.60
  271.9 0.6 copy.61
  272.5 0.5 copy.62
  273.1 0.7 copy.63
  (27 shorter events, 0.3 us)
Async XLA Ops:
  257.9 7.5 %copy-start = (bf16[8,240,768]{2,1,0:T(8,128)(2,1)S(1)}, bf16[8,240,768]{2,1,0:T(8,128)(2,1)}, u32[]{:S(2)}) copy-start(bf16[8,240,768]{2,1,0:T(8,128)(2,1)} %get-tuple-element.66) | copy-start | bytes 8847364
  265.4 1.7 copy-start.11
  265.4 2.2 copy-start.10
  265.4 2.7 copy-start.7
  265.4 3.4 %copy-start.3 = (f32[24,1536]{1,0:T(8,128)S(1)}, f32[24,1536]{1,0:T(8,128)}, u32[]{:S(2)}) copy-start(f32[24,1536]{1,0:T(8,128)} %get-tuple-element.70) | copy-start | bytes 442372
  265.5 4.0 %copy-start.6 = (f32[24,768]{1,0:T(8,128)S(1)}, f32[24,768]{1,0:T(8,128)}, u32[]{:S(2)}) copy-start(f32[24,768]{1,0:T(8,128)} %get-tuple-element.71) | copy-start | bytes 221188
  265.5 4.6 %copy-start.9 = (f32[1,24]{1,0:T(1,128)S(1)}, f32[1,24]{1,0:T(1,128)}, u32[]{:S(2)}) copy-start(f32[1,24]{1,0:T(1,128)} %get-tuple-element.38) | copy-start | bytes 292
  265.5 5.1 %copy-start.5 = (f32[24,768]{1,0:T(8,128)S(1)}, f32[24,768]{1,0:T(8,128)}, u32[]{:S(2)}) copy-start(f32[24,768]{1,0:T(8,128)} %get-tuple-element.73) | copy-start | bytes 221188
  265.5 5.8 %copy-start.2 = (f32[24,1536]{1,0:T(8,128)S(1)}, f32[24,1536]{1,0:T(8,128)}, u32[]{:S(2)}) copy-start(f32[24,1536]{1,0:T(8,128)} %get-tuple-element.74) | copy-start | bytes 442372
  265.5 6.4 %copy-start.4 = (f32[24,768]{1,0:T(8,128)S(1)}, f32[24,768]{1,0:T(8,128)}, u32[]{:S(2)}) copy-start(f32[24,768]{1,0:T(8,128)} %get-tuple-element.75) | copy-start | bytes 221188
  265.5 7.0 %copy-start.8 = (f32[1,24]{1,0:T(1,128)S(1)}, f32[1,24]{1,0:T(1,128)}, u32[]{:S(2)}) copy-start(f32[1,24]{1,0:T(1,128)} %get-tuple-element.42) | copy-start | bytes 292
  265.5 7.5 %copy-start.1 = (f32[96,768]{1,0:T(8,128)S(1)}, f32[96,768]{1,0:T(8,128)}, u32[]{:S(2)}) copy-start(f32[96,768]{1,0:T(8,128)} %get-tuple-element.78) | copy-start | bytes 884740

commit v2 on v1

v2 whole, which is shorter than its diff:
```python
import functools
import math

import jax
import jax.numpy as jnp
from jax import lax
from jax.experimental import pallas as pl
from jax.experimental.pallas import tpu as pltpu
from jax.sharding import PartitionSpec as P

HEADS = 12
DK = 64
BUCKETS = 32
QUAD = 4
WIDE = QUAD * DK
EPS = 1e-06
NEG = -1e30
HIGH = lax.Precision.HIGHEST
BF = jnp.bfloat16
F32 = jnp.float32
PIECES = 10
SQ, SK, SV, SO, CQ, CK, CV, CO, FI, FO = range(PIECES)
X_LAST = (SQ, SV, CQ, CV, CO, FI, FO)
Y_LAST = (SK, SO, CK)
Y_GATHERED_LAST = (SK, CK)
ZDIM = 4


def up16(n):
    return (n + 15) // 16 * 16


def bucket_limits():
    limits = []
    for target_bucket in range(1, 16):
        distance = 16
        while int(math.log(distance / 16.0) / math.log(8.0) * 16.0) < target_bucket:
            distance = distance + 1
        limits.append(distance)
    return limits


def bucket_of(distance):
    larger = jnp.full_like(distance, 16)
    for limit_value in bucket_limits():
        larger = larger + (distance >= limit_value).astype(jnp.int32)
    return jnp.where(distance < 16, distance, jnp.minimum(larger, 31))


def iota(shape, axis):
    return lax.broadcasted_iota(jnp.int32, shape, axis)


def nn(a, b):
    return lax.dot_general(a, b, (((1,), (0,)), ((), ())), preferred_element_type=F32)


def nt(a, b):
    return lax.dot_general(a, b, (((1,), (1,)), ((), ())), preferred_element_type=F32)


def tn(a, b):
    return lax.dot_general(a, b, (((0,), (0,)), ((), ())), preferred_element_type=F32)


def nn_high(a, b):
    return lax.dot_general(
        a, b, (((1,), (0,)), ((), ())), preferred_element_type=F32, precision=HIGH
    )


def normed(v, gain):
    return v * lax.rsqrt(jnp.mean(v * v, axis=-1, keepdims=True) + EPS) * gain


def norm_back(v, gain, dy):
    s = lax.rsqrt(jnp.mean(v * v, axis=-1, keepdims=True) + EPS)
    dyg = dy * gain
    gain_grad = jnp.sum(dy * v * s, axis=0, keepdims=True)
    dv = s * dyg - v * (s * s * s) * jnp.mean(dyg * v, axis=-1, keepdims=True)
    return dv, gain_grad


def gelu_pair(u):
    cst = 0.7978845608028654
    cubic = 0.044715
    th = jnp.tanh(cst * (u + cubic * u * u * u))
    half = 0.5 * (1.0 + th)
    slope = half + 0.5 * u * (1.0 - th * th) * cst * (1.0 + 3.0 * cubic * u * u)
    return u * half, slope


class Sizes:
    def __init__(self, mesh_shape, width, rows, targets, shard, ff_shard, hidden):
        self.Z = ZDIM
        self.X = mesh_shape["dp"] // 2
        self.Y = mesh_shape["fsdp"] // self.Z
        self.D = width
        self.R = rows
        self.T = targets
        self.r = shard
        self.rb = up16(2 * shard)
        self.nh = width // 2
        self.inside = shard % 8 == 0
        self.rff = ff_shard
        self.hid = hidden
        assert ff_shard == self.Z * shard and hidden == width


def sems(sz):
    return 264 if sz.inside else 900


def layout(sz):
    X, Y, Z, D, T, R = sz.X, sz.Y, sz.Z, sz.D, sz.T, sz.R
    rb, nh, hid = sz.rb, sz.nh, sz.hid
    na, nb = len(X_LAST), len(Y_LAST)
    NQ = HEADS // QUAD
    V = pltpu.VMEM
    sums = dict(
        rc=V((PIECES, X, Y, Z, rb, nh), BF),
        r1a=V((na, X - 1, Y, Z, rb, nh), BF),
        r1b=V((nb, Y - 1, X, Z, rb, nh), BF),
        r2a=V((na, Y - 1, Z, rb, nh), BF),
        r2b=V((nb, X - 1, Z, rb, nh), BF),
        rz=V((PIECES, Z - 1, rb, nh), BF),
    )
    return dict(
        **(sums if sz.inside else {}),
        gw=V((PIECES, 2, X, Y, Z, rb, nh), BF),
        w=V((PIECES, D, D), BF),
        fip=V((Z, rb, nh), BF),
        acc=V((D, D), F32),
        lift=V((max(Y * Z * sz.r, sz.rff) if sz.r % 8 else 8, D), F32),
        even=V((sz.r, D), F32),
        gfi=V((Z, sz.r, D), F32),
        cell=V((rb, nh), F32),
        smb=V((2, X, Y, Z, 16, 128), BF),
        hot_gain=V((128, D), BF),
        hot_bias=V((128, HEADS * BUCKETS), BF),
        gain=V((16, D), F32),
        bias=V((NQ, WIDE, T), F32),
        spread=V((16, D), F32),
        mask=V((WIDE, WIDE), BF),
        pas=V((Y * Z, R, D), BF),
        kv=V((Y * Z, R, 2 * D), BF),
        h1=V((T, D), BF),
        qs=V((T, D), BF),
        ks=V((T, D), BF),
        vs=V((T, D), BF),
        os=V((T, D), BF),
        ps=V((NQ, WIDE, T), F32),
        x1=V((T, D), F32),
        h2=V((T, D), BF),
        x2=V((T, D), F32),
        oc=V((T, D), BF),
        dx=V((T, D), F32),
        lse=V((16, T), F32),
        qc=V((Z, Y, T, D), BF),
        h3=V((Z, T, D), BF),
        g3=V((Z, T, D), BF),
        do=V((Z, Y, T, D), BF),
        dr=V((Z, Y, 16, 128), F32),
        po=V((Y, Z, T, D), BF),
        pst=V((Y, Z, 16, T), F32),
        ryo=V((Y - 1, Z, T, D), BF),
        ryst=V((Y - 1, Z, 16, T), F32),
        rzo=V((Z - 1, T, D), BF),
        rzst=V((Z - 1, 16, T), F32),
        py=V((Z, T, D), BF),
        rzy=V((Z - 1, T, D), BF),
        da=V((Z * T, hid), F32),
        gl=V((Z * T, hid), BF),
        du=V((Z * T, hid), BF),
        sm=V((8, D), F32),
        rsm=V((1 + (X - 1) + (Y - 1) + (Z - 1), 8, D), F32),
        ssem=pltpu.SemaphoreType.DMA((sems(sz),)),
        rsem=pltpu.SemaphoreType.DMA((sems(sz),)),
        lsem=pltpu.SemaphoreType.DMA((1 + Y * Z,)),
    )


INPUTS = (
    "tok", "pas_in", "len", "og", "ls", "rel", "sq", "skv", "so",
    "lc", "cq", "ckv", "co", "lf", "fi_in", "fo_in",
)
OUTPUTS = (
    "bo", "tg", "pg", "g_ls", "g_rb", "g_sq", "g_skv", "g_so",
    "g_lc", "g_cq", "g_ckv", "g_co", "g_lf", "g_fi", "g_fo",
)


def block_kernel(sz, names, *refs):
    n_in, n_out = len(INPUTS), len(OUTPUTS)
    m = dict(zip(INPUTS, refs[:n_in]))
    m.update(zip(OUTPUTS, refs[n_in : n_in + n_out]))
    m.update(zip(names, refs[n_in + n_out :]))
    X, Y, Z, D, T, R = sz.X, sz.Y, sz.Z, sz.D, sz.T, sz.R
    r, rb, nh, hid = sz.r, sz.rb, sz.nh, sz.hid
    NQ = HEADS // QUAD
    YZ = Y * Z
    dp = lax.axis_index("dp")
    fs = lax.axis_index("fsdp")
    x, c = dp // 2, dp % 2
    z, y = fs // Y, fs % Y
    oth = 1 - c

    def xs(b):
        return (x + b) % X

    def ys(b):
        return (y + b) % Y

    def zs(b):
        return (z + b) % Z

    def dev(x_=None, c_=None, y_=None, z_=None):
        x_ = x if x_ is None else x_
        c_ = c if c_ is None else c_
        y_ = y if y_ is None else y_
        z_ = z if z_ is None else z_
        return (x_ * 2 + c_, z_ * Y + y_)

    ssem, rsem, lsem = m["ssem"], m["rsem"], m["lsem"]
    n_sems = sems(sz)
    used = [0]
    pending = []

    def take(n=1):
        at = used[0]
        used[0] += n
        assert used[0] <= n_sems
        return at

    def copy_at(i, src, dst, to):
        return pltpu.make_async_remote_copy(
            src_ref=src, dst_ref=dst, send_sem=ssem.at[i], recv_sem=rsem.at[i],
            device_id=to, device_id_type=pl.DeviceIdType.MESH,
        )

    def send(src, dst, to):
        cp = copy_at(take(), src, dst, to)
        cp.start()
        pending.append(cp)
        return cp

    def got(cps):
        for cp in cps:
            cp.wait_recv()

    def sent(cps):
        for cp in cps:
            cp.wait_send()
        pending[:] = [cp for cp in pending if all(cp is not done for done in cps)]

    def drain():
        sent(list(pending))

    partners = [dev(c_=oth)]
    partners += [dev(x_=xs(b)) for b in range(1, X)]
    partners += [dev(y_=ys(b)) for b in range(1, Y)]
    partners += [dev(z_=zs(b)) for b in range(1, Z)]
    bar = pltpu.get_barrier_semaphore()
    for p in partners:
        pl.semaphore_signal(bar, inc=1, device_id=p, device_id_type=pl.DeviceIdType.MESH)
    load_pas = pltpu.make_async_copy(m["pas_in"], m["pas"], lsem.at[0])
    load_pas.start()
    pl.semaphore_wait(bar, len(partners))

    mask = m["mask"]
    mask[...] = (iota((WIDE, WIDE), 0) // DK == iota((WIDE, WIDE), 1) // DK).astype(F32).astype(BF)

    def stack4(v):
        return jnp.concatenate([v, v, v, v], axis=0) * mask[...]

    def fold4(u):
        lane = iota((T, WIDE), 1)
        out = u[0:T]
        for h in range(1, QUAD):
            out = jnp.where(lane >= h * DK, u[h * T : (h + 1) * T], out)
        return out

    def quad(t):
        return slice(t * WIDE, (t + 1) * WIDE)

    cell, lift = m["cell"], m["lift"]

    def put_halves(dst, left, right, rows, total):
        if rows % 8 == 0 and 2 * rows == total:
            dst[...] = jnp.concatenate([left, right], axis=0).astype(BF)
        else:
            cols = left.shape[1]
            cell[0:total, 0:cols] = jnp.zeros((total, cols), F32)
            cell[0:rows, 0:cols] = left
            cell[rows : 2 * rows, 0:cols] = right
            dst[...] = cell[0:total, 0:cols].astype(BF)

    def get_halves(v, rows):
        if rows % 8 == 0:
            return v[0:rows], v[rows : 2 * rows]
        cell[0 : v.shape[0], 0 : v.shape[1]] = v
        return cell[0:rows, 0 : v.shape[1]], cell[rows : 2 * rows, 0 : v.shape[1]]

    gw, w, smb = m["gw"], m["w"], m["smb"]

    def line_to(buf, over_y, blocks):
        out = []
        for k in blocks:
            block = buf.at[c, x, y, k]
            if over_y:
                out += [send(block, block, dev(y_=ys(b))) for b in range(1, Y)]
            else:
                out += [send(block, block, dev(x_=xs(b))) for b in range(1, X)]
        return out

    class Gather:
        def __init__(self, buf, y_first, feed="gather"):
            self.buf, self.y_first, self.feed = buf, y_first, feed
            own = buf.at[c, x, y, z]
            self.z = []
            for a in range(1, Z):
                if feed == "gather":
                    self.z.append(send(own, own, dev(z_=zs(a))))
                elif feed == "exchange":
                    self.z.append(send(m["fip"].at[zs(a)], own, dev(z_=zs(a))))

        def own_out(self):
            blocks = range(Z) if self.feed == "local" else [z]
            self.second = line_to(self.buf, self.y_first, blocks)
            self.third = line_to(self.buf, not self.y_first, blocks)

        def line_out(self):
            got(self.z)
            if self.feed != "local":
                blocks = [zs(Z - a) for a in range(1, Z)]
                self.second += line_to(self.buf, self.y_first, blocks)
                self.third += line_to(self.buf, not self.y_first, blocks)

        def plane_out(self):
            got(self.second)
            buf = self.buf
            if self.y_first:
                for b in range(1, Y):
                    line = buf.at[c, x, ys(b)]
                    self.third += [send(line, line, dev(x_=xs(d))) for d in range(1, X)]
            else:
                for b in range(1, X):
                    line = buf.at[c, xs(b), y]
                    self.third += [send(line, line, dev(y_=ys(d))) for d in range(1, Y)]

        def core_out(self):
            got(self.third)
            self.core = [send(self.buf.at[c], self.buf.at[c], dev(c_=oth))]

        def end(self):
            got(self.core)

    own_small = [jnp.zeros((16, 128), F32)]
    for at, key in enumerate(("ls", "lc", "lf", "rel")):
        v = m[key][...].astype(F32)
        v = jnp.concatenate([v, jnp.zeros((1, 128 - v.shape[1]), F32)], axis=1)
        own_small[0] = jnp.where(iota((16, 128), 0) == at, v, own_small[0])
    smb[c, x, y, z] = own_small[0].astype(BF)
    moves = {}

    def begin(p, feed="gather"):
        moves[p] = Gather(gw.at[p], p not in Y_GATHERED_LAST, feed)

    moves["small"] = Gather(smb, True)
    moves["small"].own_out()
    sources = (
        (m["sq"], 0), (m["skv"], 0), (m["skv"], D), (m["so"], 0),
        (m["cq"], 0), (m["ckv"], 0), (m["ckv"], D), (m["co"], 0),
    )

    def pack(p):
        ref, off = sources[p]
        v = ref[:, off : off + D].astype(F32)
        put_halves(gw.at[p, c, x, y, z], v[:, 0:nh], v[:, nh:D], r, rb)
        begin(p)
        moves[p].own_out()

    for p in (SQ, SK, SV, SO, CQ, CK, CV):
        pack(p)

    g3 = m["g3"]
    live = (iota((T, 1), 0) < m["len"][0]).astype(F32)
    g3[z] = (live * m["og"][...]).astype(BF)

    def line_start(base, buf):
        for a in range(1, Z):
            copy_at(base + a, buf.at[z], buf.at[z], dev(z_=zs(a))).start()

    def line_wait(base, buf):
        for a in range(1, Z):
            copy_at(base + a, buf.at[z], buf.at[z], dev(z_=zs(a))).wait_recv()

    def line_done(base, buf):
        for a in range(1, Z):
            copy_at(base + a, buf.at[z], buf.at[z], dev(z_=zs(a))).wait_send()

    def act_start(base, bufs):
        for n, buf in enumerate(bufs):
            for a in range(1, Z):
                copy_at(base + n * YZ + a, buf.at[z, y], buf.at[z, y], dev(z_=zs(a))).start()

    def act_forward(base, bufs, a):
        zi = zs(a)
        for n, buf in enumerate(bufs):
            for b in range(1, Y):
                copy_at(
                    base + n * YZ + b * Z + (Z - a) % Z, buf.at[zi, y], buf.at[zi, y], dev(y_=ys(b))
                ).start()

    def act_wait(base, bufs, t):
        at = base + (Y - t // Z) % Y * Z + (Z - t % Z) % Z
        for n, buf in enumerate(bufs):
            copy_at(at + n * YZ, buf.at[z, y], buf.at[z, y], dev(z_=zs(1))).wait_recv()

    def act_done(base, bufs):
        for n, buf in enumerate(bufs):
            for t in range(1, YZ):
                copy_at(base + n * YZ + t, buf.at[z, y], buf.at[z, y], dev(z_=zs(1))).wait_send()

    fip = m["fip"]
    ndp = 2 * X
    per = D // ndp

    def pack_ff():
        even = m["even"]
        for k in range(Z):
            for i in range(ndp):
                at = (i * Z + k) * per
                even[:, i * per : (i + 1) * per] = m["fi_in"][:, at : at + per].astype(F32)
            put_halves(fip.at[k], even[:, 0:nh], even[:, nh:D], r, rb)
        vo = m["fo_in"][...].astype(F32)
        if r % 8:
            lift[0 : Z * r, :] = vo
        for k in range(Z):
            part = lift[k * r : k * r + r, :] if r % 8 else vo[k * r : k * r + r]
            put_halves(gw.at[FO, c, x, y, k], part[:, 0:nh], part[:, nh:D], r, rb)
        gw[FI, c, x, y, z] = fip[z]

    g3_base = take(Z)
    line_start(g3_base, g3)

    spread = m["spread"]
    lane = iota((16, D), 1)
    row = iota((16, D), 0)
    spread[...] = ((lane >= row * DK) & (lane < row * DK + DK)).astype(F32)
    tlane = iota((T, 128), 1)
    rbs = HEADS * BUCKETS // (2 * X * YZ)

    def repeat_of(width, step):
        l0, n0 = iota((128, width), 0), iota((128, width), 1)

        def body(k, tot):
            return tot + ((n0 - l0 == k * step) & (l0 < step)).astype(F32)

        return lax.fori_loop(0, width // step, body, jnp.zeros((128, width), F32)).astype(BF)

    m["hot_gain"][...] = repeat_of(D, r)
    m["hot_bias"][...] = repeat_of(HEADS * BUCKETS, rbs)

    def unpack(p):
        group = 2 * Y * r

        if p == FO:
            group = YZ * r
            parts = [(yy, zz) for yy in range(Y) for zz in range(Z)]
        else:
            parts = [(yy, zz) for zz in range(2) for yy in range(Y)]
        per = YZ // len(parts)

        def body(g, carry):
            x_ = g // (2 * per)
            c_ = (g // per) % 2
            zp = 0 if per == 1 else g % per
            lefts, rights = [], []
            at = 0
            for yy, zz in parts:
                lo, hi = get_halves(gw[p, c_, x_, yy, 2 * zp + zz].astype(F32), r)
                if r % 8 == 0:
                    lefts.append(lo)
                    rights.append(hi)
                else:
                    lift[at : at + r, 0:nh] = lo
                    lift[at : at + r, nh:D] = hi
                at += r
            rows = pl.ds(pl.multiple_of(g * group, 16), group)
            if r % 8 == 0:
                w[p, rows, 0:nh] = jnp.concatenate(lefts, axis=0).astype(BF)
                w[p, rows, nh:D] = jnp.concatenate(rights, axis=0).astype(BF)
            else:
                w[p, rows, :] = lift[0:group, :].astype(BF)
            return carry

        lax.fori_loop(0, X * 2 * per, body, 0)

    gain = m["gain"]
    bias = m["bias"]
    def read_small():
        flat = HEADS * BUCKETS
        every = smb[...].reshape(2 * X * YZ * 16, 128)
        wide_g, wide_b = nn(every, m["hot_gain"][...]), nn(every, m["hot_bias"][...])
        ng, nb = iota((16, D), 1), iota((16, flat), 1)
        gains, tot = jnp.zeros((16, D), F32), jnp.zeros((16, flat), F32)
        at = 0
        for c_ in range(2):
            for x_ in range(X):
                for y_ in range(Y):
                    for z_ in range(Z):
                        k = (x_ * 2 + c_) * YZ + z_ * Y + y_
                        mine = (ng >= k * r) & (ng < k * r + r)
                        gains = jnp.where(mine, wide_g[at : at + 16], gains)
                        mine = (nb >= k * rbs) & (nb < k * rbs + rbs)
                        tot = jnp.where(mine, wide_b[at : at + 16], tot)
                        at += 16
        gain[...] = gains
        per = jnp.broadcast_to(tot[3:4, :], (16, flat))
        h0, n0 = iota((16, flat), 0), iota((16, flat), 1)
        per = jnp.where((n0 >= h0 * BUCKETS) & (n0 < h0 * BUCKETS + BUCKETS), per, 0.0)
        nb, mb = iota((flat, 128), 0), iota((flat, 128), 1)
        dist = jnp.where(mb == 0, 0, 128 - mb)
        hot = ((nb & (BUCKETS - 1)) == bucket_of(dist)).astype(F32).astype(BF)
        table = nn(per.astype(BF), hot)
        for h in range(HEADS):
            wide = jnp.broadcast_to(table[h : h + 1, :], (T, 128))
            rolled = pltpu.roll(wide, 0, 1, stride=1, stride_axis=0)
            bias[h // QUAD, (h % QUAD) * T : (h % QUAD + 1) * T, :] = rolled[:, 0:T]

    tok = m["tok"]

    def self_forward():
        m["h1"][...] = normed(tok[...], gain[0:1, :]).astype(BF)
        h1 = m["h1"][...]
        m["qs"][...] = nn(h1, w[SQ]).astype(BF)
        m["ks"][...] = nn(h1, w[SK]).astype(BF)
        m["vs"][...] = nn(h1, w[SV]).astype(BF)
        allowed = iota((WIDE, T), 1) <= (iota((WIDE, T), 0) & (T - 1))
        for t in range(NQ):
            s = nt(stack4(m["qs"][:, quad(t)]), m["ks"][:, quad(t)]) + bias[t]
            s = jnp.where(allowed, s, NEG)
            e = jnp.exp(s - jnp.max(s, axis=1, keepdims=True))
            pr = e / jnp.sum(e, axis=1, keepdims=True)
            m["ps"][t] = pr
            m["os"][:, quad(t)] = fold4(nn(pr.astype(BF), m["vs"][:, quad(t)])).astype(BF)

    qc = m["qc"]
    qc_base = take(YZ)

    def self_out():
        x1 = tok[...] + nn(m["os"][...], w[SO])
        m["x1"][...] = x1
        m["h2"][...] = normed(x1, gain[1:2, :]).astype(BF)

    def cross_query():
        qc[z, y] = nn(m["h2"][...], w[CQ]).astype(BF)
        act_start(qc_base, [qc])

    kv, pas = m["kv"], m["pas"]

    chunk = 4 if R % 16 == 0 else 1

    def project(p, off):
        def body(k, carry):
            if chunk == 1:
                kv[k, :, off : off + D] = nn(pas[k], w[p]).astype(BF)
            else:
                rows = pl.ds(k * chunk, chunk)
                v = nn(pas[rows].reshape(chunk * R, D), w[p])
                kv[rows, :, off : off + D] = v.astype(BF).reshape(chunk, R, D)
            return carry

        lax.fori_loop(0, YZ // chunk, body, 0)

    def query_forward():
        for a in range(Z):
            if a:
                act_wait(qc_base, [qc], a)
            act_forward(qc_base, [qc], a)

    def after(p):
        unpack(p)
        if p == SQ:
            moves["small"].end()
            read_small()
        elif p == SV:
            self_forward()
        elif p == SO:
            self_out()
        elif p == CQ:
            cross_query()
        elif p == CK:
            load_pas.wait()
            project(CK, 0)
        elif p == CV:
            query_forward()
            project(CV, D)

    order = (SQ, SK, SV, SO, CQ, CK, CV, CO, FI, FO)

    def line_out(k):
        if k == 0:
            moves["small"].line_out()
        moves[order[k]].line_out()

    def plane_out(k):
        if k == 0:
            moves["small"].plane_out()
        moves[order[k]].plane_out()

    def core_out(k):
        if k == 0:
            moves["small"].core_out()
        moves[order[k]].core_out()

    def arrive(k):
        moves[order[k]].end()
        after(order[k])

    for k in range(7):
        line_out(k)
        if k == 1:
            pack_ff()
        if k >= 1:
            plane_out(k - 1)
        if k >= 2:
            core_out(k - 2)
        if k >= 3:
            arrive(k - 3)
    plane_out(6)
    pack(CO)
    begin(FI, "exchange")
    core_out(5)
    arrive(4)
    core_out(6)
    arrive(5)
    line_out(7)
    moves[FI].own_out()
    begin(FO, "local")
    moves[FO].own_out()
    arrive(6)

    po, pst, ryo, ryst, rzo, rzst = (m[k] for k in ("po", "pst", "ryo", "ryst", "rzo", "rzst"))

    def rs_y_base():
        return take((Y - 1) * Z)

    def rs_y_send(base, src, dst, b, a):
        zi = zs(a)
        copy_at(base + (b - 1) * Z + a, src.at[b, zi], dst.at[b - 1, zi], dev(y_=ys(b))).start()

    def rs_y_wait(base, src, dst, b, a):
        copy_at(base + (b - 1) * Z + a, src.at[b, 0], dst.at[b - 1, 0], dev(y_=ys(1))).wait_recv()

    def rs_y_done(base, src, dst):
        for b in range(1, Y):
            for a in range(Z):
                copy_at(
                    base + (b - 1) * Z + a, src.at[b, 0], dst.at[b - 1, 0], dev(y_=ys(1))
                ).wait_send()

    yo_base, yst_base = rs_y_base(), rs_y_base()
    zo_base, zst_base = take(Z), take(Z)

    def attend(a, b):
        zi = zs(a)
        yi = ys(b)
        qi = zi * Y + yi
        st = jnp.zeros((T, 128), F32)
        for k in range(NQ):
            qb = stack4(qc[zi, yi, :, quad(k)])
            s = nt(qb, kv[qi, :, quad(k)])
            top = jnp.max(s, axis=1, keepdims=True)
            e = jnp.exp(s - top)
            tot = jnp.sum(e, axis=1, keepdims=True)
            u = nn(e.astype(BF), kv[qi, :, D + k * WIDE : D + (k + 1) * WIDE])
            po[b, zi, :, quad(k)] = fold4(u * (1.0 / tot)).astype(BF)
            lse = top + jnp.log(tot)
            for h in range(QUAD):
                st = jnp.where(tlane == k * QUAD + h, lse[h * T : (h + 1) * T], st)
        pst[b, zi] = st.T[0:16]

    def expand(st):
        return lax.dot_general(
            st, spread[...], (((0,), (0,)), ((), ())), preferred_element_type=F32, precision=HIGH
        )

    def merge(parts):
        top = parts[0][1]
        for _, st in parts[1:]:
            top = jnp.maximum(top, st)
        ws = [jnp.exp(st - top) for _, st in parts]
        tot = ws[0]
        for v in ws[1:]:
            tot = tot + v
        out = jnp.zeros((T, D), F32)
        for (o, _), v in zip(parts, ws):
            out = out + expand(v / tot) * o.astype(F32)
        return out, top + jnp.log(tot)

    def z_send(base, src, dst, a):
        zi = zs(a)
        copy_at(base + a, src.at[0, zi], dst.at[a - 1], dev(z_=zi)).start()

    def z_each(base, src, dst, wait):
        for a in range(1, Z):
            cp = copy_at(base + a, src.at[0, 0], dst.at[a - 1], dev(z_=zs(a)))
            if wait == "recv":
                cp.wait_recv()
            else:
                cp.wait_send()

    def attend_other(t, carry):
        a = (1 + t % Z) % Z
        b = 1 + t // Z
        act_wait(qc_base, [qc], b * Z + a)
        attend(a, b)
        rs_y_send(yo_base, po, ryo, b, a)
        rs_y_send(yst_base, pst, ryst, b, a)
        return carry

    def attend_own(t, carry):
        a = (1 + t) % Z
        zi = zs(a)
        attend(a, 0)

        @pl.when(t < Z - 1)
        def _():
            for b in range(1, Y):
                rs_y_wait(yo_base, po, ryo, b, a)
                rs_y_wait(yst_base, pst, ryst, b, a)
            o, st = merge(
                [(po[0, zi], pst[0, zi])]
                + [(ryo[b - 1, zi], ryst[b - 1, zi]) for b in range(1, Y)]
            )
            po[0, zi] = o.astype(BF)
            pst[0, zi] = st
            z_send(zo_base, po, rzo, a)
            z_send(zst_base, pst, rzst, a)

        return carry

    lax.fori_loop(0, (Y - 1) * Z, attend_other, 0)
    plane_out(7)
    line_out(8)
    line_out(9)
    lax.fori_loop(0, Z, attend_own, 0)
    core_out(7)
    plane_out(8)
    plane_out(9)
    arrive(7)
    for b in range(1, Y):
        rs_y_wait(yo_base, po, ryo, b, 0)
        rs_y_wait(yst_base, pst, ryst, b, 0)
    z_each(zo_base, po, rzo, "recv")
    z_each(zst_base, pst, rzst, "recv")
    o, lse = merge(
        [(po[0, z], pst[0, z])]
        + [(ryo[b - 1, z], ryst[b - 1, z]) for b in range(1, Y)]
        + [(rzo[a - 1], rzst[a - 1]) for a in range(1, Z)]
    )
    m["oc"][...] = o.astype(BF)
    m["lse"][...] = lse
    x2 = m["x1"][...] + nn(m["oc"][...], w[CO])
    m["x2"][...] = x2
    h3 = m["h3"]
    h3[z] = normed(x2, gain[2:3, :]).astype(BF)
    h3_base = take(Z)
    line_start(h3_base, h3)

    core_out(8)
    core_out(9)
    arrive(8)
    line_wait(g3_base, g3)
    arrive(9)
    gb = g3[...].reshape(Z * T, D)
    m["da"][...] = nt(gb, w[FO])
    act_done(qc_base, [qc])
    rs_y_done(yo_base, po, ryo)
    rs_y_done(yst_base, pst, ryst)
    z_each(zo_base, po, rzo, "send")
    z_each(zst_base, pst, rzst, "send")
    drain()
    py, rzy = m["py"], m["rzy"]
    gl, du = m["gl"], m["du"]
    line_wait(h3_base, h3)
    hb = h3[...].reshape(Z * T, D)
    act, slope = gelu_pair(nn(hb, w[FI]))
    du[...] = (m["da"][...] * slope).astype(BF)
    gl[...] = act.astype(BF)
    po[0] = nt(du[...], w[FI]).astype(BF).reshape(Z, T, D)

    def rs_z(part, rzb):
        return [send(part.at[zs(a)], rzb.at[a - 1], dev(z_=zs(a))) for a in range(1, Z)]

    def rs_total(part, rzb):
        tot = part[z].astype(F32)
        for a in range(1, Z):
            tot = tot + rzb[a - 1].astype(F32)
        return tot

    zh = rs_z(po.at[0], rzo)
    py[...] = nn(gl[...], w[FO]).astype(BF).reshape(Z, T, D)
    line_done(h3_base, h3)
    line_done(g3_base, g3)

    acc = m["acc"]

    def add_to(dst, src):
        dst[...] = (dst[...].astype(F32) + src[...].astype(F32)).astype(BF)

    rc, r1a, r1b, r2a, r2b, rz = (m.get(k) for k in ("rc", "r1a", "r1b", "r2a", "r2b", "rz"))

    def pack_grad(p):
        group = YZ * r
        if not sz.inside:
            name, off = targets[p]
            out = m[name] if p in (FI, FO) else m[name].at[:, off : off + D]
            cp = pltpu.make_async_copy(acc, out, lsem.at[0])
            cp.start()
            cp.wait()
            return None

        def body(k, carry):
            x_ = k // 2
            c_ = k % 2
            for z_ in range(Z):
                for y_ in range(Y):
                    at = (y_ * Z + z_) * r if p == FO else (z_ * Y + y_) * r
                    rows = pl.ds(pl.multiple_of(k * group + at, 8), r)
                    left, right = acc[rows, 0:nh], acc[rows, nh:D]
                    put_halves(gw.at[p, c_, x_, y_, z_], left, right, r, rb)
            return carry

        lax.fori_loop(0, 2 * X, body, 0)
        return [send(gw.at[p, oth], rc.at[p], dev(c_=oth))]

    def rs_first(p, cps):
        got(cps)

        def body(k, carry):
            x_ = k // Y
            y_ = k % Y
            add_to(gw.at[p, c, x_, y_], rc.at[p, x_, y_])
            return carry

        lax.fori_loop(0, X * Y, body, 0)
        if p in X_LAST:
            return [
                send(gw.at[p, c, xs(b)], r1a.at[X_LAST.index(p), b - 1], dev(x_=xs(b))) for b in range(1, X)
            ]
        return [
            send(gw.at[p, c, :, ys(b)], r1b.at[Y_LAST.index(p), b - 1], dev(y_=ys(b))) for b in range(1, Y)
        ]

    def rs_second(p, cps):
        got(cps)
        if p in X_LAST:
            for b in range(1, X):
                for y_ in range(Y):
                    add_to(gw.at[p, c, x, y_], r1a.at[X_LAST.index(p), b - 1, y_])
            return [
                send(gw.at[p, c, x, ys(b)], r2a.at[X_LAST.index(p), b - 1], dev(y_=ys(b)))
                for b in range(1, Y)
            ]
        for b in range(1, Y):
            for x_ in range(X):
                add_to(gw.at[p, c, x_, y], r1b.at[Y_LAST.index(p), b - 1, x_])
        return [
            send(gw.at[p, c, xs(b), y], r2b.at[Y_LAST.index(p), b - 1], dev(x_=xs(b))) for b in range(1, X)
        ]

    def rs_third(p, cps):
        got(cps)
        if p in X_LAST:
            for b in range(1, Y):
                add_to(gw.at[p, c, x, y], r2a.at[X_LAST.index(p), b - 1])
        else:
            for b in range(1, X):
                add_to(gw.at[p, c, x, y], r2b.at[Y_LAST.index(p), b - 1])
        if p == FO:
            return []
        return [
            send(gw.at[p, c, x, y, zs(a)], rz.at[p, a - 1], dev(z_=zs(a))) for a in range(1, Z)
        ]

    targets = {
        SQ: ("g_sq", 0), SK: ("g_skv", 0), SV: ("g_skv", D), SO: ("g_so", 0),
        CQ: ("g_cq", 0), CK: ("g_ckv", 0), CV: ("g_ckv", D), CO: ("g_co", 0),
        FI: ("g_fi", 0), FO: ("g_fo", 0),
    }

    def rs_last(p, cps):
        got(cps)
        name, off = targets[p]
        if p in (FI, FO):
            for a in range(Z):
                k = a if p == FO else zs(Z - a)
                if p == FO:
                    v = gw[p, c, x, y, a]
                else:
                    v = rz[p, a - 1] if a else gw[p, c, x, y, z]
                lo, hi = get_halves(v.astype(F32), r)
                if p == FI:
                    m["gfi"][k, :, 0:nh] = lo
                    m["gfi"][k, :, nh:D] = hi
                else:
                    m[name][k * r : k * r + r, 0:nh] = lo
                    m[name][k * r : k * r + r, nh:D] = hi
            if p == FI:
                for k in range(Z):
                    for i in range(ndp):
                        at = (i * Z + k) * per
                        m[name][:, at : at + per] = m["gfi"][k, :, i * per : (i + 1) * per]
            return None
        v = gw[p, c, x, y, z].astype(F32)
        for a in range(1, Z):
            v = v + rz[p, a - 1].astype(F32)
        lo, hi = get_halves(v, r)
        m[name][:, off : off + nh] = lo
        m[name][:, off + nh : off + D] = hi

    stages = (rs_first, rs_second, rs_third, rs_last) if sz.inside else ()
    moving = {}

    def grad_of(p, lhs, rhs):
        acc[...] = tn(lhs, rhs)
        grad_out(p)

    def grad_out(p):
        moving[p] = (0, pack_grad(p))

    def push(p):
        k, cps = moving[p]
        if k < len(stages):
            moving[p] = (k + 1, stages[k](p, cps))

    def push_all(ps):
        for p in ps:
            push(p)

    grad_of(FO, gl[...], gb)
    grad_of(FI, hb, du[...])
    got(zh)
    sm = m["sm"]
    sm[...] = jnp.zeros_like(sm)
    dh3 = rs_total(po.at[0], rzo)
    dv, gg = norm_back(m["x2"][...], gain[2:3, :], dh3)
    sm[2:3, :] = gg
    dx2 = live * m["og"][...] + dv
    m["dx"][...] = dx2
    dx2l = dx2.astype(BF)
    doc = nt(dx2l, w[CO]).astype(BF)
    do, dr = m["do"], m["dr"]
    do[z, y] = doc
    pick = iota((T, D), 0) == (iota((T, D), 1) & (T - 1))

    def as_rows(st):
        v = jnp.sum(jnp.where(pick, expand(st), 0.0), axis=0, keepdims=True)
        parts = [v[:, k * 128 : (k + 1) * 128] for k in range(D // 128)]
        return jnp.concatenate(parts + [jnp.zeros((8 - D // 128, 128), F32)], axis=0)

    prod = doc.astype(F32) * m["oc"][...].astype(F32)
    delta = lax.dot_general(
        spread[...], prod, (((1,), (1,)), ((), ())), preferred_element_type=F32, precision=HIGH
    )
    dr[z, y, 0:8] = as_rows(m["lse"][...])
    dr[z, y, 8:16] = as_rows(delta)
    do_base = take(2 * YZ)
    act_start(do_base, [do, dr])
    act_forward(do_base, [do, dr], 0)
    zy = rs_z(py, rzy)
    grad_of(CO, m["oc"][...], dx2l)

    sent(zh)
    yq_base = rs_y_base()

    def row_of(ref, k):
        return jnp.concatenate([ref[2 * k : 2 * k + 1, :], ref[2 * k + 1 : 2 * k + 2, :]], axis=1)

    def attend_back(t, carry):
        a = t % Z
        b = t // Z
        zi = zs(a)
        yi = ys(b)
        qi = zi * Y + yi

        @pl.when(t > 0)
        def _():
            act_wait(do_base, [do, dr], t)

        @pl.when((t > 0) & (t < Z))
        def _():
            act_forward(do_base, [do, dr], a)

        lse_rows = dr[zi, yi, 0:8]
        delta_rows = dr[zi, yi, 8:16]
        for k in range(NQ):
            qb = stack4(qc[zi, yi, :, quad(k)])
            db = stack4(do[zi, yi, :, quad(k)])
            kt = kv[qi, :, quad(k)]
            vt = kv[qi, :, D + k * WIDE : D + (k + 1) * WIDE]
            pt = jnp.exp(nt(kt, qb) - row_of(lse_rows, k))
            ds = (pt * (nt(vt, db) - row_of(delta_rows, k))).astype(BF)
            po[b, zi, :, quad(k)] = fold4(tn(ds, kt)).astype(BF)
            kv[qi, :, quad(k)] = nn(ds, qb).astype(BF)
            kv[qi, :, D + k * WIDE : D + (k + 1) * WIDE] = nn(pt.astype(BF), db).astype(BF)

        @pl.when(t >= Z)
        def _():
            rs_y_send(yq_base, po, ryo, b, a)

        return carry

    lax.fori_loop(0, 2, attend_back, 0)
    push_all([FO, FI])
    lax.fori_loop(2, Z, attend_back, 0)
    push_all([CO])
    lax.fori_loop(Z, YZ, attend_back, 0)

    def kv_grad(p, off):
        if R % 16 == 0:
            acc[...] = tn(pas[...].reshape(YZ * R, D), kv[:, :, off : off + D].reshape(YZ * R, D))
        else:
            acc[...] = jnp.zeros_like(acc)

            def body(q, carry):
                acc[...] += tn(pas[q], kv[q, :, off : off + D])
                return carry

            lax.fori_loop(0, YZ, body, 0)
        grad_out(p)

    def row_grads(k0, k1):
        def body(k, carry):
            if chunk == 1:
                pas[k] = (nt(kv[k, :, 0:D], w[CK]) + nt(kv[k, :, D : 2 * D], w[CV])).astype(BF)
            else:
                rows = pl.ds(k * chunk, chunk)
                v = nt(kv[rows, :, 0:D].reshape(chunk * R, D), w[CK])
                v = v + nt(kv[rows, :, D : 2 * D].reshape(chunk * R, D), w[CV])
                pas[rows] = v.astype(BF).reshape(chunk, R, D)
            for q in range(chunk):
                at = k * chunk + q
                pltpu.make_async_copy(pas.at[at], m["pg"].at[at], lsem.at[1 + at]).start()
            return carry

        lax.fori_loop(k0, k1, body, 0)

    kv_grad(CK, 0)
    zq = []
    for a in list(range(1, Z)) + [0]:
        zi = zs(a)
        for b in range(1, Y):
            rs_y_wait(yq_base, po, ryo, b, a)
        tot = po[0, zi].astype(F32)
        for b in range(1, Y):
            tot = tot + ryo[b - 1, zi].astype(F32)
        po[0, zi] = tot.astype(BF)
        if a:
            zq.append(send(po.at[0, zi], rzo.at[a - 1], dev(z_=zi)))
    kv_grad(CV, D)
    push_all([CK, FO, FI])
    half = YZ // chunk // 2
    row_grads(0, half)
    push_all([CV, CO])
    got(zq)
    dqc = rs_total(po.at[0], rzo).astype(BF)
    dh2 = nt(dqc, w[CQ])
    dv, gg = norm_back(m["x1"][...], gain[1:2, :], dh2)
    sm[1:2, :] = gg
    dx1 = m["dx"][...] + dv
    m["dx"][...] = dx1
    dx1l = dx1.astype(BF)
    grad_of(CQ, m["h2"][...], dqc)
    grad_of(SO, m["os"][...], dx1l)
    push_all([CQ])

    m["oc"][...] = nt(dx1l, w[SO]).astype(BF)
    grads = [[], [], []]
    tail = []
    for t in range(NQ):
        db = stack4(m["oc"][:, quad(t)])
        qb = stack4(m["qs"][:, quad(t)])
        pr = m["ps"][t]
        dps = nt(db, m["vs"][:, quad(t)])
        dss = (pr * (dps - jnp.sum(pr * dps, axis=1, keepdims=True))).astype(BF)
        grads[0].append(fold4(nn(dss, m["ks"][:, quad(t)])).astype(BF))
        grads[1].append(tn(dss, qb).astype(BF))
        grads[2].append(tn(pr.astype(BF), db).astype(BF))
        back = (iota((T, 128), 1) == T - 1 - iota((T, 128), 0)).astype(F32).astype(BF)
        turned = nn(dss, back)
        for h in range(QUAD):
            part = pltpu.roll(turned[h * T : (h + 1) * T], 0, 1, stride=1, stride_axis=0)
            tail.append(jnp.sum(part, axis=0, keepdims=True))
    dqs, dks, dvs = (jnp.concatenate(g, axis=1) for g in grads)
    h1 = m["h1"][...]
    grad_of(SV, h1, dvs)
    push(SO)
    grad_of(SQ, h1, dqs)
    push(SV)
    grad_of(SK, h1, dks)
    push(SQ)
    dh1 = nt(dqs, w[SQ]) + nt(dks, w[SK]) + nt(dvs, w[SV])
    dv, gg = norm_back(tok[...], gain[0:1, :], dh1)
    sm[0:1, :] = gg
    m["tg"][...] = m["dx"][...] + dv
    flat = HEADS * BUCKETS
    diag = jnp.concatenate(tail + [jnp.zeros((16 - HEADS, 128), F32)], axis=0)
    mi, bi = iota((128, 128), 0), iota((128, 128), 1)
    hot = ((mi >= T - 1) & (bucket_of(mi - (T - 1)) == bi) & (bi < BUCKETS)).astype(F32)
    table = nn_high(diag, hot)
    bb, nb = iota((128, flat), 0), iota((128, flat), 1)
    wide = nn_high(table, ((nb & (BUCKETS - 1)) == bb).astype(F32))
    h0, n0 = iota((16, flat), 0), iota((16, flat), 1)
    own = (n0 >= h0 * BUCKETS) & (n0 < h0 * BUCKETS + BUCKETS)
    sm[3:4, 0:flat] = jnp.sum(jnp.where(own, wide, 0.0), axis=0, keepdims=True)

    rsm = m["rsm"]
    slot = [0]

    def small_send(devs):
        cps = []
        for to in devs:
            cps.append((slot[0], send(sm, rsm.at[slot[0]], to)))
            slot[0] += 1
        return cps

    def small_end(cps):
        got([cp for _, cp in cps])
        sent([cp for _, cp in cps])
        for k, _ in cps:
            sm[...] += rsm[k]

    def small_sum(devs):
        small_end(small_send(devs))

    small_sum([dev(c_=oth)])
    push(SK)
    small_x = small_send([dev(x_=xs(b)) for b in range(1, X)])
    push(CK)
    push(CV)
    push_all([FO, FI, CO])
    row_grads(half, YZ // chunk)
    push(CQ)
    push(CK)
    push(SO)
    push(CV)
    push(SV)
    push_all([FO, FI, CO])
    small_end(small_x)
    small_y = small_send([dev(y_=ys(b)) for b in range(1, Y)])
    got(zy)
    m["bo"][...] = live * (m["x2"][...] + rs_total(py, rzy))
    push(SQ)
    push(CQ)
    push(SK)
    push(SO)
    push_all([CK, CV])
    small_end(small_y)
    small_z = small_send([dev(z_=zs(a)) for a in range(1, Z)])
    push(SV)
    push(SQ)
    push(SK)
    push_all([CQ, SO])
    small_end(small_z)
    push_all([SV, SQ, SK])
    assert all(k == len(stages) for k, _ in moving.values())
    me = dp * YZ + fs
    nd, ld = iota((D, 128), 0), iota((D, 128), 1)
    mine = nn_high(sm[...], ((nd == me * r + ld) & (ld < r)).astype(F32))
    mine_b = nn_high(sm[...], ((nd == me * rbs + ld) & (ld < rbs)).astype(F32))
    m["g_ls"][...] = mine[0:1, 0:r]
    m["g_lc"][...] = mine[1:2, 0:r]
    m["g_lf"][...] = mine[2:3, 0:r]
    m["g_rb"][...] = mine_b[3:4, 0:rbs]

    act_done(do_base, [do, dr])
    rs_y_done(yq_base, po, ryo)
    drain()

    def pg_wait(q, carry):
        pltpu.make_async_copy(pas.at[q], m["pg"].at[q], lsem.at[1 + q]).wait()
        return carry

    lax.fori_loop(0, YZ, pg_wait, 0)


def place_kernel(*refs):
    n = len(OUTPUTS)
    copies = [
        pltpu.make_async_copy(refs[k], refs[n + k], refs[2 * n].at[k]) for k in range(n)
    ]
    for cp in copies:
        cp.start()
    for cp in copies:
        cp.wait()


def per_device(
    sz,
    targets, passages, tgt_len, out_grad, ln_self, rel_bias, self_q, self_kv, self_out,
    ln_cross, cross_q, cross_kv, cross_out, ln_ff, ff_in, ff_out,
):
    T, D, r, Z = sz.T, sz.D, sz.r, sz.Z
    ndp = 2 * sz.X
    per = sz.Y * sz.rff
    scratch = layout(sz)
    names = tuple(scratch)
    gr = r if sz.inside else D
    vm = pl.BlockSpec(memory_space=pltpu.VMEM)
    hbm = pl.BlockSpec(memory_space=pltpu.HBM)
    smem = pl.BlockSpec(memory_space=pltpu.SMEM)
    shape = jax.ShapeDtypeStruct
    rbs = rel_bias.shape[0]
    out_shape = (
        shape((T, D), F32), shape((T, D), F32), shape(passages.shape, BF),
        shape((1, r), F32), shape((1, rbs), F32),
        shape((gr, D), F32), shape((gr, 2 * D), F32), shape((gr, D), F32),
        shape((1, r), F32), shape((gr, D), F32), shape((gr, 2 * D), F32), shape((gr, D), F32),
        shape((1, r), F32),
        shape((r, Z * D) if sz.inside else (D, D), F32),
        shape((Z * r, D) if sz.inside else (D, D), F32),
    )
    weight_outs = ("g_sq", "g_skv", "g_so", "g_cq", "g_ckv", "g_co", "g_fi", "g_fo")
    apart = ("pg",) if sz.inside else ("pg",) + weight_outs
    outs = pl.pallas_call(
        functools.partial(block_kernel, sz, names),
        out_shape=out_shape,
        in_specs=[{"pas_in": hbm, "len": smem}.get(n, vm) for n in INPUTS],
        out_specs=tuple(hbm if n in apart else vm for n in OUTPUTS),
        scratch_shapes=tuple(scratch.values()),
        compiler_params=pltpu.CompilerParams(
            collective_id=0, has_side_effects=True, vmem_limit_bytes=63 * 2**20
        ),
        cost_estimate=pl.CostEstimate(
            flops=20 * 10**9, bytes_accessed=2 * 10**7, transcendentals=4 * 10**6
        ),
    )(
        targets[0], passages, tgt_len, out_grad[0], ln_self[None], rel_bias[None],
        self_q, self_kv, self_out, ln_cross[None], cross_q, cross_kv, cross_out,
        ln_ff[None], ff_in, ff_out,
    )
    (bo, tg, pg, g_ls, g_rb, g_sq, g_skv, g_so, g_lc, g_cq, g_ckv, g_co, g_lf, g_fi, g_fo) = outs
    if not sz.inside:
        at = lax.axis_index("fsdp") // sz.Y
        rows = jnp.zeros((ndp, Z, per, D), F32).at[:, at].set(g_fo.reshape(ndp, per, D))
        cols = jnp.zeros((D, ndp, Z, per), F32).at[:, :, at].set(g_fi.reshape(D, ndp, per))
        g_sq, g_skv, g_so, g_cq, g_ckv, g_co, g_fi, g_fo = (
            lax.psum_scatter(g, ("dp", "fsdp"), scatter_dimension=0, tiled=True)
            for g in (
                g_sq, g_skv, g_so, g_cq, g_ckv, g_co,
                cols.reshape(D, Z * D), rows.reshape(Z * D, D),
            )
        )
    outs = (bo, tg, pg, g_ls, g_rb, g_sq, g_skv, g_so, g_lc, g_cq, g_ckv, g_co, g_lf, g_fi, g_fo)
    if sz.inside:
        outs = pl.pallas_call(
            place_kernel,
            out_shape=tuple(shape(o.shape, o.dtype) for o in outs),
            in_specs=[vm] * len(outs),
            out_specs=(hbm,) * len(outs),
            scratch_shapes=(pltpu.SemaphoreType.DMA((len(outs),)),),
            compiler_params=pltpu.CompilerParams(vmem_limit_bytes=63 * 2**20),
        )(*outs)
    (bo, tg, pg, g_ls, g_rb, g_sq, g_skv, g_so, g_lc, g_cq, g_ckv, g_co, g_lf, g_fi, g_fo) = outs
    return (
        bo[None], tg[None], pg, g_ls[0], g_rb[0], g_sq, g_skv, g_so,
        g_lc[0], g_cq, g_ckv, g_co, g_lf[0], g_fi, g_fo,
    )


def solution(mesh):
    both = ("dp", "fsdp")
    rows3, rows2, rows1 = P(both, None, None), P(both, None), P(both)
    placed = (
        rows3, P("dp", "fsdp", None), rows1, rows3, rows1, rows1, rows2, rows2, rows2,
        rows1, rows2, rows2, rows2, rows1, rows2, rows2,
    )
    outs = (
        rows3, rows3, P("dp", "fsdp", None), rows1, rows1, rows2, rows2, rows2,
        rows1, rows2, rows2, rows2, rows1, rows2, rows2,
    )

    def run(*args):
        targets, passages, self_q, ff_out = args[0], args[1], args[6], args[15]
        sz = Sizes(
            mesh.shape,
            targets.shape[2], passages.shape[1], targets.shape[1],
            self_q.shape[0], ff_out.shape[0],
            ff_out.shape[0] * mesh.shape["dp"] * mesh.shape["fsdp"] // ZDIM,
        )
        return per_device(sz, *args)

    return jax.shard_map(run, mesh=mesh, in_specs=placed, out_specs=outs, check_vma=False)
```

time: 274 us -> 210 us (0.77)
  Pallas kernels: 252 us -> 208 us
  local copies, waits for them, and re-layouts: 19.9 us -> 0 us
    pallas_call x1, Pallas kernels: 252 us -> 204 us  [per_device(): pl.pallas_call(functools.partial(block_kernel, sz, names), out_shape=out_...]
    unnamed x38 -> x0, local copies, waits for them, and re-layouts: 11.5 us -> none
    pallas_call x0 -> x1, Pallas kernels: none -> 4.65 us  [per_device(): pl.pallas_call(place_kernel, out_shape=tuple((shape(o.shape, o.dtype) for...]
    reshape x5 -> x0, local copies, waits for them, and re-layouts: 4.65 us -> none  [the longest x2 3.29 us: per_device(): g_fi.reshape(nfs, r, ndp, rff).transpose(1, 2, 0, 3)]
where the time goes in v2:
time: 210 us
  Pallas kernels  208 us (99%)
    pallas_call x1, Pallas kernels, per_device(): pl.pallas_call(functools.partial(block_kernel, sz, names), out_shape=out_...  204 us
    pallas_call x1, Pallas kernels, per_device(): pl.pallas_call(place_kernel, out_shape=tuple((shape(o.shape, o.dtype) for...  4.65 us

profile of v2, /device:TPU:0, one launch (start us, length us, event | category | flops | bytes accessed | tf_op | source)
XLA Modules:
  0.0 209.9 jit_solution(17091822599901630111)
XLA Ops:
  1.3 203.8 %shard_map.271 = (f32[64,768]{1,0:T(8,128)}, f32[64,768]{1,0:T(8,128)}, bf16[8,240,768]{2,1,0:T(8,128)(2,1)}, f32[1,24]{1,0:T(1,128)}, f32[1,12]{1,0:T(1,128)}, ...) custom-call(f32[64,768]{1,0:T(8,128)} %bitcast.12, ...), custom_call_target="tpu_custom_call" | custom-call | flops 20000000000 | bytes 20000000 | tf_op jit(solution)/shard_map/pallas_call | solution.py:1229
  205.1 4.7 %shard_map.272 = (f32[64,768]{1,0:T(8,128)}, f32[64,768]{1,0:T(8,128)}, bf16[8,240,768]{2,1,0:T(8,128)(2,1)}, f32[1,24]{1,0:T(1,128)}, f32[1,12]{1,0:T(1,128)}, ...) custom-call(f32[64,768]{1,0:T(8,128)} %get-tuple-element.45.refs_0_,, ...), custom_call_target="tpu_custom_call" | custom-call | tf_op jit(solution)/shard_map/pallas_call | solution.py:1260

commit v3 on v2

--- a/solution.py
+++ b/solution.py
@@ -20,9 +20,9 @@
 F32 = jnp.float32
 PIECES = 10
 SQ, SK, SV, SO, CQ, CK, CV, CO, FI, FO = range(PIECES)
-X_LAST = (SQ, SV, CQ, CV, CO, FI, FO)
-Y_LAST = (SK, SO, CK)
-Y_GATHERED_LAST = (SK, CK)
+X_LAST = (CK, CV, CQ, SO, SQ, SK, CO, FI, FO)
+Y_LAST = (SV,)
+Y_GATHERED_LAST = (SQ, SV, CQ)
 ZDIM = 4
 
 
@@ -88,6 +88,46 @@
     half = 0.5 * (1.0 + th)
     slope = half + 0.5 * u * (1.0 - th * th) * cst * (1.0 + 3.0 * cubic * u * u)
     return u * half, slope
+
+
+class Spot:
+    def __init__(self, base, steps=()):
+        self.base, self.steps = base, steps
+
+    @property
+    def at(self):
+        return Steps(self)
+
+    def ref(self):
+        out = self.base
+        for step in self.steps:
+            out = out.at[step]
+        return out
+
+    def __getitem__(self, key):
+        return self.ref()[key]
+
+    def __setitem__(self, key, value):
+        self.ref()[key] = value
+
+
+class Steps:
+    def __init__(self, spot):
+        self.spot = spot
+
+    def __getitem__(self, key):
+        return Spot(self.spot.base, self.spot.steps + (key,))
+
+
+class Sent:
+    def __init__(self, make):
+        self.make = make
+
+    def wait_recv(self):
+        self.make().wait_recv()
+
+    def wait_send(self):
+        self.make().wait_send()
 
 
 class Sizes:
@@ -108,7 +148,7 @@
 
 
 def sems(sz):
-    return 264 if sz.inside else 900
+    return 199 if sz.inside else 900
 
 
 def layout(sz):
@@ -130,10 +170,9 @@
         gw=V((PIECES, 2, X, Y, Z, rb, nh), BF),
         w=V((PIECES, D, D), BF),
         fip=V((Z, rb, nh), BF),
-        acc=V((D, D), F32),
+        kvacc=V((D, 2 * D), F32),
         lift=V((max(Y * Z * sz.r, sz.rff) if sz.r % 8 else 8, D), F32),
         even=V((sz.r, D), F32),
-        gfi=V((Z, sz.r, D), F32),
         cell=V((rb, nh), F32),
         smb=V((2, X, Y, Z, 16, 128), BF),
         hot_gain=V((128, D), BF),
@@ -141,6 +180,7 @@
         gain=V((16, D), F32),
         bias=V((NQ, WIDE, T), F32),
         spread=V((16, D), F32),
+        spread2=V((32, D), BF),
         mask=V((WIDE, WIDE), BF),
         pas=V((Y * Z, R, D), BF),
         kv=V((Y * Z, R, 2 * D), BF),
@@ -169,7 +209,6 @@
         rzst=V((Z - 1, 16, T), F32),
         py=V((Z, T, D), BF),
         rzy=V((Z - 1, T, D), BF),
-        da=V((Z * T, hid), F32),
         gl=V((Z * T, hid), BF),
         du=V((Z * T, hid), BF),
         sm=V((8, D), F32),
@@ -180,6 +219,65 @@
     )
 
 
+TAIL = (
+    "ck",
+    "cv",
+    "CO",
+    "FI",
+    "FO",
+    "pass",
+    "CK",
+    "CV",
+    "rows1",
+    "CO",
+    "dq",
+    "FI",
+    "cq",
+    "so",
+    "CK",
+    "FO",
+    "selfback",
+    "CQ",
+    "FO",
+    "CO",
+    "sv",
+    "SO",
+    "sq",
+    "FI",
+    "sk",
+    "CV",
+    "SV",
+    "CK",
+    "dh1",
+    "small",
+    "SQ",
+    "SK",
+    "rows2",
+    "small",
+    "CQ",
+    "CV",
+    "bo",
+    "CK",
+    "SO",
+    "SV",
+    "CV",
+    "CQ",
+    "SQ",
+    "SO",
+    "CQ",
+    "SQ",
+    "SK",
+    "small",
+    "SO",
+    "SV",
+    "SQ",
+    "SK",
+    "small",
+    "SV",
+    "SK",
+    "small",
+)
+
 INPUTS = (
     "tok", "pas_in", "len", "og", "ls", "rel", "sq", "skv", "so",
     "lc", "cq", "ckv", "co", "lf", "fi_in", "fo_in",
@@ -195,6 +293,9 @@
     m = dict(zip(INPUTS, refs[:n_in]))
     m.update(zip(OUTPUTS, refs[n_in : n_in + n_out]))
     m.update(zip(names, refs[n_in + n_out :]))
+    for name in ("gw", "smb", "fip", "rc", "r1a", "r1b", "r2a", "r2b", "rz"):
+        if name in m:
+            m[name] = Spot(m[name])
     X, Y, Z, D, T, R = sz.X, sz.Y, sz.Z, sz.D, sz.T, sz.R
     r, rb, nh, hid = sz.r, sz.rb, sz.nh, sz.hid
     NQ = HEADS // QUAD
@@ -205,42 +306,76 @@
     z, y = fs // Y, fs % Y
     oth = 1 - c
 
+    ring_x = [(x + b) % X for b in range(X)]
+    ring_y = [(y + b) % Y for b in range(Y)]
+    ring_z = [(z + b) % Z for b in range(Z)]
+
+    def around(ring, at, b):
+        return ring[b] if isinstance(b, int) else (at + b) % len(ring)
+
     def xs(b):
-        return (x + b) % X
+        return around(ring_x, x, b)
 
     def ys(b):
-        return (y + b) % Y
+        return around(ring_y, y, b)
 
     def zs(b):
-        return (z + b) % Z
-
-    def dev(x_=None, c_=None, y_=None, z_=None):
+        return around(ring_z, z, b)
+
+    def any_dev(x_=None, c_=None, y_=None, z_=None):
         x_ = x if x_ is None else x_
         c_ = c if c_ is None else c_
         y_ = y if y_ is None else y_
         z_ = z if z_ is None else z_
         return (x_ * 2 + c_, z_ * Y + y_)
 
+    near = {}
+
+    def dev(x_=None, c_=None, y_=None, z_=None):
+        key = (id(x_), id(c_), id(y_), id(z_))
+        if key not in near:
+            return any_dev(x_, c_, y_, z_)
+        return near[key]
+
+    none = id(None)
+    near[(none, id(oth), none, none)] = any_dev(c_=oth)
+    for v in ring_x:
+        near[(id(v), none, none, none)] = any_dev(x_=v)
+    for v in ring_y:
+        near[(none, none, id(v), none)] = any_dev(y_=v)
+    for v in ring_z:
+        near[(none, none, none, id(v))] = any_dev(z_=v)
+
     ssem, rsem, lsem = m["ssem"], m["rsem"], m["lsem"]
     n_sems = sems(sz)
     used = [0]
     pending = []
 
+    spare = []
+    early = [False, []]
+
     def take(n=1):
+        if n == 1 and spare:
+            return spare.pop(0)
         at = used[0]
         used[0] += n
         assert used[0] <= n_sems
         return at
 
     def copy_at(i, src, dst, to):
+        src = src.ref() if isinstance(src, Spot) else src
+        dst = dst.ref() if isinstance(dst, Spot) else dst
         return pltpu.make_async_remote_copy(
             src_ref=src, dst_ref=dst, send_sem=ssem.at[i], recv_sem=rsem.at[i],
             device_id=to, device_id_type=pl.DeviceIdType.MESH,
         )
 
     def send(src, dst, to):
-        cp = copy_at(take(), src, dst, to)
-        cp.start()
+        i = take()
+        if early[0]:
+            early[1].append(i)
+        cp = Sent(lambda: copy_at(i, src, dst, to))
+        cp.make().start()
         pending.append(cp)
         return cp
 
@@ -314,7 +449,9 @@
         return out
 
     class Gather:
-        def __init__(self, buf, y_first, feed="gather"):
+        def __init__(self, buf, y_first, feed="gather", first=False):
+            self.first = first
+            early[0] = first
             self.buf, self.y_first, self.feed = buf, y_first, feed
             own = buf.at[c, x, y, z]
             self.z = []
@@ -323,20 +460,26 @@
                     self.z.append(send(own, own, dev(z_=zs(a))))
                 elif feed == "exchange":
                     self.z.append(send(m["fip"].at[zs(a)], own, dev(z_=zs(a))))
+            early[0] = False
 
         def own_out(self):
+            early[0] = self.first
             blocks = range(Z) if self.feed == "local" else [z]
             self.second = line_to(self.buf, self.y_first, blocks)
             self.third = line_to(self.buf, not self.y_first, blocks)
+            early[0] = False
 
         def line_out(self):
+            early[0] = self.first
             got(self.z)
             if self.feed != "local":
-                blocks = [zs(Z - a) for a in range(1, Z)]
+                blocks = [zs((Z - a) % Z) for a in range(1, Z)]
                 self.second += line_to(self.buf, self.y_first, blocks)
                 self.third += line_to(self.buf, not self.y_first, blocks)
+            early[0] = False
 
         def plane_out(self):
+            early[0] = self.first
             got(self.second)
             buf = self.buf
             if self.y_first:
@@ -347,10 +490,13 @@
                 for b in range(1, X):
                     line = buf.at[c, xs(b), y]
                     self.third += [send(line, line, dev(y_=ys(d))) for d in range(1, Y)]
+            early[0] = False
 
         def core_out(self):
+            early[0] = self.first
             got(self.third)
             self.core = [send(self.buf.at[c], self.buf.at[c], dev(c_=oth))]
+            early[0] = False
 
         def end(self):
             got(self.core)
@@ -364,9 +510,9 @@
     moves = {}
 
     def begin(p, feed="gather"):
-        moves[p] = Gather(gw.at[p], p not in Y_GATHERED_LAST, feed)
-
-    moves["small"] = Gather(smb, True)
+        moves[p] = Gather(gw.at[p], p not in Y_GATHERED_LAST, feed, p < CO)
+
+    moves["small"] = Gather(smb, True, first=True)
     moves["small"].own_out()
     sources = (
         (m["sq"], 0), (m["skv"], 0), (m["skv"], D), (m["so"], 0),
@@ -380,7 +526,7 @@
         begin(p)
         moves[p].own_out()
 
-    for p in (SQ, SK, SV, SO, CQ, CK, CV):
+    for p in (SQ, SK, SV, SO, CQ, CK, CV, CO):
         pack(p)
 
     g3 = m["g3"]
@@ -442,12 +588,12 @@
         gw[FI, c, x, y, z] = fip[z]
 
     g3_base = take(Z)
-    line_start(g3_base, g3)
 
     spread = m["spread"]
     lane = iota((16, D), 1)
     row = iota((16, D), 0)
     spread[...] = ((lane >= row * DK) & (lane < row * DK + DK)).astype(F32)
+    m["spread2"][...] = jnp.concatenate([spread[...], spread[...]], axis=0).astype(BF)
     tlane = iota((T, 128), 1)
     rbs = HEADS * BUCKETS // (2 * X * YZ)
 
@@ -557,28 +703,26 @@
     def cross_query():
         qc[z, y] = nn(m["h2"][...], w[CQ]).astype(BF)
         act_start(qc_base, [qc])
+        act_forward(qc_base, [qc], 0)
 
     kv, pas = m["kv"], m["pas"]
 
     chunk = 4 if R % 16 == 0 else 1
 
     def project(p, off):
-        def body(k, carry):
-            if chunk == 1:
-                kv[k, :, off : off + D] = nn(pas[k], w[p]).astype(BF)
-            else:
-                rows = pl.ds(k * chunk, chunk)
-                v = nn(pas[rows].reshape(chunk * R, D), w[p])
-                kv[rows, :, off : off + D] = v.astype(BF).reshape(chunk, R, D)
+        def part(k, carry):
+            rows = pl.ds(k // NQ * chunk, chunk)
+            at = k % NQ * WIDE
+            cols = pl.ds(pl.multiple_of(at, WIDE), WIDE)
+            v = nn(pas[rows].reshape(chunk * R, D), w[p, :, cols])
+            cols = pl.ds(pl.multiple_of(off + at, WIDE), WIDE)
+            kv[rows, :, cols] = v.astype(BF).reshape(chunk, R, WIDE)
             return carry
 
-        lax.fori_loop(0, YZ // chunk, body, 0)
-
-    def query_forward():
-        for a in range(Z):
-            if a:
-                act_wait(qc_base, [qc], a)
-            act_forward(qc_base, [qc], a)
+        lax.fori_loop(0, YZ // chunk * NQ, part, 0)
+
+    def project_one(q, p, off):
+        kv[q, :, off : off + D] = nn(pas[q], w[p]).astype(BF)
 
     def after(p):
         unpack(p)
@@ -594,9 +738,6 @@
         elif p == CK:
             load_pas.wait()
             project(CK, 0)
-        elif p == CV:
-            query_forward()
-            project(CV, D)
 
     order = (SQ, SK, SV, SO, CQ, CK, CV, CO, FI, FO)
 
@@ -619,28 +760,51 @@
         moves[order[k]].end()
         after(order[k])
 
-    for k in range(7):
-        line_out(k)
-        if k == 1:
-            pack_ff()
-        if k >= 1:
-            plane_out(k - 1)
-        if k >= 2:
-            core_out(k - 2)
-        if k >= 3:
-            arrive(k - 3)
+    def query_out(a):
+        act_wait(qc_base, [qc], a)
+        act_forward(qc_base, [qc], a)
+
+    line_out(0)
+    line_out(1)
+    pack_ff()
+    begin(FI, "exchange")
+    plane_out(0)
+    line_out(2)
+    plane_out(1)
+    line_out(3)
+    core_out(0)
+    plane_out(2)
+    arrive(0)
+    line_out(4)
+    core_out(1)
+    plane_out(3)
+    arrive(1)
+    line_out(5)
+    core_out(2)
+    plane_out(4)
+    arrive(2)
+    line_out(6)
+    core_out(3)
+    plane_out(5)
+    arrive(3)
+    core_out(4)
+    arrive(4)
+    line_start(g3_base, g3)
     plane_out(6)
-    pack(CO)
-    begin(FI, "exchange")
     core_out(5)
-    arrive(4)
+    line_out(7)
+    begin(FO, "local")
+    moves[FI].own_out()
+    moves[FO].own_out()
+    line_out(8)
+    line_out(9)
+    arrive(5)
+    query_out(1)
     core_out(6)
-    arrive(5)
-    line_out(7)
-    moves[FI].own_out()
-    begin(FO, "local")
-    moves[FO].own_out()
+    query_out(2)
     arrive(6)
+    plane_out(7)
+    query_out(3)
 
     po, pst, ryo, ryst, rzo, rzst = (m[k] for k in ("po", "pst", "ryo", "ryst", "rzo", "rzst"))
 
@@ -687,6 +851,13 @@
             st, spread[...], (((0,), (0,)), ((), ())), preferred_element_type=F32, precision=HIGH
         )
 
+    def expand_low(v):
+        hi = v.astype(BF)
+        lo = (v - hi.astype(F32)).astype(BF)
+        both = jnp.concatenate([hi, lo], axis=0)
+        ones = m["spread2"][...]
+        return tn(both, ones)
+
     def merge(parts):
         top = parts[0][1]
         for _, st in parts[1:]:
@@ -697,7 +868,7 @@
             tot = tot + v
         out = jnp.zeros((T, D), F32)
         for (o, _), v in zip(parts, ws):
-            out = out + expand(v / tot) * o.astype(F32)
+            out = out + expand_low(v / tot) * o.astype(F32)
         return out, top + jnp.log(tot)
 
     def z_send(base, src, dst, a):
@@ -712,44 +883,52 @@
             else:
                 cp.wait_send()
 
-    def attend_other(t, carry):
+    def pass_on(a):
+        zi = zs(a)
+        for b in range(1, Y):
+            rs_y_wait(yo_base, po, ryo, b, a)
+            rs_y_wait(yst_base, pst, ryst, b, a)
+        o, st = merge(
+            [(po[0, zi], pst[0, zi])] + [(ryo[b - 1, zi], ryst[b - 1, zi]) for b in range(1, Y)]
+        )
+        po[0, zi] = o.astype(BF)
+        pst[0, zi] = st
+        z_send(zo_base, po, rzo, a)
+        z_send(zst_base, pst, rzst, a)
+
+    def attend_step(t, carry):
         a = (1 + t % Z) % Z
-        b = 1 + t // Z
-        act_wait(qc_base, [qc], b * Z + a)
+        b = (1 + t // Z) % Y
+
+        project_one(zs(a) * Y + ys(b), CV, D)
+
+        @pl.when(b > 0)
+        def _():
+            act_wait(qc_base, [qc], b * Z + a)
+
         attend(a, b)
-        rs_y_send(yo_base, po, ryo, b, a)
-        rs_y_send(yst_base, pst, ryst, b, a)
+
+        @pl.when(b > 0)
+        def _():
+            rs_y_send(yo_base, po, ryo, b, a)
+            rs_y_send(yst_base, pst, ryst, b, a)
+
+        @pl.when((b == 0) & (a > 0))
+        def _():
+            pass_on(a)
+
+        @pl.when(t == YZ - Z - 1)
+        def _():
+            core_out(7)
+
+        @pl.when(t == 1)
+        def _():
+            plane_out(8)
+            plane_out(9)
+
         return carry
 
-    def attend_own(t, carry):
-        a = (1 + t) % Z
-        zi = zs(a)
-        attend(a, 0)
-
-        @pl.when(t < Z - 1)
-        def _():
-            for b in range(1, Y):
-                rs_y_wait(yo_base, po, ryo, b, a)
-                rs_y_wait(yst_base, pst, ryst, b, a)
-            o, st = merge(
-                [(po[0, zi], pst[0, zi])]
-                + [(ryo[b - 1, zi], ryst[b - 1, zi]) for b in range(1, Y)]
-            )
-            po[0, zi] = o.astype(BF)
-            pst[0, zi] = st
-            z_send(zo_base, po, rzo, a)
-            z_send(zst_base, pst, rzst, a)
-
-        return carry
-
-    lax.fori_loop(0, (Y - 1) * Z, attend_other, 0)
-    plane_out(7)
-    line_out(8)
-    line_out(9)
-    lax.fori_loop(0, Z, attend_own, 0)
-    core_out(7)
-    plane_out(8)
-    plane_out(9)
+    lax.fori_loop(0, YZ, attend_step, 0)
     arrive(7)
     for b in range(1, Y):
         rs_y_wait(yo_base, po, ryo, b, 0)
@@ -776,7 +955,7 @@
     line_wait(g3_base, g3)
     arrive(9)
     gb = g3[...].reshape(Z * T, D)
-    m["da"][...] = nt(gb, w[FO])
+    m["kvacc"].at[0 : Z * T, 0:hid][...] = nt(gb, w[FO])
     act_done(qc_base, [qc])
     rs_y_done(yo_base, po, ryo)
     rs_y_done(yst_base, pst, ryst)
@@ -786,9 +965,8 @@
     py, rzy = m["py"], m["rzy"]
     gl, du = m["gl"], m["du"]
     line_wait(h3_base, h3)
-    hb = h3[...].reshape(Z * T, D)
-    act, slope = gelu_pair(nn(hb, w[FI]))
-    du[...] = (m["da"][...] * slope).astype(BF)
+    act, slope = gelu_pair(nn(h3[...].reshape(Z * T, D), w[FI]))
+    du[...] = (m["kvacc"].at[0 : Z * T, 0:hid][...] * slope).astype(BF)
     gl[...] = act.astype(BF)
     po[0] = nt(du[...], w[FI]).astype(BF).reshape(Z, T, D)
 
@@ -806,19 +984,26 @@
     line_done(h3_base, h3)
     line_done(g3_base, g3)
 
-    acc = m["acc"]
+    acc = m["kvacc"].at[:, 0:D]
 
     def add_to(dst, src):
         dst[...] = (dst[...].astype(F32) + src[...].astype(F32)).astype(BF)
 
+    def add_blocks(rows, dst, src):
+        def body(i, carry):
+            add_to(dst(i // Z, i % Z), src(i // Z, i % Z))
+            return carry
+
+        lax.fori_loop(0, rows * Z, body, 0)
+
     rc, r1a, r1b, r2a, r2b, rz = (m.get(k) for k in ("rc", "r1a", "r1b", "r2a", "r2b", "rz"))
 
-    def pack_grad(p):
+    def pack_grad(p, acc, col):
         group = YZ * r
         if not sz.inside:
             name, off = targets[p]
             out = m[name] if p in (FI, FO) else m[name].at[:, off : off + D]
-            cp = pltpu.make_async_copy(acc, out, lsem.at[0])
+            cp = pltpu.make_async_copy(acc.at[:, col : col + D], out, lsem.at[0])
             cp.start()
             cp.wait()
             return None
@@ -830,7 +1015,7 @@
                 for y_ in range(Y):
                     at = (y_ * Z + z_) * r if p == FO else (z_ * Y + y_) * r
                     rows = pl.ds(pl.multiple_of(k * group + at, 8), r)
-                    left, right = acc[rows, 0:nh], acc[rows, nh:D]
+                    left, right = acc[rows, col : col + nh], acc[rows, col + nh : col + D]
                     put_halves(gw.at[p, c_, x_, y_, z_], left, right, r, rb)
             return carry
 
@@ -840,13 +1025,11 @@
     def rs_first(p, cps):
         got(cps)
 
-        def body(k, carry):
-            x_ = k // Y
-            y_ = k % Y
-            add_to(gw.at[p, c, x_, y_], rc.at[p, x_, y_])
-            return carry
-
-        lax.fori_loop(0, X * Y, body, 0)
+        add_blocks(
+            X * Y,
+            lambda k, z_: gw.at[p, c, k // Y, k % Y, z_],
+            lambda k, z_: rc.at[p, k // Y, k % Y, z_],
+        )
         if p in X_LAST:
             return [
                 send(gw.at[p, c, xs(b)], r1a.at[X_LAST.index(p), b - 1], dev(x_=xs(b))) for b in range(1, X)
@@ -859,15 +1042,21 @@
         got(cps)
         if p in X_LAST:
             for b in range(1, X):
-                for y_ in range(Y):
-                    add_to(gw.at[p, c, x, y_], r1a.at[X_LAST.index(p), b - 1, y_])
+                add_blocks(
+                    Y,
+                    lambda k, z_: gw.at[p, c, x, k, z_],
+                    lambda k, z_: r1a.at[X_LAST.index(p), b - 1, k, z_],
+                )
             return [
                 send(gw.at[p, c, x, ys(b)], r2a.at[X_LAST.index(p), b - 1], dev(y_=ys(b)))
                 for b in range(1, Y)
             ]
         for b in range(1, Y):
-            for x_ in range(X):
-                add_to(gw.at[p, c, x_, y], r1b.at[Y_LAST.index(p), b - 1, x_])
+            add_blocks(
+                X,
+                lambda k, z_: gw.at[p, c, k, y, z_],
+                lambda k, z_: r1b.at[Y_LAST.index(p), b - 1, k, z_],
+            )
         return [
             send(gw.at[p, c, xs(b), y], r2b.at[Y_LAST.index(p), b - 1], dev(x_=xs(b))) for b in range(1, X)
         ]
@@ -876,10 +1065,18 @@
         got(cps)
         if p in X_LAST:
             for b in range(1, Y):
-                add_to(gw.at[p, c, x, y], r2a.at[X_LAST.index(p), b - 1])
+                add_blocks(
+                    1,
+                    lambda k, z_: gw.at[p, c, x, y, z_],
+                    lambda k, z_: r2a.at[X_LAST.index(p), b - 1, z_],
+                )
         else:
             for b in range(1, X):
-                add_to(gw.at[p, c, x, y], r2b.at[Y_LAST.index(p), b - 1])
+                add_blocks(
+                    1,
+                    lambda k, z_: gw.at[p, c, x, y, z_],
+                    lambda k, z_: r2b.at[Y_LAST.index(p), b - 1, z_],
+                )
         if p == FO:
             return []
         return [
@@ -897,15 +1094,15 @@
         name, off = targets[p]
         if p in (FI, FO):
             for a in range(Z):
-                k = a if p == FO else zs(Z - a)
+                k = a if p == FO else zs((Z - a) % Z)
                 if p == FO:
                     v = gw[p, c, x, y, a]
                 else:
                     v = rz[p, a - 1] if a else gw[p, c, x, y, z]
                 lo, hi = get_halves(v.astype(F32), r)
                 if p == FI:
-                    m["gfi"][k, :, 0:nh] = lo
-                    m["gfi"][k, :, nh:D] = hi
+                    m["kvacc"][pl.ds(pl.multiple_of(k * r, 8), r), 0:nh] = lo
+                    m["kvacc"][pl.ds(pl.multiple_of(k * r, 8), r), nh:D] = hi
                 else:
                     m[name][k * r : k * r + r, 0:nh] = lo
                     m[name][k * r : k * r + r, nh:D] = hi
@@ -913,7 +1110,7 @@
                 for k in range(Z):
                     for i in range(ndp):
                         at = (i * Z + k) * per
-                        m[name][:, at : at + per] = m["gfi"][k, :, i * per : (i + 1) * per]
+                        m[name][:, at : at + per] = m["kvacc"][k * r : k * r + r, i * per : (i + 1) * per]
             return None
         v = gw[p, c, x, y, z].astype(F32)
         for a in range(1, Z):
@@ -926,11 +1123,17 @@
     moving = {}
 
     def grad_of(p, lhs, rhs):
-        acc[...] = tn(lhs, rhs)
+        def part(k, carry):
+            cols = pl.ds(pl.multiple_of(k * WIDE, WIDE), WIDE)
+            left = lhs[:, :, cols].reshape(Z * T, WIDE) if len(lhs.shape) == 3 else lhs[:, cols]
+            acc[cols, :] = tn(left, rhs[...])
+            return carry
+
+        lax.fori_loop(0, NQ, part, 0)
         grad_out(p)
 
-    def grad_out(p):
-        moving[p] = (0, pack_grad(p))
+    def grad_out(p, src=None, col=0):
+        moving[p] = (0, pack_grad(p, acc if src is None else src, col))
 
     def push(p):
         k, cps = moving[p]
@@ -941,11 +1144,13 @@
         for p in ps:
             push(p)
 
-    grad_of(FO, gl[...], gb)
-    grad_of(FI, hb, du[...])
-    got(zh)
+    spare.extend(early[1])
+    grad_of(FO, gl, gb)
+    grad_of(FI, h3, du)
+    push_all([FO, FI])
     sm = m["sm"]
     sm[...] = jnp.zeros_like(sm)
+    got(zh)
     dh3 = rs_total(po.at[0], rzo)
     dv, gg = norm_back(m["x2"][...], gain[2:3, :], dh3)
     sm[2:3, :] = gg
@@ -972,7 +1177,7 @@
     act_start(do_base, [do, dr])
     act_forward(do_base, [do, dr], 0)
     zy = rs_z(py, rzy)
-    grad_of(CO, m["oc"][...], dx2l)
+    grad_of(CO, m["oc"], dx2l)
 
     sent(zh)
     yq_base = rs_y_base()
@@ -980,20 +1185,22 @@
     def row_of(ref, k):
         return jnp.concatenate([ref[2 * k : 2 * k + 1, :], ref[2 * k + 1 : 2 * k + 2, :]], axis=1)
 
-    def attend_back(t, carry):
-        a = t % Z
-        b = t // Z
+    zq_base = take(Z)
+
+    def pass_back(a):
+        zi = zs(a)
+        for b in range(1, Y):
+            rs_y_wait(yq_base, po, ryo, b, a)
+        tot = po[0, zi].astype(F32)
+        for b in range(1, Y):
+            tot = tot + ryo[b - 1, zi].astype(F32)
+        po[0, zi] = tot.astype(BF)
+        z_send(zq_base, po, rzo, a)
+
+    def attend_back(a, b):
         zi = zs(a)
         yi = ys(b)
         qi = zi * Y + yi
-
-        @pl.when(t > 0)
-        def _():
-            act_wait(do_base, [do, dr], t)
-
-        @pl.when((t > 0) & (t < Z))
-        def _():
-            act_forward(do_base, [do, dr], a)
 
         lse_rows = dr[zi, yi, 0:8]
         delta_rows = dr[zi, yi, 8:16]
@@ -1008,166 +1215,189 @@
             kv[qi, :, quad(k)] = nn(ds, qb).astype(BF)
             kv[qi, :, D + k * WIDE : D + (k + 1) * WIDE] = nn(pt.astype(BF), db).astype(BF)
 
+
+    kvacc = m["kvacc"]
+
+    def kv_grad(q):
+        def part(k, carry):
+            cols = pl.ds(pl.multiple_of(k * WIDE, WIDE), WIDE)
+            kvacc[cols, :] += tn(pas[q, :, cols], kv[q])
+            return carry
+
+        lax.fori_loop(0, NQ, part, 0)
+
+    def back_step(t, carry):
+        a = t % Z
+        b = t // Z
+
+        @pl.when(t > 0)
+        def _():
+            act_wait(do_base, [do, dr], t)
+
+        @pl.when((t > 0) & (t < Z))
+        def _():
+            act_forward(do_base, [do, dr], a)
+
+        attend_back(a, b)
+
         @pl.when(t >= Z)
         def _():
             rs_y_send(yq_base, po, ryo, b, a)
 
+        @pl.when(t == 1)
+        def _():
+            push(CO)
+
+        kv_grad(zs(a) * Y + ys(b))
+
         return carry
 
-    lax.fori_loop(0, 2, attend_back, 0)
-    push_all([FO, FI])
-    lax.fori_loop(2, Z, attend_back, 0)
-    push_all([CO])
-    lax.fori_loop(Z, YZ, attend_back, 0)
-
-    def kv_grad(p, off):
-        if R % 16 == 0:
-            acc[...] = tn(pas[...].reshape(YZ * R, D), kv[:, :, off : off + D].reshape(YZ * R, D))
+    kvacc[...] = jnp.zeros_like(kvacc)
+    lax.fori_loop(0, YZ, back_step, 0)
+    def row_grads(k0, k1):
+        def whole(k, carry):
+            pas[k] = (nt(kv[k, :, 0:D], w[CK]) + nt(kv[k, :, D : 2 * D], w[CV])).astype(BF)
+            pltpu.make_async_copy(pas.at[k], m["pg"].at[k], lsem.at[1 + k]).start()
+            return carry
+
+        def part(k, carry):
+            rows = pl.ds(k // NQ * chunk, chunk)
+            cols = pl.ds(pl.multiple_of(k % NQ * WIDE, WIDE), WIDE)
+            v = nt(kv[rows, :, 0:D].reshape(chunk * R, D), w[CK, cols, :])
+            v = v + nt(kv[rows, :, D : 2 * D].reshape(chunk * R, D), w[CV, cols, :])
+            pas[rows, :, cols] = v.astype(BF).reshape(chunk, R, WIDE)
+
+            @pl.when(k % NQ == NQ - 1)
+            def _():
+                for q in range(chunk):
+                    at = k // NQ * chunk + q
+                    pltpu.make_async_copy(pas.at[at], m["pg"].at[at], lsem.at[1 + at]).start()
+
+            return carry
+
+        if chunk == 1:
+            lax.fori_loop(k0, k1, whole, 0)
         else:
-            acc[...] = jnp.zeros_like(acc)
-
-            def body(q, carry):
-                acc[...] += tn(pas[q], kv[q, :, off : off + D])
-                return carry
-
-            lax.fori_loop(0, YZ, body, 0)
-        grad_out(p)
-
-    def row_grads(k0, k1):
-        def body(k, carry):
-            if chunk == 1:
-                pas[k] = (nt(kv[k, :, 0:D], w[CK]) + nt(kv[k, :, D : 2 * D], w[CV])).astype(BF)
-            else:
-                rows = pl.ds(k * chunk, chunk)
-                v = nt(kv[rows, :, 0:D].reshape(chunk * R, D), w[CK])
-                v = v + nt(kv[rows, :, D : 2 * D].reshape(chunk * R, D), w[CV])
-                pas[rows] = v.astype(BF).reshape(chunk, R, D)
-            for q in range(chunk):
-                at = k * chunk + q
-                pltpu.make_async_copy(pas.at[at], m["pg"].at[at], lsem.at[1 + at]).start()
-            return carry
-
-        lax.fori_loop(k0, k1, body, 0)
-
-    kv_grad(CK, 0)
-    zq = []
-    for a in list(range(1, Z)) + [0]:
-        zi = zs(a)
+            lax.fori_loop(k0 * NQ, k1 * NQ, part, 0)
+
+    half = YZ // chunk // 2
+    held = {}
+
+    def take_dq():
         for b in range(1, Y):
-            rs_y_wait(yq_base, po, ryo, b, a)
-        tot = po[0, zi].astype(F32)
+            rs_y_wait(yq_base, po, ryo, b, 0)
+        z_each(zq_base, po, rzo, "recv")
+        dqc = rs_total(po.at[0], rzo)
         for b in range(1, Y):
-            tot = tot + ryo[b - 1, zi].astype(F32)
-        po[0, zi] = tot.astype(BF)
-        if a:
-            zq.append(send(po.at[0, zi], rzo.at[a - 1], dev(z_=zi)))
-    kv_grad(CV, D)
-    push_all([CK, FO, FI])
-    half = YZ // chunk // 2
-    row_grads(0, half)
-    push_all([CV, CO])
-    got(zq)
-    dqc = rs_total(po.at[0], rzo).astype(BF)
-    dh2 = nt(dqc, w[CQ])
-    dv, gg = norm_back(m["x1"][...], gain[1:2, :], dh2)
-    sm[1:2, :] = gg
-    dx1 = m["dx"][...] + dv
-    m["dx"][...] = dx1
-    dx1l = dx1.astype(BF)
-    grad_of(CQ, m["h2"][...], dqc)
-    grad_of(SO, m["os"][...], dx1l)
-    push_all([CQ])
-
-    m["oc"][...] = nt(dx1l, w[SO]).astype(BF)
-    grads = [[], [], []]
-    tail = []
-    for t in range(NQ):
-        db = stack4(m["oc"][:, quad(t)])
-        qb = stack4(m["qs"][:, quad(t)])
-        pr = m["ps"][t]
-        dps = nt(db, m["vs"][:, quad(t)])
-        dss = (pr * (dps - jnp.sum(pr * dps, axis=1, keepdims=True))).astype(BF)
-        grads[0].append(fold4(nn(dss, m["ks"][:, quad(t)])).astype(BF))
-        grads[1].append(tn(dss, qb).astype(BF))
-        grads[2].append(tn(pr.astype(BF), db).astype(BF))
+            dqc = dqc + ryo[b - 1, z].astype(F32)
+        held["dqc"] = dqc.astype(BF)
+        dh2 = nt(held["dqc"], w[CQ])
+        dv, gg = norm_back(m["x1"][...], gain[1:2, :], dh2)
+        sm[1:2, :] = gg
+        dx1 = m["dx"][...] + dv
+        m["dx"][...] = dx1
+        held["dx1l"] = dx1.astype(BF)
+
+    def self_back():
+        m["oc"][...] = nt(held["dx1l"], w[SO]).astype(BF)
+        grads = [[], [], []]
+        held["tail"] = []
         back = (iota((T, 128), 1) == T - 1 - iota((T, 128), 0)).astype(F32).astype(BF)
-        turned = nn(dss, back)
-        for h in range(QUAD):
-            part = pltpu.roll(turned[h * T : (h + 1) * T], 0, 1, stride=1, stride_axis=0)
-            tail.append(jnp.sum(part, axis=0, keepdims=True))
-    dqs, dks, dvs = (jnp.concatenate(g, axis=1) for g in grads)
-    h1 = m["h1"][...]
-    grad_of(SV, h1, dvs)
-    push(SO)
-    grad_of(SQ, h1, dqs)
-    push(SV)
-    grad_of(SK, h1, dks)
-    push(SQ)
-    dh1 = nt(dqs, w[SQ]) + nt(dks, w[SK]) + nt(dvs, w[SV])
-    dv, gg = norm_back(tok[...], gain[0:1, :], dh1)
-    sm[0:1, :] = gg
-    m["tg"][...] = m["dx"][...] + dv
-    flat = HEADS * BUCKETS
-    diag = jnp.concatenate(tail + [jnp.zeros((16 - HEADS, 128), F32)], axis=0)
-    mi, bi = iota((128, 128), 0), iota((128, 128), 1)
-    hot = ((mi >= T - 1) & (bucket_of(mi - (T - 1)) == bi) & (bi < BUCKETS)).astype(F32)
-    table = nn_high(diag, hot)
-    bb, nb = iota((128, flat), 0), iota((128, flat), 1)
-    wide = nn_high(table, ((nb & (BUCKETS - 1)) == bb).astype(F32))
-    h0, n0 = iota((16, flat), 0), iota((16, flat), 1)
-    own = (n0 >= h0 * BUCKETS) & (n0 < h0 * BUCKETS + BUCKETS)
-    sm[3:4, 0:flat] = jnp.sum(jnp.where(own, wide, 0.0), axis=0, keepdims=True)
+        for t in range(NQ):
+            db = stack4(m["oc"][:, quad(t)])
+            qb = stack4(m["qs"][:, quad(t)])
+            pr = m["ps"][t]
+            dps = nt(db, m["vs"][:, quad(t)])
+            dss = (pr * (dps - jnp.sum(pr * dps, axis=1, keepdims=True))).astype(BF)
+            grads[0].append(fold4(nn(dss, m["ks"][:, quad(t)])).astype(BF))
+            grads[1].append(tn(dss, qb).astype(BF))
+            grads[2].append(tn(pr.astype(BF), db).astype(BF))
+            turned = nn(dss, back)
+            for h in range(QUAD):
+                part = pltpu.roll(turned[h * T : (h + 1) * T], 0, 1, stride=1, stride_axis=0)
+                held["tail"].append(jnp.sum(part, axis=0, keepdims=True))
+        held["dqs"], held["dks"], held["dvs"] = (jnp.concatenate(g, axis=1) for g in grads)
+
+    def token_grad():
+        dh1 = nt(held["dqs"], w[SQ]) + nt(held["dks"], w[SK]) + nt(held["dvs"], w[SV])
+        dv, gg = norm_back(tok[...], gain[0:1, :], dh1)
+        sm[0:1, :] = gg
+        m["tg"][...] = m["dx"][...] + dv
+        flat = HEADS * BUCKETS
+        diag = jnp.concatenate(held["tail"] + [jnp.zeros((16 - HEADS, 128), F32)], axis=0)
+        mi, bi = iota((128, 128), 0), iota((128, 128), 1)
+        hot = ((mi >= T - 1) & (bucket_of(mi - (T - 1)) == bi) & (bi < BUCKETS)).astype(F32)
+        table = nn_high(diag, hot)
+        bb, nb = iota((128, flat), 0), iota((128, flat), 1)
+        wide = nn_high(table, ((nb & (BUCKETS - 1)) == bb).astype(F32))
+        h0, n0 = iota((16, flat), 0), iota((16, flat), 1)
+        own = (n0 >= h0 * BUCKETS) & (n0 < h0 * BUCKETS + BUCKETS)
+        sm[3:4, 0:flat] = jnp.sum(jnp.where(own, wide, 0.0), axis=0, keepdims=True)
 
     rsm = m["rsm"]
     slot = [0]
 
-    def small_send(devs):
-        cps = []
+    def small_to(devs):
+        held["small"] = []
         for to in devs:
-            cps.append((slot[0], send(sm, rsm.at[slot[0]], to)))
+            held["small"].append((slot[0], send(sm, rsm.at[slot[0]], to)))
             slot[0] += 1
-        return cps
-
-    def small_end(cps):
-        got([cp for _, cp in cps])
-        sent([cp for _, cp in cps])
-        for k, _ in cps:
+
+    def small_got():
+        got([cp for _, cp in held["small"]])
+        sent([cp for _, cp in held["small"]])
+        for k, _ in held["small"]:
             sm[...] += rsm[k]
 
-    def small_sum(devs):
-        small_end(small_send(devs))
-
-    small_sum([dev(c_=oth)])
-    push(SK)
-    small_x = small_send([dev(x_=xs(b)) for b in range(1, X)])
-    push(CK)
-    push(CV)
-    push_all([FO, FI, CO])
-    row_grads(half, YZ // chunk)
-    push(CQ)
-    push(CK)
-    push(SO)
-    push(CV)
-    push(SV)
-    push_all([FO, FI, CO])
-    small_end(small_x)
-    small_y = small_send([dev(y_=ys(b)) for b in range(1, Y)])
-    got(zy)
-    m["bo"][...] = live * (m["x2"][...] + rs_total(py, rzy))
-    push(SQ)
-    push(CQ)
-    push(SK)
-    push(SO)
-    push_all([CK, CV])
-    small_end(small_y)
-    small_z = small_send([dev(z_=zs(a)) for a in range(1, Z)])
-    push(SV)
-    push(SQ)
-    push(SK)
-    push_all([CQ, SO])
-    small_end(small_z)
-    push_all([SV, SQ, SK])
-    assert all(k == len(stages) for k, _ in moving.values())
+    def small_step(k):
+        if k:
+            small_got()
+        if k < 4:
+            small_to(
+                (
+                    [dev(c_=oth)],
+                    [dev(x_=xs(b)) for b in range(1, X)],
+                    [dev(y_=ys(b)) for b in range(1, Y)],
+                    [dev(z_=zs(a)) for a in range(1, Z)],
+                )[k]
+            )
+
+    def block_out():
+        got(zy)
+        m["bo"][...] = live * (m["x2"][...] + rs_total(py, rzy))
+
+    steps = {
+        "ck": lambda: grad_out(CK, kvacc, 0),
+        "cv": lambda: grad_out(CV, kvacc, D),
+        "pass": lambda: [pass_back(a) for a in range(1, Z)],
+        "rows1": lambda: row_grads(0, half),
+        "rows2": lambda: row_grads(half, YZ // chunk),
+        "dq": take_dq,
+        "cq": lambda: grad_of(CQ, m["h2"], held["dqc"]),
+        "so": lambda: grad_of(SO, m["os"], held["dx1l"]),
+        "selfback": self_back,
+        "sv": lambda: grad_of(SV, m["h1"], held["dvs"]),
+        "sq": lambda: grad_of(SQ, m["h1"], held["dqs"]),
+        "sk": lambda: grad_of(SK, m["h1"], held["dks"]),
+        "dh1": token_grad,
+        "bo": block_out,
+    }
+    pieces = dict(SQ=SQ, SK=SK, SV=SV, SO=SO, CQ=CQ, CK=CK, CV=CV, CO=CO, FI=FI, FO=FO)
+    small_at = [0]
+
+    def run(name):
+        if name == "small":
+            small_step(small_at[0])
+            small_at[0] += 1
+        elif name in pieces:
+            push(pieces[name])
+        else:
+            steps[name]()
+
+    for name in TAIL:
+        run(name)
+    assert all(k == len(stages) for k, _ in moving.values()), moving
+    assert small_at[0] == 5
     me = dp * YZ + fs
     nd, ld = iota((D, 128), 0), iota((D, 128), 1)
     mine = nn_high(sm[...], ((nd == me * r + ld) & (ld < r)).astype(F32))
@@ -1179,6 +1409,7 @@
 
     act_done(do_base, [do, dr])
     rs_y_done(yq_base, po, ryo)
+    z_each(zq_base, po, rzo, "send")
     drain()
 
     def pg_wait(q, carry):
@@ -1190,12 +1421,15 @@
 
 def place_kernel(*refs):
     n = len(OUTPUTS)
-    copies = [
-        pltpu.make_async_copy(refs[k], refs[n + k], refs[2 * n].at[k]) for k in range(n)
-    ]
-    for cp in copies:
+    given, put, held, sem = refs[:n], refs[n : 2 * n], refs[2 * n : 3 * n], refs[3 * n]
+    loads = [pltpu.make_async_copy(given[k], held[k], sem.at[k]) for k in range(n)]
+    stores = [pltpu.make_async_copy(held[k], put[k], sem.at[n + k]) for k in range(n)]
+    for cp in loads:
         cp.start()
-    for cp in copies:
+    for load, store in zip(loads, stores):
+        load.wait()
+        store.start()
+    for cp in stores:
         cp.wait()
 
 
@@ -1260,9 +1494,10 @@
         outs = pl.pallas_call(
             place_kernel,
             out_shape=tuple(shape(o.shape, o.dtype) for o in outs),
-            in_specs=[vm] * len(outs),
+            in_specs=[hbm] * len(outs),
             out_specs=(hbm,) * len(outs),
-            scratch_shapes=(pltpu.SemaphoreType.DMA((len(outs),)),),
+            scratch_shapes=tuple(pltpu.VMEM(o.shape, o.dtype) for o in outs)
+            + (pltpu.SemaphoreType.DMA((2 * len(outs),)),),
             compiler_params=pltpu.CompilerParams(vmem_limit_bytes=63 * 2**20),
         )(*outs)
     (bo, tg, pg, g_ls, g_rb, g_sq, g_skv, g_so, g_lc, g_cq, g_ckv, g_co, g_lf, g_fi, g_fo) = outs

time: 210 us -> 197 us (0.938)
  Pallas kernels: 208 us -> 195 us
    pallas_call x1, Pallas kernels: 204 us -> 190 us  [per_device(): pl.pallas_call(functools.partial(block_kernel, sz, names), out_shape=out_...]
where the time goes in v3:
time: 197 us; the launch traced here: 196 us
  Pallas kernels  195 us (99%)
    pallas_call x1, Pallas kernels, per_device(): pl.pallas_call(functools.partial(block_kernel, sz, names), out_shape=out_...  190 us
    pallas_call x1, Pallas kernels, per_device(): pl.pallas_call(place_kernel, out_shape=tuple((shape(o.shape, o.dtype) for...  4.47 us

profile of v3, /device:TPU:0, one launch (start us, length us, event | category | flops | bytes accessed | tf_op | source)
XLA Modules:
  0.0 196.4 jit_solution(11467489533960743956)
XLA Ops:
  1.3 190.5 %shard_map.271 = (f32[64,768]{1,0:T(8,128)}, f32[64,768]{1,0:T(8,128)}, bf16[8,240,768]{2,1,0:T(8,128)(2,1)}, f32[1,24]{1,0:T(1,128)}, f32[1,12]{1,0:T(1,128)}, ...) custom-call(f32[64,768]{1,0:T(8,128)} %bitcast.12, ...), custom_call_target="tpu_custom_call" | custom-call | flops 20000000000 | bytes 20000000 | tf_op jit(solution)/shard_map/pallas_call | solution.py:1463
  191.8 4.5 %shard_map.272 = (f32[64,768]{1,0:T(8,128)}, f32[64,768]{1,0:T(8,128)}, bf16[8,240,768]{2,1,0:T(8,128)(2,1)}, f32[1,24]{1,0:T(1,128)}, f32[1,12]{1,0:T(1,128)}, ...) custom-call(f32[64,768]{1,0:T(8,128)} %get-tuple-element.45.refs_0_,, ...), custom_call_target="tpu_custom_call" | custom-call | tf_op jit(solution)/shard_map/pallas_call | solution.py:1494

commit v4 on v3

--- a/solution.py
+++ b/solution.py
@@ -20,8 +20,10 @@
 F32 = jnp.float32
 PIECES = 10
 SQ, SK, SV, SO, CQ, CK, CV, CO, FI, FO = range(PIECES)
-X_LAST = (CK, CV, CQ, SO, SQ, SK, CO, FI, FO)
-Y_LAST = (SV,)
+WIDE_PIECES = (CK, CV, FI, FO)
+Y_SUMMED_FIRST = (CK, CV)
+FACTORS = {SQ: "h1", SK: "h1", SV: "h1", SO: "os", CQ: "h2", CO: "oc"}
+ACTS = ("h1", "os", "h2", "oc")
 Y_GATHERED_LAST = (SQ, SV, CQ)
 ZDIM = 4
 
@@ -88,6 +90,10 @@
     half = 0.5 * (1.0 + th)
     slope = half + 0.5 * u * (1.0 - th * th) * cst * (1.0 + 3.0 * cubic * u * u)
     return u * half, slope
+
+
+class Buffers:
+    pass
 
 
 class Spot:
@@ -148,22 +154,24 @@
 
 
 def sems(sz):
-    return 199 if sz.inside else 900
+    return 156 if sz.inside else 900
 
 
 def layout(sz):
     X, Y, Z, D, T, R = sz.X, sz.Y, sz.Z, sz.D, sz.T, sz.R
     rb, nh, hid = sz.rb, sz.nh, sz.hid
-    na, nb = len(X_LAST), len(Y_LAST)
+    nw = len(WIDE_PIECES)
     NQ = HEADS // QUAD
     V = pltpu.VMEM
     sums = dict(
-        rc=V((PIECES, X, Y, Z, rb, nh), BF),
-        r1a=V((na, X - 1, Y, Z, rb, nh), BF),
-        r1b=V((nb, Y - 1, X, Z, rb, nh), BF),
-        r2a=V((na, Y - 1, Z, rb, nh), BF),
-        r2b=V((nb, X - 1, Z, rb, nh), BF),
-        rz=V((PIECES, Z - 1, rb, nh), BF),
+        rc=V((nw, X, Y, Z, rb, nh), BF),
+        r1=V((nw, X - 1, Y, Z, rb, nh), BF),
+        r1y=V((nw, Y - 1, X, Z, rb, nh), BF),
+        r2x=V((nw, X - 1, Z, rb, nh), BF),
+        r2=V((PIECES, Y - 1, Z, rb, nh), BF),
+        rz=V((PIECES, 3, rb, nh), BF),
+        act=V((len(ACTS), X, 2, T, D), BF),
+        cot=V((PIECES, X, 2, T, D), BF),
     )
     return dict(
         **(sums if sz.inside else {}),
@@ -219,65 +227,24 @@
     )
 
 
+(
+    DO_CK, DO_CV, DO_PASS, DO_ROWS1, DO_ROWS2, DO_ROWS3,
+    DO_ROWS4, DO_DQ, DO_CQ, DO_SO, DO_SELFBACK, DO_SV,
+    DO_SQ, DO_SK, DO_DH1, DO_BO, DO_SMALL,
+) = range(PIECES, PIECES + 17)
 TAIL = (
-    "ck",
-    "cv",
-    "CO",
-    "FI",
-    "FO",
-    "pass",
-    "CK",
-    "CV",
-    "rows1",
-    "CO",
-    "dq",
-    "FI",
-    "cq",
-    "so",
-    "CK",
-    "FO",
-    "selfback",
-    "CQ",
-    "FO",
-    "CO",
-    "sv",
-    "SO",
-    "sq",
-    "FI",
-    "sk",
-    "CV",
-    "SV",
-    "CK",
-    "dh1",
-    "small",
-    "SQ",
-    "SK",
-    "rows2",
-    "small",
-    "CQ",
-    "CV",
-    "bo",
-    "CK",
-    "SO",
-    "SV",
-    "CV",
-    "CQ",
-    "SQ",
-    "SO",
-    "CQ",
-    "SQ",
-    "SK",
-    "small",
-    "SO",
-    "SV",
-    "SQ",
-    "SK",
-    "small",
-    "SV",
-    "SK",
-    "small",
+    FO, DO_CK, DO_CV, CO, FO, FO, DO_PASS, CK,
+    CV, DO_ROWS1, FI, CO, DO_DQ, DO_CQ, DO_SO, DO_SELFBACK,
+    DO_SV, DO_SQ, DO_SK, DO_DH1, DO_SMALL, CK, DO_BO, FI,
+    CQ, FI, DO_SMALL, CO, SO, CQ, DO_ROWS2, SV,
+    SO, CV, CO, SQ, SV, SK, CQ, SQ,
+    DO_ROWS3, SK, CK, SO, DO_SMALL, CQ, DO_ROWS4, SV,
+    CV, CK, SQ, SO, CQ, SV, SK, DO_SMALL,
+    CV, CK, SQ, SO, SV, SK, DO_SMALL, CV,
+    SQ, SK,
 )
 
+SPOTS = ("gw", "smb", "fip", "rc", "r1", "r1y", "r2", "r2x", "rz", "act", "cot")
 INPUTS = (
     "tok", "pas_in", "len", "og", "ls", "rel", "sq", "skv", "so",
     "lc", "cq", "ckv", "co", "lf", "fi_in", "fo_in",
@@ -289,13 +256,11 @@
 
 
 def block_kernel(sz, names, *refs):
-    n_in, n_out = len(INPUTS), len(OUTPUTS)
-    m = dict(zip(INPUTS, refs[:n_in]))
-    m.update(zip(OUTPUTS, refs[n_in : n_in + n_out]))
-    m.update(zip(names, refs[n_in + n_out :]))
-    for name in ("gw", "smb", "fip", "rc", "r1a", "r1b", "r2a", "r2b", "rz"):
-        if name in m:
-            m[name] = Spot(m[name])
+    m = Buffers()
+    vars(m).update(zip(INPUTS + OUTPUTS + names, refs))
+    for name in SPOTS:
+        if hasattr(m, name):
+            setattr(m, name, Spot(getattr(m, name)))
     X, Y, Z, D, T, R = sz.X, sz.Y, sz.Z, sz.D, sz.T, sz.R
     r, rb, nh, hid = sz.r, sz.rb, sz.nh, sz.hid
     NQ = HEADS // QUAD
@@ -346,7 +311,12 @@
     for v in ring_z:
         near[(none, none, none, id(v))] = any_dev(z_=v)
 
-    ssem, rsem, lsem = m["ssem"], m["rsem"], m["lsem"]
+    z_near = z + 1 - 2 * (z % 2)
+    z_far = ring_z[2]
+    z_cross = (z_near + 2) % Z
+    near[(none, none, none, id(z_near))] = any_dev(z_=z_near)
+
+    ssem, rsem, lsem = m.ssem, m.rsem, m.lsem
     n_sems = sems(sz)
     used = [0]
     pending = []
@@ -357,6 +327,8 @@
     def take(n=1):
         if n == 1 and spare:
             return spare.pop(0)
+        if n == 0:
+            return 0
         at = used[0]
         used[0] += n
         assert used[0] <= n_sems
@@ -372,8 +344,6 @@
 
     def send(src, dst, to):
         i = take()
-        if early[0]:
-            early[1].append(i)
         cp = Sent(lambda: copy_at(i, src, dst, to))
         cp.make().start()
         pending.append(cp)
@@ -398,11 +368,11 @@
     bar = pltpu.get_barrier_semaphore()
     for p in partners:
         pl.semaphore_signal(bar, inc=1, device_id=p, device_id_type=pl.DeviceIdType.MESH)
-    load_pas = pltpu.make_async_copy(m["pas_in"], m["pas"], lsem.at[0])
+    load_pas = pltpu.make_async_copy(m.pas_in, m.pas, lsem.at[0])
     load_pas.start()
     pl.semaphore_wait(bar, len(partners))
 
-    mask = m["mask"]
+    mask = m.mask
     mask[...] = (iota((WIDE, WIDE), 0) // DK == iota((WIDE, WIDE), 1) // DK).astype(F32).astype(BF)
 
     def stack4(v):
@@ -418,7 +388,7 @@
     def quad(t):
         return slice(t * WIDE, (t + 1) * WIDE)
 
-    cell, lift = m["cell"], m["lift"]
+    cell, lift = m.cell, m.lift
 
     def put_halves(dst, left, right, rows, total):
         if rows % 8 == 0 and 2 * rows == total:
@@ -436,74 +406,110 @@
         cell[0 : v.shape[0], 0 : v.shape[1]] = v
         return cell[0:rows, 0 : v.shape[1]], cell[rows : 2 * rows, 0 : v.shape[1]]
 
-    gw, w, smb = m["gw"], m["w"], m["smb"]
-
-    def line_to(buf, over_y, blocks):
-        out = []
-        for k in blocks:
-            block = buf.at[c, x, y, k]
-            if over_y:
-                out += [send(block, block, dev(y_=ys(b))) for b in range(1, Y)]
+    gw, w, smb = m.gw, m.w, m.smb
+
+    class Gather:
+
+        def __init__(self, buf, y_first, feed="gather", first=False):
+            self.buf, self.y_first, self.feed = buf, y_first, feed
+            self.iz, self.iy, self.ix, self.ic = take(), take(Y - 1), take(X - 1), take()
+            self.far = take() if feed == "gather" else 0
+            if first:
+                early[1].extend([self.iz, self.ic, self.far])
+                early[1].extend(range(self.iy, self.iy + Y - 1))
+                early[1].extend(range(self.ix, self.ix + X - 1))
+            if feed == "exchange":
+                own = buf.at[c, x, y, z]
+                for a in range(1, Z):
+                    copy_at(self.iz, m.fip.at[zs(a)], own, dev(z_=zs(a))).start()
+                some = buf.at[c, x, y, 0 : Z - 1]
+                pending.append(Sent(lambda: copy_at(self.iz, some, some, dev(z_=z_near))))
+
+        def z_out(self):
+            own = self.buf.at[c, x, y, z]
+            copy_at(self.far, own, own, dev(z_=z_far)).start()
+            copy_at(self.iz, own, own, dev(z_=z_near)).start()
+
+        def pair_out(self):
+            block = self.buf.at[c, x, y, z_far]
+            far = Sent(lambda: copy_at(self.far, block, block, dev(z_=z_far)))
+            far.wait_recv()
+            copy_at(self.iz, block, block, dev(z_=z_near)).start()
+            pair = self.buf.at[c, x, y, 0:2]
+            pending.extend([far, Sent(lambda: copy_at(self.iz, pair, pair, dev(z_=z_near)))])
+            self.over(self.y_first, block)
+            self.over(not self.y_first, block)
+
+        def over(self, is_y, block):
+            if is_y:
+                for b in range(1, Y):
+                    copy_at(self.iy + b - 1, block, block, dev(y_=ys(b))).start()
             else:
-                out += [send(block, block, dev(x_=xs(b))) for b in range(1, X)]
-        return out
-
-    class Gather:
-        def __init__(self, buf, y_first, feed="gather", first=False):
-            self.first = first
-            early[0] = first
-            self.buf, self.y_first, self.feed = buf, y_first, feed
-            own = buf.at[c, x, y, z]
-            self.z = []
-            for a in range(1, Z):
-                if feed == "gather":
-                    self.z.append(send(own, own, dev(z_=zs(a))))
-                elif feed == "exchange":
-                    self.z.append(send(m["fip"].at[zs(a)], own, dev(z_=zs(a))))
-            early[0] = False
+                for b in range(1, X):
+                    copy_at(self.ix + b - 1, block, block, dev(x_=xs(b))).start()
 
         def own_out(self):
-            early[0] = self.first
-            blocks = range(Z) if self.feed == "local" else [z]
-            self.second = line_to(self.buf, self.y_first, blocks)
-            self.third = line_to(self.buf, not self.y_first, blocks)
-            early[0] = False
+            at = (c, x, y) if self.feed == "local" else (c, x, y, z)
+            self.over(self.y_first, self.buf.at[at])
+            self.over(not self.y_first, self.buf.at[at])
 
         def line_out(self):
-            early[0] = self.first
-            got(self.z)
-            if self.feed != "local":
-                blocks = [zs((Z - a) % Z) for a in range(1, Z)]
-                self.second += line_to(self.buf, self.y_first, blocks)
-                self.third += line_to(self.buf, not self.y_first, blocks)
-            early[0] = False
+            if self.feed == "local":
+                return
+            if self.feed == "gather":
+                some = self.buf.at[c, x, y, 0:2]
+                blocks = (z_near, z_cross)
+            else:
+                some = self.buf.at[c, x, y, 0 : Z - 1]
+                blocks = ring_z[1:]
+            copy_at(self.iz, some, some, dev(z_=z_near)).wait_recv()
+            for k in blocks:
+                block = self.buf.at[c, x, y, k]
+                self.over(self.y_first, block)
+                self.over(not self.y_first, block)
+
+        def arrived(self, is_y, all_of_it):
+            buf = self.buf
+            if is_y:
+                ref = buf.at[c, 0 : X, y] if all_of_it else buf.at[c, x, y]
+                for b in range(1, Y):
+                    yield Sent(
+                        lambda b=b: copy_at(self.iy + b - 1, ref, ref, dev(y_=ys(b)))
+                    )
+            else:
+                ref = buf.at[c, x] if all_of_it else buf.at[c, x, y]
+                for b in range(1, X):
+                    yield Sent(
+                        lambda b=b: copy_at(self.ix + b - 1, ref, ref, dev(x_=xs(b)))
+                    )
 
         def plane_out(self):
-            early[0] = self.first
-            got(self.second)
-            buf = self.buf
+            second = list(self.arrived(self.y_first, False))
+            got(second)
+            pending.extend(second)
             if self.y_first:
                 for b in range(1, Y):
-                    line = buf.at[c, x, ys(b)]
-                    self.third += [send(line, line, dev(x_=xs(d))) for d in range(1, X)]
+                    self.over(False, self.buf.at[c, x, ys(b)])
             else:
                 for b in range(1, X):
-                    line = buf.at[c, xs(b), y]
-                    self.third += [send(line, line, dev(y_=ys(d))) for d in range(1, Y)]
-            early[0] = False
+                    self.over(True, self.buf.at[c, xs(b), y])
 
         def core_out(self):
-            early[0] = self.first
-            got(self.third)
-            self.core = [send(self.buf.at[c], self.buf.at[c], dev(c_=oth))]
-            early[0] = False
+            third = list(self.arrived(not self.y_first, True))
+            got(third)
+            pending.extend(third)
+            plane = self.buf.at[c]
+            self.core = [Sent(lambda: copy_at(self.ic, plane, plane, dev(c_=oth)))]
+            self.core[0].make().start()
+            pending.extend(self.core)
+            self.last = third + self.core
 
         def end(self):
             got(self.core)
 
     own_small = [jnp.zeros((16, 128), F32)]
     for at, key in enumerate(("ls", "lc", "lf", "rel")):
-        v = m[key][...].astype(F32)
+        v = getattr(m, key)[...].astype(F32)
         v = jnp.concatenate([v, jnp.zeros((1, 128 - v.shape[1]), F32)], axis=1)
         own_small[0] = jnp.where(iota((16, 128), 0) == at, v, own_small[0])
     smb[c, x, y, z] = own_small[0].astype(BF)
@@ -513,10 +519,11 @@
         moves[p] = Gather(gw.at[p], p not in Y_GATHERED_LAST, feed, p < CO)
 
     moves["small"] = Gather(smb, True, first=True)
+    moves["small"].z_out()
     moves["small"].own_out()
     sources = (
-        (m["sq"], 0), (m["skv"], 0), (m["skv"], D), (m["so"], 0),
-        (m["cq"], 0), (m["ckv"], 0), (m["ckv"], D), (m["co"], 0),
+        (m.sq, 0), (m.skv, 0), (m.skv, D), (m.so, 0),
+        (m.cq, 0), (m.ckv, 0), (m.ckv, D), (m.co, 0),
     )
 
     def pack(p):
@@ -524,14 +531,16 @@
         v = ref[:, off : off + D].astype(F32)
         put_halves(gw.at[p, c, x, y, z], v[:, 0:nh], v[:, nh:D], r, rb)
         begin(p)
+        if p in (SQ, SK, SV):
+            moves[p].z_out()
         moves[p].own_out()
 
     for p in (SQ, SK, SV, SO, CQ, CK, CV, CO):
         pack(p)
 
-    g3 = m["g3"]
-    live = (iota((T, 1), 0) < m["len"][0]).astype(F32)
-    g3[z] = (live * m["og"][...]).astype(BF)
+    g3 = m.g3
+    live = (iota((T, 1), 0) < m.len[...]).astype(F32)
+    g3[z] = (live * m.og[...]).astype(BF)
 
     def line_start(base, buf):
         for a in range(1, Z):
@@ -568,18 +577,18 @@
             for t in range(1, YZ):
                 copy_at(base + n * YZ + t, buf.at[z, y], buf.at[z, y], dev(z_=zs(1))).wait_send()
 
-    fip = m["fip"]
+    fip = m.fip
     ndp = 2 * X
     per = D // ndp
 
     def pack_ff():
-        even = m["even"]
+        even = m.even
         for k in range(Z):
             for i in range(ndp):
                 at = (i * Z + k) * per
-                even[:, i * per : (i + 1) * per] = m["fi_in"][:, at : at + per].astype(F32)
+                even[:, i * per : (i + 1) * per] = m.fi_in[:, at : at + per].astype(F32)
             put_halves(fip.at[k], even[:, 0:nh], even[:, nh:D], r, rb)
-        vo = m["fo_in"][...].astype(F32)
+        vo = m.fo_in[...].astype(F32)
         if r % 8:
             lift[0 : Z * r, :] = vo
         for k in range(Z):
@@ -589,11 +598,11 @@
 
     g3_base = take(Z)
 
-    spread = m["spread"]
+    spread = m.spread
     lane = iota((16, D), 1)
     row = iota((16, D), 0)
     spread[...] = ((lane >= row * DK) & (lane < row * DK + DK)).astype(F32)
-    m["spread2"][...] = jnp.concatenate([spread[...], spread[...]], axis=0).astype(BF)
+    m.spread2[...] = jnp.concatenate([spread[...], spread[...]], axis=0).astype(BF)
     tlane = iota((T, 128), 1)
     rbs = HEADS * BUCKETS // (2 * X * YZ)
 
@@ -605,8 +614,8 @@
 
         return lax.fori_loop(0, width // step, body, jnp.zeros((128, width), F32)).astype(BF)
 
-    m["hot_gain"][...] = repeat_of(D, r)
-    m["hot_bias"][...] = repeat_of(HEADS * BUCKETS, rbs)
+    m.hot_gain[...] = repeat_of(D, r)
+    m.hot_bias[...] = repeat_of(HEADS * BUCKETS, rbs)
 
     def unpack(p):
         group = 2 * Y * r
@@ -643,12 +652,12 @@
 
         lax.fori_loop(0, X * 2 * per, body, 0)
 
-    gain = m["gain"]
-    bias = m["bias"]
+    gain = m.gain
+    bias = m.bias
     def read_small():
         flat = HEADS * BUCKETS
         every = smb[...].reshape(2 * X * YZ * 16, 128)
-        wide_g, wide_b = nn(every, m["hot_gain"][...]), nn(every, m["hot_bias"][...])
+        wide_g, wide_b = nn(every, m.hot_gain[...]), nn(every, m.hot_bias[...])
         ng, nb = iota((16, D), 1), iota((16, flat), 1)
         gains, tot = jnp.zeros((16, D), F32), jnp.zeros((16, flat), F32)
         at = 0
@@ -675,54 +684,58 @@
             rolled = pltpu.roll(wide, 0, 1, stride=1, stride_axis=0)
             bias[h // QUAD, (h % QUAD) * T : (h % QUAD + 1) * T, :] = rolled[:, 0:T]
 
-    tok = m["tok"]
+    tok = m.tok
 
     def self_forward():
-        m["h1"][...] = normed(tok[...], gain[0:1, :]).astype(BF)
-        h1 = m["h1"][...]
-        m["qs"][...] = nn(h1, w[SQ]).astype(BF)
-        m["ks"][...] = nn(h1, w[SK]).astype(BF)
-        m["vs"][...] = nn(h1, w[SV]).astype(BF)
+        m.h1[...] = normed(tok[...], gain[0:1, :]).astype(BF)
+        h1 = m.h1[...]
+        m.qs[...] = nn(h1, w[SQ]).astype(BF)
+        m.ks[...] = nn(h1, w[SK]).astype(BF)
+        m.vs[...] = nn(h1, w[SV]).astype(BF)
         allowed = iota((WIDE, T), 1) <= (iota((WIDE, T), 0) & (T - 1))
         for t in range(NQ):
-            s = nt(stack4(m["qs"][:, quad(t)]), m["ks"][:, quad(t)]) + bias[t]
+            s = nt(stack4(m.qs[:, quad(t)]), m.ks[:, quad(t)]) + bias[t]
             s = jnp.where(allowed, s, NEG)
             e = jnp.exp(s - jnp.max(s, axis=1, keepdims=True))
             pr = e / jnp.sum(e, axis=1, keepdims=True)
-            m["ps"][t] = pr
-            m["os"][:, quad(t)] = fold4(nn(pr.astype(BF), m["vs"][:, quad(t)])).astype(BF)
-
-    qc = m["qc"]
+            m.ps[t] = pr
+            m.os[:, quad(t)] = fold4(nn(pr.astype(BF), m.vs[:, quad(t)])).astype(BF)
+
+    qc = m.qc
     qc_base = take(YZ)
 
     def self_out():
-        x1 = tok[...] + nn(m["os"][...], w[SO])
-        m["x1"][...] = x1
-        m["h2"][...] = normed(x1, gain[1:2, :]).astype(BF)
+        x1 = tok[...] + nn(m.os[...], w[SO])
+        m.x1[...] = x1
+        m.h2[...] = normed(x1, gain[1:2, :]).astype(BF)
 
     def cross_query():
-        qc[z, y] = nn(m["h2"][...], w[CQ]).astype(BF)
+        qc[z, y] = nn(m.h2[...], w[CQ]).astype(BF)
         act_start(qc_base, [qc])
         act_forward(qc_base, [qc], 0)
 
-    kv, pas = m["kv"], m["pas"]
-
-    chunk = 4 if R % 16 == 0 else 1
-
-    def project(p, off):
+    kv, pas = m.kv, m.pas
+
+    chunk = 2 if R % 16 == 0 else 1
+
+    tall = 4 if R % 16 == 0 else 1
+
+    def project(p, off, k0, k1):
         def part(k, carry):
-            rows = pl.ds(k // NQ * chunk, chunk)
+            rows = pl.ds(k // NQ * tall, tall)
             at = k % NQ * WIDE
             cols = pl.ds(pl.multiple_of(at, WIDE), WIDE)
-            v = nn(pas[rows].reshape(chunk * R, D), w[p, :, cols])
+            v = nn(pas[rows].reshape(tall * R, D), w[p, :, cols])
             cols = pl.ds(pl.multiple_of(off + at, WIDE), WIDE)
-            kv[rows, :, cols] = v.astype(BF).reshape(chunk, R, WIDE)
+            kv[rows, :, cols] = v.astype(BF).reshape(tall, R, WIDE)
             return carry
 
-        lax.fori_loop(0, YZ // chunk * NQ, part, 0)
+        lax.fori_loop(k0 * NQ, k1 * NQ, part, 0)
 
     def project_one(q, p, off):
         kv[q, :, off : off + D] = nn(pas[q], w[p]).astype(BF)
+
+    held = Buffers()
 
     def after(p):
         unpack(p)
@@ -737,7 +750,7 @@
             cross_query()
         elif p == CK:
             load_pas.wait()
-            project(CK, 0)
+            project(CK, 0, 0, YZ // tall // 2)
 
     order = (SQ, SK, SV, SO, CQ, CK, CV, CO, FI, FO)
 
@@ -746,6 +759,13 @@
             moves["small"].line_out()
         moves[order[k]].line_out()
 
+    def pair_out(k):
+        if k == 0:
+            moves["small"].pair_out()
+        moves[order[k]].pair_out()
+        if k + 3 < 8:
+            moves[order[k + 3]].z_out()
+
     def plane_out(k):
         if k == 0:
             moves["small"].plane_out()
@@ -764,32 +784,40 @@
         act_wait(qc_base, [qc], a)
         act_forward(qc_base, [qc], a)
 
+    pair_out(0)
+    pair_out(1)
     line_out(0)
+    pack_ff()
+    pair_out(2)
     line_out(1)
-    pack_ff()
-    begin(FI, "exchange")
     plane_out(0)
+    pair_out(3)
     line_out(2)
     plane_out(1)
+    core_out(0)
+    pair_out(4)
     line_out(3)
-    core_out(0)
+    begin(FI, "exchange")
     plane_out(2)
     arrive(0)
+    core_out(1)
+    pair_out(5)
     line_out(4)
-    core_out(1)
     plane_out(3)
     arrive(1)
+    core_out(2)
+    pair_out(6)
     line_out(5)
-    core_out(2)
+    line_start(g3_base, g3)
     plane_out(4)
     arrive(2)
+    core_out(3)
     line_out(6)
-    core_out(3)
     plane_out(5)
+    pair_out(7)
     arrive(3)
     core_out(4)
     arrive(4)
-    line_start(g3_base, g3)
     plane_out(6)
     core_out(5)
     line_out(7)
@@ -799,14 +827,15 @@
     line_out(8)
     line_out(9)
     arrive(5)
+    core_out(6)
     query_out(1)
-    core_out(6)
+    project(CK, 0, YZ // tall // 2, YZ // tall)
+    arrive(6)
     query_out(2)
-    arrive(6)
     plane_out(7)
     query_out(3)
 
-    po, pst, ryo, ryst, rzo, rzst = (m[k] for k in ("po", "pst", "ryo", "ryst", "rzo", "rzst"))
+    po, pst, ryo, ryst, rzo, rzst = m.po, m.pst, m.ryo, m.ryst, m.rzo, m.rzst
 
     def rs_y_base():
         return take((Y - 1) * Z)
@@ -855,7 +884,7 @@
         hi = v.astype(BF)
         lo = (v - hi.astype(F32)).astype(BF)
         both = jnp.concatenate([hi, lo], axis=0)
-        ones = m["spread2"][...]
+        ones = m.spread2[...]
         return tn(both, ones)
 
     def merge(parts):
@@ -896,39 +925,37 @@
         z_send(zo_base, po, rzo, a)
         z_send(zst_base, pst, rzst, a)
 
-    def attend_step(t, carry):
-        a = (1 + t % Z) % Z
-        b = (1 + t // Z) % Y
-
-        project_one(zs(a) * Y + ys(b), CV, D)
-
-        @pl.when(b > 0)
-        def _():
+    def attend_own(a):
+        project_one(zs(a) * Y + y, CV, D)
+        attend(a, 0)
+
+    def attend_others(a):
+        def body(b, carry):
+            project_one(zs(a) * Y + ys(b), CV, D)
             act_wait(qc_base, [qc], b * Z + a)
-
-        attend(a, b)
-
-        @pl.when(b > 0)
-        def _():
+            attend(a, b)
             rs_y_send(yo_base, po, ryo, b, a)
             rs_y_send(yst_base, pst, ryst, b, a)
-
-        @pl.when((b == 0) & (a > 0))
-        def _():
-            pass_on(a)
-
-        @pl.when(t == YZ - Z - 1)
+            return carry
+
+        lax.fori_loop(1, Y, body, 0)
+
+    def attend_step(k, carry):
+        attend_others((k + 1) % Z)
+        attend_own(k)
+        pass_on(k)
+
+        @pl.when(k == 2)
         def _():
             core_out(7)
 
-        @pl.when(t == 1)
-        def _():
-            plane_out(8)
-            plane_out(9)
-
         return carry
 
-    lax.fori_loop(0, YZ, attend_step, 0)
+    attend_own(0)
+    attend_others(1)
+    plane_out(8)
+    plane_out(9)
+    lax.fori_loop(1, Z, attend_step, 0)
     arrive(7)
     for b in range(1, Y):
         rs_y_wait(yo_base, po, ryo, b, 0)
@@ -940,14 +967,47 @@
         + [(ryo[b - 1, z], ryst[b - 1, z]) for b in range(1, Y)]
         + [(rzo[a - 1], rzst[a - 1]) for a in range(1, Z)]
     )
-    m["oc"][...] = o.astype(BF)
-    m["lse"][...] = lse
-    x2 = m["x1"][...] + nn(m["oc"][...], w[CO])
-    m["x2"][...] = x2
-    h3 = m["h3"]
+    m.oc[...] = o.astype(BF)
+    m.lse[...] = lse
+    x2 = m.x1[...] + nn(m.oc[...], w[CO])
+    m.x2[...] = x2
+    h3 = m.h3
     h3[z] = normed(x2, gain[2:3, :]).astype(BF)
     h3_base = take(Z)
     line_start(h3_base, h3)
+
+    rc, r1, r1y, r2, r2x, rz, act, cot = (getattr(m, k, None) for k in SPOTS[3:])
+
+    def share(buf):
+        own = buf.at[x, c]
+        near_c = send(own, own, dev(c_=oth))
+        return [send(own, own, dev(x_=xs(b))) for b in range(1, X)], near_c
+
+    def share_on(buf, cps):
+        far, near_c = cps
+        got(far)
+        out = [near_c]
+        for b in range(1, X):
+            block = buf.at[xs(b), c]
+            out.append(send(block, block, dev(c_=oth)))
+        return out
+
+    def share_acts():
+        if sz.inside:
+            for n, name in enumerate(ACTS):
+                act[n, x, c] = getattr(m, name)[...]
+            held.acts = [share(act.at[n]) for n in range(len(ACTS))]
+
+    def share_acts_on():
+        if sz.inside:
+            held.acts = [share_on(act.at[n], cps) for n, cps in enumerate(held.acts)]
+
+    def share_acts_end():
+        if sz.inside:
+            for cps in held.acts:
+                got(cps)
+    drain()
+    share_acts()
 
     core_out(8)
     core_out(9)
@@ -955,19 +1015,18 @@
     line_wait(g3_base, g3)
     arrive(9)
     gb = g3[...].reshape(Z * T, D)
-    m["kvacc"].at[0 : Z * T, 0:hid][...] = nt(gb, w[FO])
+    m.kvacc.at[0 : Z * T, 0:hid][...] = nt(gb, w[FO])
     act_done(qc_base, [qc])
     rs_y_done(yo_base, po, ryo)
     rs_y_done(yst_base, pst, ryst)
     z_each(zo_base, po, rzo, "send")
     z_each(zst_base, pst, rzst, "send")
-    drain()
-    py, rzy = m["py"], m["rzy"]
-    gl, du = m["gl"], m["du"]
+    py, rzy = Spot(m.py), Spot(m.rzy)
+    gl, du = m.gl, m.du
     line_wait(h3_base, h3)
-    act, slope = gelu_pair(nn(h3[...].reshape(Z * T, D), w[FI]))
-    du[...] = (m["kvacc"].at[0 : Z * T, 0:hid][...] * slope).astype(BF)
-    gl[...] = act.astype(BF)
+    lifted, slope = gelu_pair(nn(h3[...].reshape(Z * T, D), w[FI]))
+    du[...] = (m.kvacc.at[0 : Z * T, 0:hid][...] * slope).astype(BF)
+    gl[...] = lifted.astype(BF)
     po[0] = nt(du[...], w[FI]).astype(BF).reshape(Z, T, D)
 
     def rs_z(part, rzb):
@@ -984,7 +1043,7 @@
     line_done(h3_base, h3)
     line_done(g3_base, g3)
 
-    acc = m["kvacc"].at[:, 0:D]
+    acc = m.kvacc.at[:, 0:D]
 
     def add_to(dst, src):
         dst[...] = (dst[...].astype(F32) + src[...].astype(F32)).astype(BF)
@@ -996,13 +1055,11 @@
 
         lax.fori_loop(0, rows * Z, body, 0)
 
-    rc, r1a, r1b, r2a, r2b, rz = (m.get(k) for k in ("rc", "r1a", "r1b", "r2a", "r2b", "rz"))
-
     def pack_grad(p, acc, col):
         group = YZ * r
         if not sz.inside:
             name, off = targets[p]
-            out = m[name] if p in (FI, FO) else m[name].at[:, off : off + D]
+            out = getattr(m, name) if p in (FI, FO) else getattr(m, name).at[:, off : off + D]
             cp = pltpu.make_async_copy(acc.at[:, col : col + D], out, lsem.at[0])
             cp.start()
             cp.wait()
@@ -1020,68 +1077,95 @@
             return carry
 
         lax.fori_loop(0, 2 * X, body, 0)
-        return [send(gw.at[p, oth], rc.at[p], dev(c_=oth))]
+        return [send(gw.at[p, oth], rc.at[WIDE_PIECES.index(p)], dev(c_=oth))]
 
     def rs_first(p, cps):
         got(cps)
-
+        n = WIDE_PIECES.index(p)
         add_blocks(
             X * Y,
             lambda k, z_: gw.at[p, c, k // Y, k % Y, z_],
-            lambda k, z_: rc.at[p, k // Y, k % Y, z_],
+            lambda k, z_: rc.at[n, k // Y, k % Y, z_],
         )
-        if p in X_LAST:
+        if p in Y_SUMMED_FIRST:
             return [
-                send(gw.at[p, c, xs(b)], r1a.at[X_LAST.index(p), b - 1], dev(x_=xs(b))) for b in range(1, X)
+                send(gw.at[p, c, :, ys(b)], r1y.at[n, b - 1], dev(y_=ys(b))) for b in range(1, Y)
+            ]
+        return [send(gw.at[p, c, xs(b)], r1.at[n, b - 1], dev(x_=xs(b))) for b in range(1, X)]
+
+    def to_y(p):
+        return [send(gw.at[p, c, x, ys(b)], r2.at[p, b - 1], dev(y_=ys(b))) for b in range(1, Y)]
+
+    def rs_second(p, cps):
+        got(cps)
+        n = WIDE_PIECES.index(p)
+        if p in Y_SUMMED_FIRST:
+            for b in range(1, Y):
+                add_blocks(
+                    X,
+                    lambda k, z_: gw.at[p, c, k, y, z_],
+                    lambda k, z_: r1y.at[n, b - 1, k, z_],
+                )
+            return [
+                send(gw.at[p, c, xs(b), y], r2x.at[n, b - 1], dev(x_=xs(b))) for b in range(1, X)
+            ]
+        for b in range(1, X):
+            add_blocks(
+                Y,
+                lambda k, z_: gw.at[p, c, x, k, z_],
+                lambda k, z_: r1.at[n, b - 1, k, z_],
+            )
+        return to_y(p)
+
+    def factor_on(p, cps):
+        return share_on(cot.at[p], cps)
+
+    def factor_product(p, cps):
+        got(cps)
+        group = YZ * r
+        first = (x * 2 + c) * group
+        lanes = first // 128 * 128
+        shift = pl.multiple_of(first - lanes, 8)
+        lhs = act[ACTS.index(FACTORS[p]), :, :, :, pl.ds(pl.multiple_of(lanes, 128), WIDE)]
+        acc[0:WIDE, :] = tn(lhs.reshape(2 * X * T, WIDE), cot[p].reshape(2 * X * T, D))
+
+        def body(i, carry):
+            y_ = i % Y
+            z_ = i // Y
+            rows = pl.ds(pl.multiple_of(shift + i * r, 8), r)
+            put_halves(gw.at[p, c, x, y_, z_], acc[rows, 0:nh], acc[rows, nh:D], r, rb)
+            return carry
+
+        lax.fori_loop(0, YZ, body, 0)
+        return to_y(p)
+
+    def rs_third(p, cps):
+        got(cps)
+        second = (
+            [r2x.at[WIDE_PIECES.index(p), b - 1] for b in range(1, X)]
+            if p in Y_SUMMED_FIRST
+            else [r2.at[p, b - 1] for b in range(1, Y)]
+        )
+        for part in second:
+            add_blocks(1, lambda k, z_: gw.at[p, c, x, y, z_], lambda k, z_: part.at[z_])
+        if p == FO:
+            return []
+        if p == FI:
+            return [
+                send(gw.at[p, c, x, y, zs(a)], rz.at[p, a - 1], dev(z_=zs(a)))
+                for a in range(1, Z)
             ]
         return [
-            send(gw.at[p, c, :, ys(b)], r1b.at[Y_LAST.index(p), b - 1], dev(y_=ys(b))) for b in range(1, Y)
+            send(gw.at[p, c, x, y, k], rz.at[p, n], dev(z_=z_near))
+            for n, k in enumerate((z_near, z_cross))
         ]
 
-    def rs_second(p, cps):
+    def rs_fourth(p, cps):
         got(cps)
-        if p in X_LAST:
-            for b in range(1, X):
-                add_blocks(
-                    Y,
-                    lambda k, z_: gw.at[p, c, x, k, z_],
-                    lambda k, z_: r1a.at[X_LAST.index(p), b - 1, k, z_],
-                )
-            return [
-                send(gw.at[p, c, x, ys(b)], r2a.at[X_LAST.index(p), b - 1], dev(y_=ys(b)))
-                for b in range(1, Y)
-            ]
-        for b in range(1, Y):
-            add_blocks(
-                X,
-                lambda k, z_: gw.at[p, c, k, y, z_],
-                lambda k, z_: r1b.at[Y_LAST.index(p), b - 1, k, z_],
-            )
-        return [
-            send(gw.at[p, c, xs(b), y], r2b.at[Y_LAST.index(p), b - 1], dev(x_=xs(b))) for b in range(1, X)
-        ]
-
-    def rs_third(p, cps):
-        got(cps)
-        if p in X_LAST:
-            for b in range(1, Y):
-                add_blocks(
-                    1,
-                    lambda k, z_: gw.at[p, c, x, y, z_],
-                    lambda k, z_: r2a.at[X_LAST.index(p), b - 1, z_],
-                )
-        else:
-            for b in range(1, X):
-                add_blocks(
-                    1,
-                    lambda k, z_: gw.at[p, c, x, y, z_],
-                    lambda k, z_: r2b.at[Y_LAST.index(p), b - 1, z_],
-                )
-        if p == FO:
+        if p in (FI, FO):
             return []
-        return [
-            send(gw.at[p, c, x, y, zs(a)], rz.at[p, a - 1], dev(z_=zs(a))) for a in range(1, Z)
-        ]
+        add_to(gw.at[p, c, x, y, z_far], rz.at[p, 1])
+        return [send(gw.at[p, c, x, y, z_far], rz.at[p, 2], dev(z_=z_far))]
 
     targets = {
         SQ: ("g_sq", 0), SK: ("g_skv", 0), SV: ("g_skv", D), SO: ("g_so", 0),
@@ -1101,28 +1185,36 @@
                     v = rz[p, a - 1] if a else gw[p, c, x, y, z]
                 lo, hi = get_halves(v.astype(F32), r)
                 if p == FI:
-                    m["kvacc"][pl.ds(pl.multiple_of(k * r, 8), r), 0:nh] = lo
-                    m["kvacc"][pl.ds(pl.multiple_of(k * r, 8), r), nh:D] = hi
+                    m.kvacc[pl.ds(pl.multiple_of(k * r, 8), r), 0:nh] = lo
+                    m.kvacc[pl.ds(pl.multiple_of(k * r, 8), r), nh:D] = hi
                 else:
-                    m[name][k * r : k * r + r, 0:nh] = lo
-                    m[name][k * r : k * r + r, nh:D] = hi
+                    getattr(m, name)[k * r : k * r + r, 0:nh] = lo
+                    getattr(m, name)[k * r : k * r + r, nh:D] = hi
             if p == FI:
                 for k in range(Z):
                     for i in range(ndp):
                         at = (i * Z + k) * per
-                        m[name][:, at : at + per] = m["kvacc"][k * r : k * r + r, i * per : (i + 1) * per]
+                        getattr(m, name)[:, at : at + per] = m.kvacc[k * r : k * r + r, i * per : (i + 1) * per]
             return None
-        v = gw[p, c, x, y, z].astype(F32)
-        for a in range(1, Z):
-            v = v + rz[p, a - 1].astype(F32)
+        v = gw[p, c, x, y, z].astype(F32) + rz[p, 0].astype(F32) + rz[p, 2].astype(F32)
         lo, hi = get_halves(v, r)
-        m[name][:, off : off + nh] = lo
-        m[name][:, off + nh : off + D] = hi
-
-    stages = (rs_first, rs_second, rs_third, rs_last) if sz.inside else ()
+        getattr(m, name)[:, off : off + nh] = lo
+        getattr(m, name)[:, off + nh : off + D] = hi
+
+    wide_stages = (rs_first, rs_second, rs_third, rs_fourth, rs_last) if sz.inside else ()
+    factor_stages = (factor_on, factor_product, rs_third, rs_fourth, rs_last) if sz.inside else ()
+
+    def stages_of(p):
+        return factor_stages if p in FACTORS else wide_stages
+
     moving = {}
 
     def grad_of(p, lhs, rhs):
+        if sz.inside and p in FACTORS:
+            cot[p, x, c] = rhs[...]
+            moving[p] = (0, share(cot.at[p]))
+            return
+
         def part(k, carry):
             cols = pl.ds(pl.multiple_of(k * WIDE, WIDE), WIDE)
             left = lhs[:, :, cols].reshape(Z * T, WIDE) if len(lhs.shape) == 3 else lhs[:, cols]
@@ -1137,28 +1229,30 @@
 
     def push(p):
         k, cps = moving[p]
-        if k < len(stages):
-            moving[p] = (k + 1, stages[k](p, cps))
+        if k < len(stages_of(p)):
+            moving[p] = (k + 1, stages_of(p)[k](p, cps))
 
     def push_all(ps):
         for p in ps:
             push(p)
 
+    sent(moves[FI].last + moves[FO].last)
     spare.extend(early[1])
     grad_of(FO, gl, gb)
     grad_of(FI, h3, du)
     push_all([FO, FI])
-    sm = m["sm"]
+    share_acts_on()
+    sm = m.sm
     sm[...] = jnp.zeros_like(sm)
     got(zh)
     dh3 = rs_total(po.at[0], rzo)
-    dv, gg = norm_back(m["x2"][...], gain[2:3, :], dh3)
+    dv, gg = norm_back(m.x2[...], gain[2:3, :], dh3)
     sm[2:3, :] = gg
-    dx2 = live * m["og"][...] + dv
-    m["dx"][...] = dx2
+    dx2 = live * m.og[...] + dv
+    m.dx[...] = dx2
     dx2l = dx2.astype(BF)
     doc = nt(dx2l, w[CO]).astype(BF)
-    do, dr = m["do"], m["dr"]
+    do, dr = m.do, m.dr
     do[z, y] = doc
     pick = iota((T, D), 0) == (iota((T, D), 1) & (T - 1))
 
@@ -1167,17 +1261,16 @@
         parts = [v[:, k * 128 : (k + 1) * 128] for k in range(D // 128)]
         return jnp.concatenate(parts + [jnp.zeros((8 - D // 128, 128), F32)], axis=0)
 
-    prod = doc.astype(F32) * m["oc"][...].astype(F32)
+    prod = doc.astype(F32) * m.oc[...].astype(F32)
     delta = lax.dot_general(
         spread[...], prod, (((1,), (1,)), ((), ())), preferred_element_type=F32, precision=HIGH
     )
-    dr[z, y, 0:8] = as_rows(m["lse"][...])
+    dr[z, y, 0:8] = as_rows(m.lse[...])
     dr[z, y, 8:16] = as_rows(delta)
     do_base = take(2 * YZ)
     act_start(do_base, [do, dr])
     act_forward(do_base, [do, dr], 0)
-    zy = rs_z(py, rzy)
-    grad_of(CO, m["oc"], dx2l)
+    grad_of(CO, m.oc, dx2l)
 
     sent(zh)
     yq_base = rs_y_base()
@@ -1216,7 +1309,7 @@
             kv[qi, :, D + k * WIDE : D + (k + 1) * WIDE] = nn(pt.astype(BF), db).astype(BF)
 
 
-    kvacc = m["kvacc"]
+    kvacc = m.kvacc
 
     def kv_grad(q):
         def part(k, carry):
@@ -1226,38 +1319,47 @@
 
         lax.fori_loop(0, NQ, part, 0)
 
-    def back_step(t, carry):
-        a = t % Z
-        b = t // Z
-
-        @pl.when(t > 0)
-        def _():
-            act_wait(do_base, [do, dr], t)
-
-        @pl.when((t > 0) & (t < Z))
-        def _():
-            act_forward(do_base, [do, dr], a)
-
-        attend_back(a, b)
-
-        @pl.when(t >= Z)
-        def _():
+    def back_own(a):
+        attend_back(a, 0)
+        kv_grad(zs(a) * Y + y)
+
+    def back_others(a):
+        def body(b, carry):
+            act_wait(do_base, [do, dr], b * Z + a)
+            attend_back(a, b)
             rs_y_send(yq_base, po, ryo, b, a)
-
-        @pl.when(t == 1)
+            kv_grad(zs(a) * Y + ys(b))
+            return carry
+
+        lax.fori_loop(1, Y, body, 0)
+
+    def back_step(k, carry):
+        act_wait(do_base, [do, dr], k + 1)
+        act_forward(do_base, [do, dr], k + 1)
+        back_others(k)
+
+        @pl.when(k == 1)
         def _():
             push(CO)
-
-        kv_grad(zs(a) * Y + ys(b))
-
+            share_acts_end()
+            held.zy = rs_z(py, rzy)
+
+        @pl.when(k == Z - 2)
+        def _():
+            push(FI)
+
+        back_own(k + 1)
         return carry
 
     kvacc[...] = jnp.zeros_like(kvacc)
-    lax.fori_loop(0, YZ, back_step, 0)
+    back_own(0)
+    push(FO)
+    lax.fori_loop(0, Z - 1, back_step, 0)
+    back_others(Z - 1)
     def row_grads(k0, k1):
         def whole(k, carry):
             pas[k] = (nt(kv[k, :, 0:D], w[CK]) + nt(kv[k, :, D : 2 * D], w[CV])).astype(BF)
-            pltpu.make_async_copy(pas.at[k], m["pg"].at[k], lsem.at[1 + k]).start()
+            pltpu.make_async_copy(pas.at[k], m.pg.at[k], lsem.at[1 + k]).start()
             return carry
 
         def part(k, carry):
@@ -1271,7 +1373,7 @@
             def _():
                 for q in range(chunk):
                     at = k // NQ * chunk + q
-                    pltpu.make_async_copy(pas.at[at], m["pg"].at[at], lsem.at[1 + at]).start()
+                    pltpu.make_async_copy(pas.at[at], m.pg.at[at], lsem.at[1 + at]).start()
 
             return carry
 
@@ -1280,8 +1382,7 @@
         else:
             lax.fori_loop(k0 * NQ, k1 * NQ, part, 0)
 
-    half = YZ // chunk // 2
-    held = {}
+    part = YZ // chunk // 4
 
     def take_dq():
         for b in range(1, Y):
@@ -1290,41 +1391,41 @@
         dqc = rs_total(po.at[0], rzo)
         for b in range(1, Y):
             dqc = dqc + ryo[b - 1, z].astype(F32)
-        held["dqc"] = dqc.astype(BF)
-        dh2 = nt(held["dqc"], w[CQ])
-        dv, gg = norm_back(m["x1"][...], gain[1:2, :], dh2)
+        held.dqc = dqc.astype(BF)
+        dh2 = nt(held.dqc, w[CQ])
+        dv, gg = norm_back(m.x1[...], gain[1:2, :], dh2)
         sm[1:2, :] = gg
-        dx1 = m["dx"][...] + dv
-        m["dx"][...] = dx1
-        held["dx1l"] = dx1.astype(BF)
+        dx1 = m.dx[...] + dv
+        m.dx[...] = dx1
+        held.dx1l = dx1.astype(BF)
 
     def self_back():
-        m["oc"][...] = nt(held["dx1l"], w[SO]).astype(BF)
+        m.oc[...] = nt(held.dx1l, w[SO]).astype(BF)
         grads = [[], [], []]
-        held["tail"] = []
+        held.tail = []
         back = (iota((T, 128), 1) == T - 1 - iota((T, 128), 0)).astype(F32).astype(BF)
         for t in range(NQ):
-            db = stack4(m["oc"][:, quad(t)])
-            qb = stack4(m["qs"][:, quad(t)])
-            pr = m["ps"][t]
-            dps = nt(db, m["vs"][:, quad(t)])
+            db = stack4(m.oc[:, quad(t)])
+            qb = stack4(m.qs[:, quad(t)])
+            pr = m.ps[t]
+            dps = nt(db, m.vs[:, quad(t)])
             dss = (pr * (dps - jnp.sum(pr * dps, axis=1, keepdims=True))).astype(BF)
-            grads[0].append(fold4(nn(dss, m["ks"][:, quad(t)])).astype(BF))
+            grads[0].append(fold4(nn(dss, m.ks[:, quad(t)])).astype(BF))
             grads[1].append(tn(dss, qb).astype(BF))
             grads[2].append(tn(pr.astype(BF), db).astype(BF))
             turned = nn(dss, back)
             for h in range(QUAD):
                 part = pltpu.roll(turned[h * T : (h + 1) * T], 0, 1, stride=1, stride_axis=0)
-                held["tail"].append(jnp.sum(part, axis=0, keepdims=True))
-        held["dqs"], held["dks"], held["dvs"] = (jnp.concatenate(g, axis=1) for g in grads)
+                held.tail.append(jnp.sum(part, axis=0, keepdims=True))
+        held.dqs, held.dks, held.dvs = (jnp.concatenate(g, axis=1) for g in grads)
 
     def token_grad():
-        dh1 = nt(held["dqs"], w[SQ]) + nt(held["dks"], w[SK]) + nt(held["dvs"], w[SV])
+        dh1 = nt(held.dqs, w[SQ]) + nt(held.dks, w[SK]) + nt(held.dvs, w[SV])
         dv, gg = norm_back(tok[...], gain[0:1, :], dh1)
         sm[0:1, :] = gg
-        m["tg"][...] = m["dx"][...] + dv
+        m.tg[...] = m.dx[...] + dv
         flat = HEADS * BUCKETS
-        diag = jnp.concatenate(held["tail"] + [jnp.zeros((16 - HEADS, 128), F32)], axis=0)
+        diag = jnp.concatenate(held.tail + [jnp.zeros((16 - HEADS, 128), F32)], axis=0)
         mi, bi = iota((128, 128), 0), iota((128, 128), 1)
         hot = ((mi >= T - 1) & (bucket_of(mi - (T - 1)) == bi) & (bi < BUCKETS)).astype(F32)
         table = nn_high(diag, hot)
@@ -1334,19 +1435,19 @@
         own = (n0 >= h0 * BUCKETS) & (n0 < h0 * BUCKETS + BUCKETS)
         sm[3:4, 0:flat] = jnp.sum(jnp.where(own, wide, 0.0), axis=0, keepdims=True)
 
-    rsm = m["rsm"]
+    rsm = m.rsm
     slot = [0]
 
     def small_to(devs):
-        held["small"] = []
+        held.small = []
         for to in devs:
-            held["small"].append((slot[0], send(sm, rsm.at[slot[0]], to)))
+            held.small.append((slot[0], send(sm, rsm.at[slot[0]], to)))
             slot[0] += 1
 
     def small_got():
-        got([cp for _, cp in held["small"]])
-        sent([cp for _, cp in held["small"]])
-        for k, _ in held["small"]:
+        got([cp for _, cp in held.small])
+        sent([cp for _, cp in held.small])
+        for k, _ in held.small:
             sm[...] += rsm[k]
 
     def small_step(k):
@@ -1363,49 +1464,50 @@
             )
 
     def block_out():
-        got(zy)
-        m["bo"][...] = live * (m["x2"][...] + rs_total(py, rzy))
+        got(held.zy)
+        m.bo[...] = live * (m.x2[...] + rs_total(py, rzy))
 
     steps = {
-        "ck": lambda: grad_out(CK, kvacc, 0),
-        "cv": lambda: grad_out(CV, kvacc, D),
-        "pass": lambda: [pass_back(a) for a in range(1, Z)],
-        "rows1": lambda: row_grads(0, half),
-        "rows2": lambda: row_grads(half, YZ // chunk),
-        "dq": take_dq,
-        "cq": lambda: grad_of(CQ, m["h2"], held["dqc"]),
-        "so": lambda: grad_of(SO, m["os"], held["dx1l"]),
-        "selfback": self_back,
-        "sv": lambda: grad_of(SV, m["h1"], held["dvs"]),
-        "sq": lambda: grad_of(SQ, m["h1"], held["dqs"]),
-        "sk": lambda: grad_of(SK, m["h1"], held["dks"]),
-        "dh1": token_grad,
-        "bo": block_out,
+        DO_CK: lambda: grad_out(CK, kvacc, 0),
+        DO_CV: lambda: grad_out(CV, kvacc, D),
+        DO_PASS: lambda: [pass_back(a) for a in range(1, Z)],
+        DO_ROWS1: lambda: row_grads(0, part),
+        DO_ROWS2: lambda: row_grads(part, 2 * part),
+        DO_ROWS3: lambda: row_grads(2 * part, 3 * part),
+        DO_ROWS4: lambda: row_grads(3 * part, YZ // chunk),
+        DO_DQ: take_dq,
+        DO_CQ: lambda: grad_of(CQ, m.h2, held.dqc),
+        DO_SO: lambda: grad_of(SO, m.os, held.dx1l),
+        DO_SELFBACK: self_back,
+        DO_SV: lambda: grad_of(SV, m.h1, held.dvs),
+        DO_SQ: lambda: grad_of(SQ, m.h1, held.dqs),
+        DO_SK: lambda: grad_of(SK, m.h1, held.dks),
+        DO_DH1: token_grad,
+        DO_BO: block_out,
     }
-    pieces = dict(SQ=SQ, SK=SK, SV=SV, SO=SO, CQ=CQ, CK=CK, CV=CV, CO=CO, FI=FI, FO=FO)
     small_at = [0]
 
     def run(name):
-        if name == "small":
+        if name == DO_SMALL:
             small_step(small_at[0])
             small_at[0] += 1
-        elif name in pieces:
-            push(pieces[name])
+        elif name < PIECES:
+            push(name)
         else:
             steps[name]()
 
     for name in TAIL:
         run(name)
-    assert all(k == len(stages) for k, _ in moving.values()), moving
+    assert all(k == len(stages_of(p)) for p, (k, _) in moving.items()), moving
     assert small_at[0] == 5
     me = dp * YZ + fs
     nd, ld = iota((D, 128), 0), iota((D, 128), 1)
     mine = nn_high(sm[...], ((nd == me * r + ld) & (ld < r)).astype(F32))
     mine_b = nn_high(sm[...], ((nd == me * rbs + ld) & (ld < rbs)).astype(F32))
-    m["g_ls"][...] = mine[0:1, 0:r]
-    m["g_lc"][...] = mine[1:2, 0:r]
-    m["g_lf"][...] = mine[2:3, 0:r]
-    m["g_rb"][...] = mine_b[3:4, 0:rbs]
+    m.g_ls[...] = mine[0:1, 0:r]
+    m.g_lc[...] = mine[1:2, 0:r]
+    m.g_lf[...] = mine[2:3, 0:r]
+    m.g_rb[...] = mine_b[3:4, 0:rbs]
 
     act_done(do_base, [do, dr])
     rs_y_done(yq_base, po, ryo)
@@ -1413,7 +1515,7 @@
     drain()
 
     def pg_wait(q, carry):
-        pltpu.make_async_copy(pas.at[q], m["pg"].at[q], lsem.at[1 + q]).wait()
+        pltpu.make_async_copy(pas.at[q], m.pg.at[q], lsem.at[1 + q]).wait()
         return carry
 
     lax.fori_loop(0, YZ, pg_wait, 0)
@@ -1422,8 +1524,13 @@
 def place_kernel(*refs):
     n = len(OUTPUTS)
     given, put, held, sem = refs[:n], refs[n : 2 * n], refs[2 * n : 3 * n], refs[3 * n]
-    loads = [pltpu.make_async_copy(given[k], held[k], sem.at[k]) for k in range(n)]
-    stores = [pltpu.make_async_copy(held[k], put[k], sem.at[n + k]) for k in range(n)]
+    loads, stores = [], []
+    for k in range(n):
+        parts = [slice(None)] if len(given[k].shape) < 3 else range(given[k].shape[0])
+        for part in parts:
+            at = len(loads)
+            loads.append(pltpu.make_async_copy(given[k].at[part], held[k].at[part], sem.at[0, at]))
+            stores.append(pltpu.make_async_copy(held[k].at[part], put[k].at[part], sem.at[1, at]))
     for cp in loads:
         cp.start()
     for load, store in zip(loads, stores):
@@ -1446,7 +1553,6 @@
     gr = r if sz.inside else D
     vm = pl.BlockSpec(memory_space=pltpu.VMEM)
     hbm = pl.BlockSpec(memory_space=pltpu.HBM)
-    smem = pl.BlockSpec(memory_space=pltpu.SMEM)
     shape = jax.ShapeDtypeStruct
     rbs = rel_bias.shape[0]
     out_shape = (
@@ -1463,7 +1569,7 @@
     outs = pl.pallas_call(
         functools.partial(block_kernel, sz, names),
         out_shape=out_shape,
-        in_specs=[{"pas_in": hbm, "len": smem}.get(n, vm) for n in INPUTS],
+        in_specs=[hbm if n == "pas_in" else vm for n in INPUTS],
         out_specs=tuple(hbm if n in apart else vm for n in OUTPUTS),
         scratch_shapes=tuple(scratch.values()),
         compiler_params=pltpu.CompilerParams(
@@ -1473,7 +1579,7 @@
             flops=20 * 10**9, bytes_accessed=2 * 10**7, transcendentals=4 * 10**6
         ),
     )(
-        targets[0], passages, tgt_len, out_grad[0], ln_self[None], rel_bias[None],
+        targets[0], passages, tgt_len[None], out_grad[0], ln_self[None], rel_bias[None],
         self_q, self_kv, self_out, ln_cross[None], cross_q, cross_kv, cross_out,
         ln_ff[None], ff_in, ff_out,
     )
@@ -1497,7 +1603,7 @@
             in_specs=[hbm] * len(outs),
             out_specs=(hbm,) * len(outs),
             scratch_shapes=tuple(pltpu.VMEM(o.shape, o.dtype) for o in outs)
-            + (pltpu.SemaphoreType.DMA((2 * len(outs),)),),
+            + (pltpu.SemaphoreType.DMA((2, len(outs) - 1 + passages.shape[0])),),
             compiler_params=pltpu.CompilerParams(vmem_limit_bytes=63 * 2**20),
         )(*outs)
     (bo, tg, pg, g_ls, g_rb, g_sq, g_skv, g_so, g_lc, g_cq, g_ckv, g_co, g_lf, g_fi, g_fo) = outs

time: 197 us -> 180 us (0.914)
  Pallas kernels: 195 us -> 178 us
    pallas_call x1, Pallas kernels: 190 us -> 173 us  [per_device(): pl.pallas_call(functools.partial(block_kernel, sz, names), out_shape=out_...]
where the time goes in v4:
time: 180 us; the launch traced here: 179 us
  Pallas kernels  178 us (99%)
    pallas_call x1, Pallas kernels, per_device(): pl.pallas_call(functools.partial(block_kernel, sz, names), out_shape=out_...  173 us
    pallas_call x1, Pallas kernels, per_device(): pl.pallas_call(place_kernel, out_shape=tuple((shape(o.shape, o.dtype) for...  4.56 us

profile of v4, /device:TPU:0, one launch (start us, length us, event | category | flops | bytes accessed | tf_op | source)
XLA Modules:
  0.0 179.5 jit_solution(17293019213679547625)
XLA Ops:
  1.3 173.4 %shard_map.271 = (f32[64,768]{1,0:T(8,128)}, f32[64,768]{1,0:T(8,128)}, bf16[8,240,768]{2,1,0:T(8,128)(2,1)}, f32[1,24]{1,0:T(1,128)}, f32[1,12]{1,0:T(1,128)}, ...) custom-call(f32[64,768]{1,0:T(8,128)} %bitcast.14, ...), custom_call_target="tpu_custom_call" | custom-call | flops 20000000000 | bytes 20000000 | tf_op jit(solution)/shard_map/pallas_call | solution.py:1569
  174.7 4.6 %shard_map.272 = (f32[64,768]{1,0:T(8,128)}, f32[64,768]{1,0:T(8,128)}, bf16[8,240,768]{2,1,0:T(8,128)(2,1)}, f32[1,24]{1,0:T(1,128)}, f32[1,12]{1,0:T(1,128)}, ...) custom-call(f32[64,768]{1,0:T(8,128)} %get-tuple-element.45.refs_0_,, ...), custom_call_target="tpu_custom_call" | custom-call | tf_op jit(solution)/shard_map/pallas_call | solution.py:1600

commit v5 on v4

--- a/solution.py
+++ b/solution.py
@@ -21,7 +21,8 @@
 PIECES = 10
 SQ, SK, SV, SO, CQ, CK, CV, CO, FI, FO = range(PIECES)
 WIDE_PIECES = (CK, CV, FI, FO)
-Y_SUMMED_FIRST = (CK, CV)
+Y_SUMMED_FIRST = (CK,)
+Z_AT_ONCE = (FI, SQ, SK)
 FACTORS = {SQ: "h1", SK: "h1", SV: "h1", SO: "os", CQ: "h2", CO: "oc"}
 ACTS = ("h1", "os", "h2", "oc")
 Y_GATHERED_LAST = (SQ, SV, CQ)
@@ -228,20 +229,20 @@
 
 
 (
-    DO_CK, DO_CV, DO_PASS, DO_ROWS1, DO_ROWS2, DO_ROWS3,
-    DO_ROWS4, DO_DQ, DO_CQ, DO_SO, DO_SELFBACK, DO_SV,
-    DO_SQ, DO_SK, DO_DH1, DO_BO, DO_SMALL,
-) = range(PIECES, PIECES + 17)
+    DO_KVG1, DO_CK, DO_CV, DO_PASS, DO_ROWS1, DO_ROWS2,
+    DO_ROWS3, DO_ROWS4, DO_DQ, DO_CQ, DO_SO, DO_SELFBACK,
+    DO_SV, DO_SQ, DO_SK, DO_DH1, DO_BO, DO_SMALL,
+) = range(PIECES, PIECES + 18)
 TAIL = (
-    FO, DO_CK, DO_CV, CO, FO, FO, DO_PASS, CK,
-    CV, DO_ROWS1, FI, CO, DO_DQ, DO_CQ, DO_SO, DO_SELFBACK,
-    DO_SV, DO_SQ, DO_SK, DO_DH1, DO_SMALL, CK, DO_BO, FI,
-    CQ, FI, DO_SMALL, CO, SO, CQ, DO_ROWS2, SV,
-    SO, CV, CO, SQ, SV, SK, CQ, SQ,
-    DO_ROWS3, SK, CK, SO, DO_SMALL, CQ, DO_ROWS4, SV,
-    CV, CK, SQ, SO, CQ, SV, SK, DO_SMALL,
-    CV, CK, SQ, SO, SV, SK, DO_SMALL, CV,
-    SQ, SK,
+    FO, DO_KVG1, FO, DO_CK, DO_CV, FO, DO_PASS, CO,
+    CK, CV, FI, DO_ROWS1, DO_DQ, DO_CQ, DO_SO, CO,
+    DO_SELFBACK, DO_SV, DO_SQ, DO_SK, DO_DH1, DO_SMALL, FI, DO_BO,
+    CV, CO, FI, CK, DO_SMALL, CQ, DO_ROWS2, CO,
+    SO, CQ, CV, SV, SO, DO_ROWS3, SQ, SV,
+    CV, SK, CQ, SQ, SK, CK, CV, SO,
+    DO_SMALL, DO_ROWS4, CQ, SV, CK, SO, SQ, CQ,
+    SV, SK, CK, DO_SMALL, SO, SQ, SV, SK,
+    DO_SMALL, SQ, SK,
 )
 
 SPOTS = ("gw", "smb", "fip", "rc", "r1", "r1y", "r2", "r2x", "rz", "act", "cot")
@@ -1150,7 +1151,7 @@
             add_blocks(1, lambda k, z_: gw.at[p, c, x, y, z_], lambda k, z_: part.at[z_])
         if p == FO:
             return []
-        if p == FI:
+        if p in Z_AT_ONCE:
             return [
                 send(gw.at[p, c, x, y, zs(a)], rz.at[p, a - 1], dev(z_=zs(a)))
                 for a in range(1, Z)
@@ -1162,7 +1163,7 @@
 
     def rs_fourth(p, cps):
         got(cps)
-        if p in (FI, FO):
+        if p == FO or p in Z_AT_ONCE:
             return []
         add_to(gw.at[p, c, x, y, z_far], rz.at[p, 1])
         return [send(gw.at[p, c, x, y, z_far], rz.at[p, 2], dev(z_=z_far))]
@@ -1197,6 +1198,8 @@
                         getattr(m, name)[:, at : at + per] = m.kvacc[k * r : k * r + r, i * per : (i + 1) * per]
             return None
         v = gw[p, c, x, y, z].astype(F32) + rz[p, 0].astype(F32) + rz[p, 2].astype(F32)
+        if p in Z_AT_ONCE:
+            v = v + rz[p, 1].astype(F32)
         lo, hi = get_halves(v, r)
         getattr(m, name)[:, off : off + nh] = lo
         getattr(m, name)[:, off + nh : off + D] = hi
@@ -1244,6 +1247,16 @@
     share_acts_on()
     sm = m.sm
     sm[...] = jnp.zeros_like(sm)
+    do, dr = m.do, m.dr
+    do_base = take(2 * YZ)
+    pick = iota((T, D), 0) == (iota((T, D), 1) & (T - 1))
+
+    def as_rows(st):
+        v = jnp.sum(jnp.where(pick, expand(st), 0.0), axis=0, keepdims=True)
+        parts = [v[:, k * 128 : (k + 1) * 128] for k in range(D // 128)]
+        return jnp.concatenate(parts + [jnp.zeros((8 - D // 128, 128), F32)], axis=0)
+
+    dr[z, y, 0:8] = as_rows(m.lse[...])
     got(zh)
     dh3 = rs_total(po.at[0], rzo)
     dv, gg = norm_back(m.x2[...], gain[2:3, :], dh3)
@@ -1252,24 +1265,16 @@
     m.dx[...] = dx2
     dx2l = dx2.astype(BF)
     doc = nt(dx2l, w[CO]).astype(BF)
-    do, dr = m.do, m.dr
     do[z, y] = doc
-    pick = iota((T, D), 0) == (iota((T, D), 1) & (T - 1))
-
-    def as_rows(st):
-        v = jnp.sum(jnp.where(pick, expand(st), 0.0), axis=0, keepdims=True)
-        parts = [v[:, k * 128 : (k + 1) * 128] for k in range(D // 128)]
-        return jnp.concatenate(parts + [jnp.zeros((8 - D // 128, 128), F32)], axis=0)
-
+    act_start(do_base, [do])
+    act_forward(do_base, [do], 0)
     prod = doc.astype(F32) * m.oc[...].astype(F32)
     delta = lax.dot_general(
         spread[...], prod, (((1,), (1,)), ((), ())), preferred_element_type=F32, precision=HIGH
     )
-    dr[z, y, 0:8] = as_rows(m.lse[...])
     dr[z, y, 8:16] = as_rows(delta)
-    do_base = take(2 * YZ)
-    act_start(do_base, [do, dr])
-    act_forward(do_base, [do, dr], 0)
+    act_start(do_base + YZ, [dr])
+    act_forward(do_base + YZ, [dr], 0)
     grad_of(CO, m.oc, dx2l)
 
     sent(zh)
@@ -1319,16 +1324,21 @@
 
         lax.fori_loop(0, NQ, part, 0)
 
+    def kv_grads(t0, t1):
+        def body(t, carry):
+            kv_grad(zs(t // Y) * Y + ys(t % Y))
+            return carry
+
+        lax.fori_loop(t0, t1, body, 0)
+
     def back_own(a):
         attend_back(a, 0)
-        kv_grad(zs(a) * Y + y)
 
     def back_others(a):
         def body(b, carry):
             act_wait(do_base, [do, dr], b * Z + a)
             attend_back(a, b)
             rs_y_send(yq_base, po, ryo, b, a)
-            kv_grad(zs(a) * Y + ys(b))
             return carry
 
         lax.fori_loop(1, Y, body, 0)
@@ -1337,6 +1347,10 @@
         act_wait(do_base, [do, dr], k + 1)
         act_forward(do_base, [do, dr], k + 1)
         back_others(k)
+
+        @pl.when(k < Z - 2)
+        def _():
+            kv_grads(k * Y + 1, k * Y + Y)
 
         @pl.when(k == 1)
         def _():
@@ -1349,10 +1363,16 @@
             push(FI)
 
         back_own(k + 1)
+
+        @pl.when(k < Z - 2)
+        def _():
+            kv_grads(k * Y + Y, k * Y + Y + 1)
+
         return carry
 
     kvacc[...] = jnp.zeros_like(kvacc)
     back_own(0)
+    kv_grad(z * Y + y)
     push(FO)
     lax.fori_loop(0, Z - 1, back_step, 0)
     back_others(Z - 1)
@@ -1470,6 +1490,7 @@
     steps = {
         DO_CK: lambda: grad_out(CK, kvacc, 0),
         DO_CV: lambda: grad_out(CV, kvacc, D),
+        DO_KVG1: lambda: kv_grads((Z - 2) * Y + 1, YZ),
         DO_PASS: lambda: [pass_back(a) for a in range(1, Z)],
         DO_ROWS1: lambda: row_grads(0, part),
         DO_ROWS2: lambda: row_grads(part, 2 * part),

time: 180 us -> 179 us (level)
  no operation moved by 1% of the time
where the time goes in v5:
time: 179 us
  Pallas kernels  178 us (99%)
    pallas_call x1, Pallas kernels, per_device(): pl.pallas_call(functools.partial(block_kernel, sz, names), out_shape=out_...  173 us
    pallas_call x1, Pallas kernels, per_device(): pl.pallas_call(place_kernel, out_shape=tuple((shape(o.shape, o.dtype) for...  4.56 us

profile of v5, /device:TPU:0, one launch (start us, length us, event | category | flops | bytes accessed | tf_op | source)
XLA Modules:
  0.0 179.0 jit_solution(1446378550365960072)
XLA Ops:
  1.3 173.0 %shard_map.271 = (f32[64,768]{1,0:T(8,128)}, f32[64,768]{1,0:T(8,128)}, bf16[8,240,768]{2,1,0:T(8,128)(2,1)}, f32[1,24]{1,0:T(1,128)}, f32[1,12]{1,0:T(1,128)}, ...) custom-call(f32[64,768]{1,0:T(8,128)} %bitcast.14, ...), custom_call_target="tpu_custom_call" | custom-call | flops 20000000000 | bytes 20000000 | tf_op jit(solution)/shard_map/pallas_call | solution.py:1590
  174.3 4.6 %shard_map.272 = (f32[64,768]{1,0:T(8,128)}, f32[64,768]{1,0:T(8,128)}, bf16[8,240,768]{2,1,0:T(8,128)(2,1)}, f32[1,24]{1,0:T(1,128)}, f32[1,12]{1,0:T(1,128)}, ...) custom-call(f32[64,768]{1,0:T(8,128)} %get-tuple-element.45.refs_0_,, ...), custom_call_target="tpu_custom_call" | custom-call | tf_op jit(solution)/shard_map/pallas_call | solution.py:1621

commit v6 on v5

--- a/solution.py
+++ b/solution.py
@@ -371,7 +371,6 @@
         pl.semaphore_signal(bar, inc=1, device_id=p, device_id_type=pl.DeviceIdType.MESH)
     load_pas = pltpu.make_async_copy(m.pas_in, m.pas, lsem.at[0])
     load_pas.start()
-    pl.semaphore_wait(bar, len(partners))
 
     mask = m.mask
     mask[...] = (iota((WIDE, WIDE), 0) // DK == iota((WIDE, WIDE), 1) // DK).astype(F32).astype(BF)
@@ -520,17 +519,22 @@
         moves[p] = Gather(gw.at[p], p not in Y_GATHERED_LAST, feed, p < CO)
 
     moves["small"] = Gather(smb, True, first=True)
-    moves["small"].z_out()
-    moves["small"].own_out()
     sources = (
         (m.sq, 0), (m.skv, 0), (m.skv, D), (m.so, 0),
         (m.cq, 0), (m.ckv, 0), (m.ckv, D), (m.co, 0),
     )
 
-    def pack(p):
+    def store(p):
         ref, off = sources[p]
         v = ref[:, off : off + D].astype(F32)
         put_halves(gw.at[p, c, x, y, z], v[:, 0:nh], v[:, nh:D], r, rb)
+
+    for p in (SQ, SK, SV, SO, CQ, CK, CV, CO):
+        store(p)
+    pl.semaphore_wait(bar, len(partners))
+    moves["small"].z_out()
+    moves["small"].own_out()
+    def pack(p):
         begin(p)
         if p in (SQ, SK, SV):
             moves[p].z_out()
@@ -1257,6 +1261,8 @@
         return jnp.concatenate(parts + [jnp.zeros((8 - D // 128, 128), F32)], axis=0)
 
     dr[z, y, 0:8] = as_rows(m.lse[...])
+    if sz.inside:
+        m.kvacc[...] = jnp.zeros_like(m.kvacc)
     got(zh)
     dh3 = rs_total(po.at[0], rzo)
     dv, gg = norm_back(m.x2[...], gain[2:3, :], dh3)
@@ -1370,7 +1376,8 @@
 
         return carry
 
-    kvacc[...] = jnp.zeros_like(kvacc)
+    if not sz.inside:
+        kvacc[...] = jnp.zeros_like(kvacc)
     back_own(0)
     kv_grad(z * Y + y)
     push(FO)

time: 179 us -> 179 us (level)
  no operation moved by 1% of the time
where the time goes in v6:
time: 179 us
  Pallas kernels  178 us (99%)
    pallas_call x1, Pallas kernels, per_device(): pl.pallas_call(functools.partial(block_kernel, sz, names), out_shape=out_...  173 us
    pallas_call x1, Pallas kernels, per_device(): pl.pallas_call(place_kernel, out_shape=tuple((shape(o.shape, o.dtype) for...  4.56 us

profile of v6, /device:TPU:0, one launch (start us, length us, event | category | flops | bytes accessed | tf_op | source)
XLA Modules:
  0.0 179.2 jit_solution(3103086467954682554)
XLA Ops:
  1.3 173.2 %shard_map.271 = (f32[64,768]{1,0:T(8,128)}, f32[64,768]{1,0:T(8,128)}, bf16[8,240,768]{2,1,0:T(8,128)(2,1)}, f32[1,24]{1,0:T(1,128)}, f32[1,12]{1,0:T(1,128)}, ...) custom-call(f32[64,768]{1,0:T(8,128)} %bitcast.14, ...), custom_call_target="tpu_custom_call" | custom-call | flops 20000000000 | bytes 20000000 | tf_op jit(solution)/shard_map/pallas_call | solution.py:1597
  174.5 4.6 %shard_map.272 = (f32[64,768]{1,0:T(8,128)}, f32[64,768]{1,0:T(8,128)}, bf16[8,240,768]{2,1,0:T(8,128)(2,1)}, f32[1,24]{1,0:T(1,128)}, f32[1,12]{1,0:T(1,128)}, ...) custom-call(f32[64,768]{1,0:T(8,128)} %get-tuple-element.45.refs_0_,, ...), custom_call_target="tpu_custom_call" | custom-call | tf_op jit(solution)/shard_map/pallas_call | solution.py:1628
